TPU v7x, 32 devices: a whole 2x2x4 slice. The times are simulated.
32 devices in a mesh: tm: 4 (over x, core), space: 8 (over z, y).
Axes of the slice: x: 2, y: 2, z: 4, core: 2. Of those that a mesh axis runs over, the one named last changes fastest.
Arguments:
- snapshots: bfloat16 [8, 32, 4, 512], P('tm', 'space'), may hold values from -6 to 6
- conv_weight: bfloat16 [32, 4, 3, 3, 3], replicated, may hold values from -0.625 to 0.625
- conv_bias: float32 [32], replicated, may hold values from -3 to 3
- tap_weight: bfloat16 [3, 32, 3, 32], replicated, may hold values from -0.625 to 0.625
- tap_bias: float32 [3, 32], replicated, may hold values from -3 to 3
- mix_weight: bfloat16 [3, 32, 32], replicated, may hold values from -1 to 1
- mix_bias: float32 [3, 32], replicated, may hold values from -3 to 3
Outputs:
- refined: bfloat16 [8, 32, 32, 512], P('tm', 'space')
All inputs are finite; a program needn't handle non-finite values.
Results may differ from a plain program's by a relative error of at most 0.0063.
Values may be sent and summed in bfloat16 or wider, within the bound.
No kernel may reach another device: no remote copies, remote signals or barrier semaphores. Data moves between devices by JAX's collectives and lax.ppermute only.
A program may use at most 64 MiB of HBM per device.

v0:
```python
import functools
import math

import jax
import jax.numpy as jnp
from jax import lax
from jax.experimental import pallas as pl
from jax.experimental.pallas import tpu as pltpu
from jax.sharding import PartitionSpec as P

LEVELS = 3
NZ = 32
GROUP = 4
CELLS = 256
SLOPE = math.sqrt(2.0 / math.pi)
CUBIC = SLOPE * 0.044715
BF16 = jnp.bfloat16
F32 = jnp.float32


def frame_blocks(axis_size, frames):
    needed = [0]
    counts = [1]
    for level in reversed(range(LEVELS)):
        reach = set()
        for offset in needed:
            for frame in range(frames):
                for step in (-(2**level), 2**level):
                    reach.add((offset + (frame + step) // frames) % axis_size)
        needed = needed + sorted(reach - set(needed))
        spare = [offset for offset in range(axis_size) if offset not in needed]
        while len(needed) * frames % GROUP and spare:
            needed.append(spare.pop(0))
        counts.append(len(needed))
    return needed, counts[::-1]


def gelu(value):
    half = 0.5 * value
    return (half + half * jnp.tanh(value * (SLOPE + CUBIC * (value * value)))).astype(BF16)


def column(row, copies):
    count = row.shape[1]
    down = lax.broadcasted_iota(jnp.int32, (count, count), 0)
    across = lax.broadcasted_iota(jnp.int32, (count, count), 1)
    tall = jnp.sum(jnp.where(down == across, row, 0.0), axis=1, keepdims=True)
    return jnp.broadcast_to(jnp.concatenate([tall] * copies, axis=0), (count * copies, 128))


def spread(block, rows, columns):
    channels = block.shape[0]
    tall = jnp.concatenate([block] * (rows // channels), axis=0)
    down = lax.broadcasted_iota(jnp.int32, (channels, columns), 0)
    across = lax.broadcasted_iota(jnp.int32, (channels, columns), 1)
    pick = jnp.where(across % channels == down, 1.0, 0.0).astype(BF16)
    return jnp.dot(tall, pick, preferred_element_type=F32)


def prepare_kernel(slot_of, *refs):
    sources, outs, landed, sems = refs[:7], refs[7:-7], refs[-7:-1], refs[-1]
    copies = [
        pltpu.make_async_copy(source, target, sems.at[index])
        for index, (source, target) in enumerate(zip(sources, (outs[0], *landed)))
    ]
    for copy in copies:
        copy.start()
    for copy in copies:
        copy.wait()
    conv, conv_shift, taps, tap_shift, mix, mix_shift = landed
    frames = outs[0].shape[0]
    conv_out, conv_shift_out = outs[1], outs[2]
    tap_outs = outs[3 : 3 + LEVELS]
    tap_shift_out, mix_out, mix_shift_out = outs[3 + LEVELS :]
    places, fields, channels = conv.shape
    depth = places * fields
    wide = depth * GROUP
    flat = conv[...].astype(F32).reshape(depth, channels).astype(BF16)
    down = lax.broadcasted_iota(jnp.int32, (depth, wide), 0)
    across = lax.broadcasted_iota(jnp.int32, (depth, wide), 1)
    same = (down // fields == across // (GROUP * fields)) & (down % fields == across % fields)
    pick = jnp.where(same, 1.0, 0.0).astype(BF16)
    full = lax.dot_general(flat, pick, (((0,), (0,)), ((), ())), preferred_element_type=F32)
    full = jnp.concatenate([full] * GROUP, axis=0)
    down = lax.broadcasted_iota(jnp.int32, full.shape, 0)
    across = lax.broadcasted_iota(jnp.int32, full.shape, 1)
    keep = down // channels == across // fields % GROUP
    conv_out[...] = jnp.where(keep, full, 0.0).astype(BF16)
    conv_shift_out[...] = column(conv_shift[...], GROUP)
    slots = slot_of(lax.axis_index("tm"))
    for level in range(LEVELS):
        rows, columns = tap_outs[level].shape

        def frame_of(axis):
            place = lax.broadcasted_iota(jnp.int32, (rows, columns), axis) // channels
            block = place // frames
            start = jnp.zeros((rows, columns), jnp.int32)
            for index, slot in enumerate(slots[: (rows, columns)[axis] // channels // frames]):
                start = jnp.where(block == index, slot * frames, start)
            return start + place % frames

        gap = frame_of(1) - frame_of(0)
        total = jnp.zeros((rows, columns), F32)
        for tap in range(3):
            block = spread(taps[level, tap], rows, columns)
            total = jnp.where(gap == (tap - 1) * 2**level, block, total)
        tap_outs[level][...] = total.astype(BF16)
        tap_shift_out[level] = column(tap_shift[level : level + 1], GROUP)
        size = GROUP * channels
        down = lax.broadcasted_iota(jnp.int32, (size, size), 0)
        across = lax.broadcasted_iota(jnp.int32, (size, size), 1)
        full = spread(mix[level], size, size)
        mix_out[level] = jnp.where(down // channels == across // channels, full, 0.0).astype(BF16)
        mix_shift_out[level] = column(mix_shift[level : level + 1], GROUP)


def shifted(lines):
    plane = lines.shape[-1]
    depth = lax.broadcasted_iota(jnp.int32, (1, plane), 1) % NZ
    blank = jnp.zeros_like(lines)
    below = jnp.where(depth == 0, blank, pltpu.roll(lines, 1, 1))
    above = jnp.where(depth == NZ - 1, blank, pltpu.roll(lines, plane - 1, 1))
    for delta_y in (-1, 0, 1):
        for piece in (below, lines, above):
            yield pltpu.roll(piece, -delta_y * NZ % plane, 1) if delta_y else piece


def parity():
    return lax.rem(lax.axis_index("space") + lax.axis_index("tm"), 2)


def joined(parts, axis):
    return parts[0] if len(parts) == 1 else jnp.concatenate(parts, axis=axis)


def wide(shift, cells):
    return joined([shift] * (cells // 128), 1)


def encode(windows, weights, frames, store):
    conv, conv_shift = weights[:2]
    taps = weights[2 : 2 + LEVELS]
    tap_shift, mix, mix_shift = weights[2 + LEVELS :]
    tall = conv.shape[0]
    channels = tall // GROUP
    groups = taps[0].shape[1] // tall
    hidden = []
    for window in windows:
        parts = []
        for group in range(groups):
            summed = jnp.dot(conv[...], window(group), preferred_element_type=F32)
            parts.append(gelu(summed + wide(conv_shift[...], summed.shape[1])))
        hidden.append(joined(parts, 0))
    for level, tap in enumerate(taps):
        rows, columns = tap.shape
        later = []
        for current in hidden:
            cells = current.shape[1]
            summed = jnp.dot(tap[...], current[:columns], preferred_element_type=F32)
            parts = []
            for first in range(0, rows, tall):
                size = min(tall, rows - first)
                piece = summed[first : first + size]
                gated = gelu(piece + wide(tap_shift[level, :size], cells))
                mixed = jnp.dot(mix[level, :size, :size], gated, preferred_element_type=F32)
                kept = current[first : first + size].astype(F32)
                parts.append((kept + mixed + wide(mix_shift[level, :size], cells)).astype(BF16))
            later.append(joined(parts, 0))
        hidden = later
    for index, final in enumerate(hidden):
        for frame in range(frames):
            store(index, frame, final[frame * channels : (frame + 1) * channels])


def stack(sources, group, depth, cells):
    part = slice(group * depth, (group + 1) * depth)
    return jnp.concatenate(
        [source[:, part, cells].reshape(9 * depth, -1) for source in sources], axis=0
    )


def pack_kernel(*refs):
    blocks, out = refs[:-1], refs[-1]
    frames, row_count = blocks[0].shape[:2]
    first, last = [
        jnp.concatenate([block[frame, row] for block in blocks for frame in range(frames)], axis=0)
        for row in (0, row_count - 1)
    ]
    out[...] = jnp.where(parity() == 0, first, last)


def inner_kernel(count, *rest):
    blocks, weights, (patches, out) = rest[:count], rest[count:-2], rest[-2:]
    frames, row_count, _, plane = blocks[0].shape
    depth = weights[0].shape[1] // 27
    width = math.gcd(plane, CELLS)
    for index in range(row_count):
        lines = [block[frame, index] for block in blocks for frame in range(frames)]
        for place, piece in enumerate(shifted(jnp.concatenate(lines, axis=0))):
            patches[index, place] = piece
    places = [
        (row, slice(start, start + width))
        for row in range(1, row_count - 1)
        for start in range(0, plane, width)
    ]
    windows = [
        functools.partial(
            stack, [patches.at[row + step] for step in (-1, 0, 1)], depth=depth, cells=cells
        )
        for row, cells in places
    ]

    def store(index, frame, final):
        row, cells = places[index]
        out[frame, row - 1, :, cells] = final

    encode(windows, weights, out.shape[0], store)


def outer_kernel(paired, mine, other, patches, inner, *rest):
    weights, (out, edges, borders, sems) = rest[:-4], rest[-4:]
    row_count, _, lines, plane = patches.shape
    depth = weights[0].shape[1] // 27
    width = math.gcd(plane, CELLS)
    middle = pltpu.make_async_copy(inner, out.at[:, 1 : row_count - 1], sems.at[0])
    middle.start()
    first, second = mine[...], other[...]
    if paired:
        half = lines // 2
        second = jnp.concatenate([second[half:], second[:half]], axis=0)
        below = parity() == 0
        first, second = jnp.where(below, first, second), jnp.where(below, second, first)
    for index, halo in enumerate((first, second)):
        for place, piece in enumerate(shifted(halo)):
            borders[index, place] = piece
    sources = [
        [borders.at[0], patches.at[0], patches.at[1]],
        [patches.at[row_count - 2], patches.at[row_count - 1], borders.at[1]],
    ]
    places = [
        (edge, slice(start, start + width)) for edge in range(2) for start in range(0, plane, width)
    ]
    windows = [
        functools.partial(stack, sources[edge], depth=depth, cells=cells) for edge, cells in places
    ]

    def store(index, frame, final):
        edge, cells = places[index]
        edges[frame, edge, :, cells] = final

    encode(windows, weights, out.shape[0], store)
    copies = [
        pltpu.make_async_copy(edges.at[:, edge], out.at[:, row], sems.at[edge + 1])
        for edge, row in ((0, 0), (1, row_count - 1))
    ]
    for copy in copies:
        copy.start()
    middle.wait()
    for copy in copies:
        copy.wait()


VMEM = pl.BlockSpec(memory_space=pltpu.VMEM)
PARAMS = pltpu.CompilerParams(vmem_limit_bytes=40 * 2**20)


def ring(count, step):
    return [(index, (index + step) % count) for index in range(count)]


def shards(snapshots, conv_weight, conv_bias, tap_weight, tap_bias, mix_weight, mix_bias):
    frames, row_count, fields, plane = snapshots.shape
    channels = conv_weight.shape[0]
    times = lax.axis_size("tm")
    spaces = lax.axis_size("space")
    offsets, counts = frame_blocks(times, frames)
    paired = times == 4 and sorted(offsets) == [0, 1, 2, 3] and spaces % 2 == 0
    tall = GROUP * channels
    total = len(offsets) * frames * fields

    if paired:
        offsets = [0, 2, 1, 3]
        slot_of = lambda index: [index ^ offset for offset in offsets]
    else:
        slot_of = lambda index: [(index + offset) % times for offset in offsets]

    shapes = [
        jax.ShapeDtypeStruct(snapshots.shape, BF16),
        jax.ShapeDtypeStruct((tall, 27 * GROUP * fields), BF16),
        jax.ShapeDtypeStruct((tall, 128), F32),
    ]
    for level in range(LEVELS):
        rows, columns = counts[level + 1], counts[level]
        shapes.append(
            jax.ShapeDtypeStruct((rows * frames * channels, columns * frames * channels), BF16)
        )
    shapes += [
        jax.ShapeDtypeStruct((LEVELS, tall, 128), F32),
        jax.ShapeDtypeStruct((LEVELS, tall, tall), BF16),
        jax.ShapeDtypeStruct((LEVELS, tall, 128), F32),
    ]
    sources = [
        snapshots,
        conv_weight.transpose(2, 3, 4, 1, 0).reshape(27, fields, channels),
        conv_bias.reshape(1, channels),
        tap_weight.transpose(0, 2, 1, 3),
        tap_bias,
        mix_weight,
        mix_bias,
    ]
    sources = [pltpu.with_memory_space_constraint(source, pltpu.HBM) for source in sources]
    own, *weights = pl.pallas_call(
        functools.partial(prepare_kernel, slot_of),
        out_shape=shapes,
        in_specs=[pl.BlockSpec(memory_space=pl.ANY)] * len(sources),
        out_specs=[VMEM] * len(shapes),
        scratch_shapes=[pltpu.VMEM(source.shape, source.dtype) for source in sources[1:]]
        + [pltpu.SemaphoreType.DMA((len(sources),))],
        compiler_params=PARAMS,
        name="prepare",
    )(*sources)

    if paired:
        across = [(index, index ^ 2) for index in range(times)]
        beside = [(index, index ^ 1) for index in range(times)]
        far = lax.ppermute(snapshots, "tm", across)
        near = lax.ppermute(snapshots, "tm", beside)
        far, own, *weights = lax.optimization_barrier((far, own, *weights))
        both = lax.ppermute(far, "tm", beside)
        blocks = [own, far, near, both]
    else:
        blocks = [own] + [
            lax.ppermute(snapshots, "tm", ring(times, -offset)) for offset in offsets[1:]
        ]

    if paired:
        message = pl.pallas_call(
            pack_kernel,
            out_shape=jax.ShapeDtypeStruct((total, plane), BF16),
            in_specs=[VMEM] * len(blocks),
            out_specs=VMEM,
            compiler_params=PARAMS,
            name="pack",
        )(*blocks)
        pairs = []
        for time in range(times):
            for space in range(spaces):
                step = -1 if (space + time) % 2 == 0 else 1
                target = (space + step) % spaces
                pairs.append((time * spaces + space, time * spaces + target))
        mine = lax.ppermute(message, ("tm", "space"), pairs)

    patches, inner = pl.pallas_call(
        functools.partial(inner_kernel, len(blocks)),
        out_shape=[
            jax.ShapeDtypeStruct((row_count, 9, total, plane), BF16),
            jax.ShapeDtypeStruct((frames, row_count - 2, channels, plane), BF16),
        ],
        in_specs=[VMEM] * (len(blocks) + len(weights)),
        out_specs=[VMEM] * 2,
        compiler_params=PARAMS,
        name="inner",
    )(*blocks, *weights)

    if paired:
        mine, patches, inner = lax.optimization_barrier((mine, patches, inner))
        other = lax.ppermute(mine, "tm", beside)
    else:
        low, high = [
            jnp.concatenate([block[:, row] for block in blocks], axis=0).reshape(total, plane)
            for row in (0, row_count - 1)
        ]
        mine = lax.ppermute(high, "space", ring(spaces, 1))
        other = lax.ppermute(low, "space", ring(spaces, -1))

    return pl.pallas_call(
        functools.partial(outer_kernel, paired),
        out_shape=jax.ShapeDtypeStruct((frames, row_count, channels, plane), BF16),
        in_specs=[VMEM] * (4 + len(weights)),
        out_specs=pl.BlockSpec(memory_space=pl.ANY),
        scratch_shapes=[
            pltpu.VMEM((frames, 2, channels, plane), BF16),
            pltpu.VMEM((2, 9, total, plane), BF16),
            pltpu.SemaphoreType.DMA((3,)),
        ],
        compiler_params=PARAMS,
        name="outer",
    )(mine, other, patches, inner, *weights)


def solution(mesh):
    in_specs = (P("tm", "space", None, None), P(), P(), P(), P(), P(), P())
    out_specs = P("tm", "space", None, None)
    return jax.shard_map(shards, mesh=mesh, in_specs=in_specs, out_specs=out_specs, check_vma=False)
```

profile of v0, /device:TPU:0, one launch (start us, length us, event | category | flops | bytes accessed | tf_op | source)
XLA Modules:
  0.0 17.4 jit_solution(16454438881109159313)
XLA Ops:
  0.0 2.9 %collective-permute-start = (bf16[2,4,4,512]{3,2,1,0:T(4,128)(2,1)}, bf16[2,4,4,512]{3,2,1,0:T(4,128)(2,1)S(1)}, u32[]{:S(2)}, u32[]{:S(2)}) collective-permute-start(bf16[2,4,4,512]{3,2,1,0:T(4,128)(2,1)} %refs_0_.1), channel_id=1, source_target_pairs={{0,16},{8,24},{16,0},{24,8},{1,17},{9,25},{17,1},{25,9},{2,18},{10... | collective-permute-start | bytes 98312 | tf_op jit(solution)/shard_map/ppermute | solution.py:326
  2.9 0.0 collective-permute-start.1
  2.9 1.4 %prepare.1 = (bf16[2,4,4,512]{3,2,1,0:T(4,128)(2,1)S(1)}, bf16[128,432]{1,0:T(8,128)(2,1)S(1)}, f32[128,128]{1,0:T(8,128)S(1)}, bf16[256,256]{1,0:T(8,128)(2,1)S...) custom-call(bf16[2,4,4,512]{3,2,1,0:T(4,128)(2,1)} %refs_0_.1, ...), custom_call_target="tpu_custom_call" | custom-call | tf_op jit(solution)/shard_map/prepare/pallas_call | solution.py:312
  4.4 0.7 %collective-permute-done.refs_1_.rest_1_ = bf16[2,4,4,512]{3,2,1,0:T(4,128)(2,1)S(1)} collective-permute-done((bf16[2,4,4,512]{3,2,1,0:T(4,128)(2,1)}, bf16[2,4,4,512]{3,2,1,0:T(4,128)(2,1)S(1)}, u32[]{:S(2)}, u32[]{:S(2)}) %collective-permute-start) | collective-permute-done | bytes 32800 | tf_op jit(solution)/shard_map/ppermute | solution.py:326
  5.0 0.0 collective-permute-start.2
  5.0 0.0 collective-permute-done.1.refs_2_.rest_2_
  5.0 1.2 %collective-permute-done.2.refs_3_.rest_3_ = bf16[2,4,4,512]{3,2,1,0:T(4,128)(2,1)S(1)} collective-permute-done((bf16[2,4,4,512]{3,2,1,0:T(4,128)(2,1)S(1)}, bf16[2,4,4,512]{3,2,1,0:T(4,128)(2,1)S(1)}, u32[]{:S(2)}, u32[]{:S(2)}) %collective-permute-start.2) | collective-permute-done | bytes 32800 | tf_op jit(solution)/shard_map/ppermute | solution.py:329
  6.3 5.2 %collective-permute-start.3 = (bf16[32,512]{1,0:T(8,128)(2,1)S(1)}, bf16[32,512]{1,0:T(8,128)(2,1)S(1)}, u32[]{:S(2)}, u32[]{:S(2)}) collective-permute-start(bf16[32,512]{1,0:T(8,128)(2,1)S(1)} %pack.1), channel_id=1, source_target_pairs={{0,7},{1,2},{2,1},{3,4},{4,3},{5,6},{6,5},{7,0},{8,9},{9,8},{10,11... | collective-permute-start | bytes 98312 | tf_op jit(solution)/shard_map/ppermute | solution.py:351
  11.4 2.1 %inner.1 = (bf16[4,9,32,512]{3,2,1,0:T(8,128)(2,1)S(1)}, bf16[2,2,32,512]{3,2,1,0:T(8,128)(2,1)S(1)}) custom-call(bf16[2,4,4,512]{3,2,1,0:T(4,128)(2,1)S(1)} %get-tuple-element.38.refs_0_.rest_0_, bf16[2,4,4,512]{3,2,1,0:T(4,128)(2,1)S(1)} %collective-permute-done.refs_1_.rest_1_, bf16[2,4,4,512]{3,2,1,0:T(4,128)(2,1)S(1)} %collective-permute-done.1.refs_2_.rest_2_, ...), custom_call_target="tpu_custom_call" | custom-call | tf_op jit(solution)/shard_map/inner/pallas_call | solution.py:353
  13.5 0.0 collective-permute-done.3.mine
  13.5 0.1 collective-permute-start.4
  13.6 1.2 %collective-permute-done.4.other = bf16[32,512]{1,0:T(8,128)(2,1)S(1)} collective-permute-done((bf16[32,512]{1,0:T(8,128)(2,1)S(1)}, bf16[32,512]{1,0:T(8,128)(2,1)S(1)}, u32[]{:S(2)}, u32[]{:S(2)}) %collective-permute-start.4) | collective-permute-done | bytes 32800 | tf_op jit(solution)/shard_map/ppermute | solution.py:367
  14.8 2.7 %outer.1 = bf16[2,4,32,512]{3,2,1,0:T(8,128)(2,1)} custom-call(bf16[32,512]{1,0:T(8,128)(2,1)S(1)} %collective-permute-done.3.mine, bf16[32,512]{1,0:T(8,128)(2,1)S(1)} %collective-permute-done.4.other, bf16[4,9,32,512]{3,2,1,0:T(8,128)(2,1)S(1)} %get-tuple-element.51.patches, bf16[2,2,32,512]{3,2,1,0:T(8,128)(2,1)S(1)} %get-tuple-element.52.inner, ...), custom_call_target="tpu_custom_call" | custom-call | tf_op jit(solution)/shard_map/outer/pallas_call | solution.py:376
  (1 shorter events, 0.0 us)
Async XLA Ops:
  0.0 5.0 %collective-permute-start = (bf16[2,4,4,512]{3,2,1,0:T(4,128)(2,1)}, bf16[2,4,4,512]{3,2,1,0:T(4,128)(2,1)S(1)}, u32[]{:S(2)}, u32[]{:S(2)}) collective-permute-start(bf16[2,4,4,512]{3,2,1,0:T(4,128)(2,1)} %refs_0_.1), channel_id=1, source_target_pairs={{0,16},{8,24},{16,0},{24,8},{1,17},{9,25},{17,1},{25,9},{2,18},{10... | collective-permute-start | bytes 98312 | tf_op jit(solution)/shard_map/ppermute | solution.py:326
  2.9 2.1 %collective-permute-start.1 = (bf16[2,4,4,512]{3,2,1,0:T(4,128)(2,1)}, bf16[2,4,4,512]{3,2,1,0:T(4,128)(2,1)S(1)}, u32[]{:S(2)}, u32[]{:S(2)}) collective-permute-start(bf16[2,4,4,512]{3,2,1,0:T(4,128)(2,1)} %refs_0_.1), channel_id=1, source_target_pairs={{0,8},{8,0},{16,24},{24,16},{1,9},{9,1},{17,25},{25,17},{2,10},{10... | collective-permute-start | bytes 98312 | tf_op jit(solution)/shard_map/ppermute | solution.py:327
  5.0 1.2 %collective-permute-start.2 = (bf16[2,4,4,512]{3,2,1,0:T(4,128)(2,1)S(1)}, bf16[2,4,4,512]{3,2,1,0:T(4,128)(2,1)S(1)}, u32[]{:S(2)}, u32[]{:S(2)}) collective-permute-start(bf16[2,4,4,512]{3,2,1,0:T(4,128)(2,1)S(1)} %collective-permute-done.refs_1_.rest_1_), channel_id=1, source_target_pairs={{0,8},{8,0},{16,24},{24,16},{1,9},{9,1},{17,25},{25,17},{2,10},{10... | collective-permute-start | bytes 98312 | tf_op jit(solution)/shard_map/ppermute | solution.py:329
  6.3 7.2 %collective-permute-start.3 = (bf16[32,512]{1,0:T(8,128)(2,1)S(1)}, bf16[32,512]{1,0:T(8,128)(2,1)S(1)}, u32[]{:S(2)}, u32[]{:S(2)}) collective-permute-start(bf16[32,512]{1,0:T(8,128)(2,1)S(1)} %pack.1), channel_id=1, source_target_pairs={{0,7},{1,2},{2,1},{3,4},{4,3},{5,6},{6,5},{7,0},{8,9},{9,8},{10,11... | collective-permute-start | bytes 98312 | tf_op jit(solution)/shard_map/ppermute | solution.py:351
  13.5 1.3 %collective-permute-start.4 = (bf16[32,512]{1,0:T(8,128)(2,1)S(1)}, bf16[32,512]{1,0:T(8,128)(2,1)S(1)}, u32[]{:S(2)}, u32[]{:S(2)}) collective-permute-start(bf16[32,512]{1,0:T(8,128)(2,1)S(1)} %collective-permute-done.3.mine), channel_id=1, source_target_pairs={{0,8},{8,0},{16,24},{24,16},{1,9},{9,1},{17,25},{25,17},{2,10},{10... | collective-permute-start | bytes 98312 | tf_op jit(solution)/shard_map/ppermute | solution.py:367
where the time goes:
time: 17.6 us; the launch traced here: 17.4 us
  starting transfers between devices  8.17 us (46%)
  Pallas kernels  6.15 us (35%)
  waiting for transfers between devices  3.09 us (18%)
    ppermute x1, starting transfers between devices, shards(): mine = lax.ppermute(message, ('tm', 'space'), pairs)  5.15 us
    ppermute x1, starting transfers between devices, shards(): far = lax.ppermute(snapshots, 'tm', across)  2.94 us
    pallas_call x1, Pallas kernels, shards(): pl.pallas_call(functools.partial(outer_kernel, paired), out_shape=jax.Sha...  2.67 us
    pallas_call x1, Pallas kernels, shards(): pl.pallas_call(functools.partial(inner_kernel, len(blocks)), out_shape=[j...  2.05 us
    pallas_call x1, Pallas kernels, shards(): pl.pallas_call(functools.partial(prepare_kernel, slot_of), out_shape=shap...  1.4 us
    ppermute x1, waiting for transfers between devices, shards(): both = lax.ppermute(far, 'tm', beside)  1.2 us
    ppermute x1, waiting for transfers between devices, shards(): other = lax.ppermute(mine, 'tm', beside)  1.19 us
    ppermute x1, waiting for transfers between devices, shards(): far = lax.ppermute(snapshots, 'tm', across)  0.69 us
  transfers between devices with their start and end apart: 5, of which 3 were waited for; matrix products, arithmetic and copies ran while one was open for 0% of the time, Pallas kernels for 20%

commit v1 on v0

--- a/solution.py
+++ b/solution.py
@@ -57,7 +57,7 @@
     return jnp.dot(tall, pick, preferred_element_type=F32)
 
 
-def prepare_kernel(slot_of, *refs):
+def prepare_kernel(paired, slot_of, *refs):
     sources, outs, landed, sems = refs[:7], refs[7:-7], refs[-7:-1], refs[-1]
     copies = [
         pltpu.make_async_copy(source, target, sems.at[index])
@@ -69,9 +69,9 @@
         copy.wait()
     conv, conv_shift, taps, tap_shift, mix, mix_shift = landed
     frames = outs[0].shape[0]
-    conv_out, conv_shift_out = outs[1], outs[2]
-    tap_outs = outs[3 : 3 + LEVELS]
-    tap_shift_out, mix_out, mix_shift_out = outs[3 + LEVELS :]
+    conv_outs, conv_shift_out = outs[1:4], outs[4]
+    tap_outs = outs[5 : 5 + LEVELS]
+    tap_shift_out, mix_out, mix_shift_out = outs[5 + LEVELS :]
     places, fields, channels = conv.shape
     depth = places * fields
     wide = depth * GROUP
@@ -85,7 +85,13 @@
     down = lax.broadcasted_iota(jnp.int32, full.shape, 0)
     across = lax.broadcasted_iota(jnp.int32, full.shape, 1)
     keep = down // channels == across // fields % GROUP
-    conv_out[...] = jnp.where(keep, full, 0.0).astype(BF16)
+    full = jnp.where(keep, full, 0.0)
+    third = wide // 3
+    turned = jnp.concatenate([full[:, 2 * third :], full[:, third : -third], full[:, :third]], axis=1)
+    even = parity(paired) == 0
+    conv_outs[0][...] = full.astype(BF16)
+    conv_outs[1][...] = jnp.where(even, full, turned).astype(BF16)
+    conv_outs[2][...] = jnp.where(even, turned, full).astype(BF16)
     conv_shift_out[...] = column(conv_shift[...], GROUP)
     slots = slot_of(lax.axis_index("tm"))
     for level in range(LEVELS):
@@ -125,8 +131,8 @@
             yield pltpu.roll(piece, -delta_y * NZ % plane, 1) if delta_y else piece
 
 
-def parity():
-    return lax.rem(lax.axis_index("space") + lax.axis_index("tm"), 2)
+def parity(paired):
+    return lax.rem(lax.axis_index("space"), 2) if paired else 0
 
 
 def joined(parts, axis):
@@ -179,14 +185,21 @@
     )
 
 
-def pack_kernel(*refs):
-    blocks, out = refs[:-1], refs[-1]
-    frames, row_count = blocks[0].shape[:2]
-    first, last = [
-        jnp.concatenate([block[frame, row] for block in blocks for frame in range(frames)], axis=0)
-        for row in (0, row_count - 1)
-    ]
-    out[...] = jnp.where(parity() == 0, first, last)
+def pack_kernel(edges, near, *outs):
+    frames, row_count = near.shape[:2]
+    even = parity(True) == 0
+    first = lax.rem(lax.axis_index("tm"), 2) == 0
+    for place, (out, row, other) in enumerate(
+        zip(outs, (0, row_count - 1), (row_count - 1, 0))
+    ):
+        mine = jnp.concatenate([edges[frame, place] for frame in range(frames)], axis=0)
+        beside = jnp.concatenate(
+            [jnp.where(even, near[frame, row], near[frame, other]) for frame in range(frames)],
+            axis=0,
+        )
+        out[...] = jnp.concatenate(
+            [jnp.where(first, mine, beside), jnp.where(first, beside, mine)], axis=0
+        )
 
 
 def inner_kernel(count, *rest):
@@ -217,50 +230,72 @@
     encode(windows, weights, out.shape[0], store)
 
 
-def outer_kernel(paired, mine, other, patches, inner, *rest):
-    weights, (out, edges, borders, sems) = rest[:-4], rest[-4:]
-    row_count, _, lines, plane = patches.shape
+def halo_lines(halos):
+    if len(halos) == 1:
+        return halos[0][...]
+    first = lax.rem(lax.axis_index("tm"), 2) == 0
+    got, other = halos[0][...], halos[1][...]
+    half = got.shape[0] // 2
+    parts = [[], []]
+    for held in (jnp.where(first, got, other), jnp.where(first, other, got)):
+        upper, lower = held[:half], held[half:]
+        parts[0].append(jnp.where(first, upper, lower))
+        parts[1].append(jnp.where(first, lower, upper))
+    return jnp.concatenate(parts[0] + parts[1], axis=0)
+
+
+def edge_row(paired, far, row_count):
+    top = (parity(paired) == 0) == far
+    return jnp.where(top, 0, row_count - 1), jnp.where(top, 1, row_count - 2)
+
+
+def encode_edge(paired, far, halos, patches, weights, border, frames, store):
+    row_count, _, _, plane = patches.shape
     depth = weights[0].shape[1] // 27
     width = math.gcd(plane, CELLS)
-    middle = pltpu.make_async_copy(inner, out.at[:, 1 : row_count - 1], sems.at[0])
-    middle.start()
-    first, second = mine[...], other[...]
-    if paired:
-        half = lines // 2
-        second = jnp.concatenate([second[half:], second[:half]], axis=0)
-        below = parity() == 0
-        first, second = jnp.where(below, first, second), jnp.where(below, second, first)
-    for index, halo in enumerate((first, second)):
-        for place, piece in enumerate(shifted(halo)):
-            borders[index, place] = piece
-    sources = [
-        [borders.at[0], patches.at[0], patches.at[1]],
-        [patches.at[row_count - 2], patches.at[row_count - 1], borders.at[1]],
-    ]
-    places = [
-        (edge, slice(start, start + width)) for edge in range(2) for start in range(0, plane, width)
-    ]
-    windows = [
-        functools.partial(stack, sources[edge], depth=depth, cells=cells) for edge, cells in places
-    ]
-
-    def store(index, frame, final):
-        edge, cells = places[index]
-        edges[frame, edge, :, cells] = final
-
-    encode(windows, weights, out.shape[0], store)
+    for place, piece in enumerate(shifted(halo_lines(halos))):
+        border[place] = piece
+    edge, inside = edge_row(paired, far, row_count)
+    cells = [slice(start, start + width) for start in range(0, plane, width)]
+    sources = [border, patches.at[edge], patches.at[inside]]
+    windows = [functools.partial(stack, sources, depth=depth, cells=part) for part in cells]
+    encode(windows, weights, frames, lambda index, frame, final: store(frame, cells[index], final))
+
+
+def near_kernel(paired, count, *refs):
+    halos, patches, weights, (out, border) = refs[:count], refs[count], refs[count + 1 : -2], refs[-2:]
+
+    def store(frame, cells, final):
+        out[frame, :, cells] = final
+
+    encode_edge(paired, False, halos, patches, weights, border, out.shape[0], store)
+
+
+def far_kernel(paired, count, *refs):
+    halos, patches, inner, near = refs[:count], *refs[count : count + 3]
+    weights, (out, border, done, sems) = refs[count + 3 : -4], refs[-4:]
+    row_count = patches.shape[0]
+    far_row, _ = edge_row(paired, True, row_count)
+    near_row, _ = edge_row(paired, False, row_count)
     copies = [
-        pltpu.make_async_copy(edges.at[:, edge], out.at[:, row], sems.at[edge + 1])
-        for edge, row in ((0, 0), (1, row_count - 1))
+        pltpu.make_async_copy(inner, out.at[:, 1 : row_count - 1], sems.at[0]),
+        pltpu.make_async_copy(near, out.at[:, near_row], sems.at[1]),
     ]
     for copy in copies:
         copy.start()
-    middle.wait()
+
+    def store(frame, cells, final):
+        done[frame, :, cells] = final
+
+    encode_edge(paired, True, halos, patches, weights, border, out.shape[0], store)
+    copies.append(pltpu.make_async_copy(done, out.at[:, far_row], sems.at[2]))
+    copies[-1].start()
     for copy in copies:
         copy.wait()
 
 
 VMEM = pl.BlockSpec(memory_space=pltpu.VMEM)
+CHEAP = pl.CostEstimate(flops=1, bytes_accessed=1, transcendentals=0)
 PARAMS = pltpu.CompilerParams(vmem_limit_bytes=40 * 2**20)
 
 
@@ -278,15 +313,52 @@
     tall = GROUP * channels
     total = len(offsets) * frames * fields
 
+    sources = [
+        snapshots,
+        conv_weight.transpose(2, 3, 4, 1, 0).reshape(27, fields, channels),
+        conv_bias.reshape(1, channels),
+        tap_weight.transpose(0, 2, 1, 3),
+        tap_bias,
+        mix_weight,
+        mix_bias,
+    ]
     if paired:
         offsets = [0, 2, 1, 3]
         slot_of = lambda index: [index ^ offset for offset in offsets]
+        across = [(index, index ^ 2) for index in range(times)]
+        beside = [(index, index ^ 1) for index in range(times)]
+        near = lax.ppermute(snapshots, "tm", beside)
+        far = lax.ppermute(snapshots, "tm", across)
+        both = lax.ppermute(snapshots, "tm", [(index, index ^ 3) for index in range(times)])
+        even = parity(True) == 0
+        low, high = snapshots[:, 0], snapshots[:, -1]
+        edges = jnp.where(even, jnp.stack([low, high], axis=1), jnp.stack([high, low], axis=1))
+        to_far, to_near = pl.pallas_call(
+            pack_kernel,
+            out_shape=[jax.ShapeDtypeStruct((total // 2, plane), BF16)] * 2,
+            in_specs=[VMEM] * 2,
+            out_specs=[VMEM] * 2,
+            compiler_params=PARAMS,
+            cost_estimate=CHEAP,
+            name="pack",
+        )(edges, near)
+        far_pairs, near_pairs = [], []
+        for time in range(times):
+            for space in range(spaces):
+                target = (time ^ (time % 2 * 2)) * spaces
+                step = 2 * (space % 2) - 1
+                far_pairs.append((time * spaces + space, target + (space + step) % spaces))
+                near_pairs.append((time * spaces + space, target + space - step))
+        near_halo = lax.ppermute(to_near, ("tm", "space"), near_pairs)
+        far_halo = lax.ppermute(to_far, ("tm", "space"), far_pairs)
+        near_other = lax.ppermute(near_halo, "tm", beside)
+        near_halos = [near_halo, near_other]
     else:
         slot_of = lambda index: [(index + offset) % times for offset in offsets]
 
     shapes = [
         jax.ShapeDtypeStruct(snapshots.shape, BF16),
-        jax.ShapeDtypeStruct((tall, 27 * GROUP * fields), BF16),
+        *[jax.ShapeDtypeStruct((tall, 27 * GROUP * fields), BF16)] * 3,
         jax.ShapeDtypeStruct((tall, 128), F32),
     ]
     for level in range(LEVELS):
@@ -299,56 +371,31 @@
         jax.ShapeDtypeStruct((LEVELS, tall, tall), BF16),
         jax.ShapeDtypeStruct((LEVELS, tall, 128), F32),
     ]
-    sources = [
-        snapshots,
-        conv_weight.transpose(2, 3, 4, 1, 0).reshape(27, fields, channels),
-        conv_bias.reshape(1, channels),
-        tap_weight.transpose(0, 2, 1, 3),
-        tap_bias,
-        mix_weight,
-        mix_bias,
-    ]
     sources = [pltpu.with_memory_space_constraint(source, pltpu.HBM) for source in sources]
-    own, *weights = pl.pallas_call(
-        functools.partial(prepare_kernel, slot_of),
+    own, conv, conv_far, conv_near, *weights = pl.pallas_call(
+        functools.partial(prepare_kernel, paired, slot_of),
         out_shape=shapes,
         in_specs=[pl.BlockSpec(memory_space=pl.ANY)] * len(sources),
         out_specs=[VMEM] * len(shapes),
         scratch_shapes=[pltpu.VMEM(source.shape, source.dtype) for source in sources[1:]]
         + [pltpu.SemaphoreType.DMA((len(sources),))],
         compiler_params=PARAMS,
+        cost_estimate=CHEAP,
         name="prepare",
     )(*sources)
 
     if paired:
-        across = [(index, index ^ 2) for index in range(times)]
-        beside = [(index, index ^ 1) for index in range(times)]
-        far = lax.ppermute(snapshots, "tm", across)
-        near = lax.ppermute(snapshots, "tm", beside)
-        far, own, *weights = lax.optimization_barrier((far, own, *weights))
-        both = lax.ppermute(far, "tm", beside)
         blocks = [own, far, near, both]
     else:
         blocks = [own] + [
             lax.ppermute(snapshots, "tm", ring(times, -offset)) for offset in offsets[1:]
         ]
-
-    if paired:
-        message = pl.pallas_call(
-            pack_kernel,
-            out_shape=jax.ShapeDtypeStruct((total, plane), BF16),
-            in_specs=[VMEM] * len(blocks),
-            out_specs=VMEM,
-            compiler_params=PARAMS,
-            name="pack",
-        )(*blocks)
-        pairs = []
-        for time in range(times):
-            for space in range(spaces):
-                step = -1 if (space + time) % 2 == 0 else 1
-                target = (space + step) % spaces
-                pairs.append((time * spaces + space, time * spaces + target))
-        mine = lax.ppermute(message, ("tm", "space"), pairs)
+        low, high = [
+            jnp.concatenate([block[:, row] for block in blocks], axis=0).reshape(total, plane)
+            for row in (0, row_count - 1)
+        ]
+        far_halos = [lax.ppermute(high, "space", ring(spaces, 1))]
+        near_halos = [lax.ppermute(low, "space", ring(spaces, -1))]
 
     patches, inner = pl.pallas_call(
         functools.partial(inner_kernel, len(blocks)),
@@ -356,36 +403,43 @@
             jax.ShapeDtypeStruct((row_count, 9, total, plane), BF16),
             jax.ShapeDtypeStruct((frames, row_count - 2, channels, plane), BF16),
         ],
-        in_specs=[VMEM] * (len(blocks) + len(weights)),
+        in_specs=[VMEM] * (len(blocks) + 1 + len(weights)),
         out_specs=[VMEM] * 2,
         compiler_params=PARAMS,
+        cost_estimate=CHEAP,
         name="inner",
-    )(*blocks, *weights)
+    )(*blocks, conv, *weights)
 
     if paired:
-        mine, patches, inner = lax.optimization_barrier((mine, patches, inner))
-        other = lax.ppermute(mine, "tm", beside)
-    else:
-        low, high = [
-            jnp.concatenate([block[:, row] for block in blocks], axis=0).reshape(total, plane)
-            for row in (0, row_count - 1)
-        ]
-        mine = lax.ppermute(high, "space", ring(spaces, 1))
-        other = lax.ppermute(low, "space", ring(spaces, -1))
+        far_halo, patches, inner = lax.optimization_barrier((far_halo, patches, inner))
+        far_other = lax.ppermute(far_halo, "tm", beside)
+        far_halos = [far_halo, far_other]
+
+    near = pl.pallas_call(
+        functools.partial(near_kernel, paired, len(near_halos)),
+        out_shape=jax.ShapeDtypeStruct((frames, channels, plane), BF16),
+        in_specs=[VMEM] * (len(near_halos) + 2 + len(weights)),
+        out_specs=VMEM,
+        scratch_shapes=[pltpu.VMEM((9, total, plane), BF16)],
+        compiler_params=PARAMS,
+        cost_estimate=CHEAP,
+        name="near",
+    )(*near_halos, patches, conv_near, *weights)
 
     return pl.pallas_call(
-        functools.partial(outer_kernel, paired),
+        functools.partial(far_kernel, paired, len(far_halos)),
         out_shape=jax.ShapeDtypeStruct((frames, row_count, channels, plane), BF16),
-        in_specs=[VMEM] * (4 + len(weights)),
+        in_specs=[VMEM] * (len(far_halos) + 4 + len(weights)),
         out_specs=pl.BlockSpec(memory_space=pl.ANY),
         scratch_shapes=[
-            pltpu.VMEM((frames, 2, channels, plane), BF16),
-            pltpu.VMEM((2, 9, total, plane), BF16),
+            pltpu.VMEM((9, total, plane), BF16),
+            pltpu.VMEM((frames, channels, plane), BF16),
             pltpu.SemaphoreType.DMA((3,)),
         ],
         compiler_params=PARAMS,
-        name="outer",
-    )(mine, other, patches, inner, *weights)
+        cost_estimate=CHEAP,
+        name="far",
+    )(*far_halos, patches, inner, near, conv_far, *weights)
 
 
 def solution(mesh):

time: 17.6 us -> 18.2 us (1.034)
  waiting for transfers between devices: 3.09 us -> 0.77 us
  starting transfers between devices: 8.17 us -> 9.21 us
  Pallas kernels: 6.15 us -> 7.19 us
  local copies, waits for them, and re-layouts: 0 us -> 0.74 us
    ppermute x3 -> x5, waiting for transfers between devices: 2.4 us -> 0.76 us  [the longest x1 0.75 us: shards(): near_other = lax.ppermute(near_halo, 'tm', beside)]
    ppermute x3 -> x5, starting transfers between devices: 5.23 us -> 6.27 us  [the longest x1 3.54 us: shards(): far_halo = lax.ppermute(to_far, ('tm', 'space'), far_pairs)]
    pallas_call x3 -> x4, Pallas kernels: 4.09 us -> 5.13 us  [the longest x1 2.17 us: shards(): pl.pallas_call(functools.partial(far_kernel, paired, len(far_halos)), out...]
    slice x0 -> x1, local copies, waits for them, and re-layouts: none -> 0.74 us  [shards(): low, high = (snapshots[:, 0], snapshots[:, -1])]
    ppermute x1, waiting for transfers between devices: 0.69 us -> 0.01 us  [shards(): far = lax.ppermute(snapshots, 'tm', across)]
    ppermute x1, starting transfers between devices: 0.01 us -> 0.45 us  [shards(): near = lax.ppermute(snapshots, 'tm', beside)]
    ppermute x1, starting transfers between devices: 2.94 us -> 2.49 us  [shards(): far = lax.ppermute(snapshots, 'tm', across)]
  transfers between devices with their start and end apart: 5 -> 7, of which waited for: 3 -> 1; matrix products, arithmetic and copies ran while one was open for 0% -> 4% of each run, Pallas kernels for 20% -> 28%
where the time goes in v1:
time: 18.2 us; the launch traced here: 18 us
  starting transfers between devices  9.21 us (51%)
  Pallas kernels  7.19 us (40%)
  waiting for transfers between devices  0.77 us (4%)
  local copies, waits for them, and re-layouts  0.74 us (4%)
    ppermute x1, starting transfers between devices, shards(): far_halo = lax.ppermute(to_far, ('tm', 'space'), far_pairs)  3.54 us
    ppermute x1, starting transfers between devices, shards(): far = lax.ppermute(snapshots, 'tm', across)  2.49 us
    pallas_call x1, Pallas kernels, shards(): pl.pallas_call(functools.partial(far_kernel, paired, len(far_halos)), out...  2.17 us
    pallas_call x1, Pallas kernels, shards(): pl.pallas_call(functools.partial(inner_kernel, len(blocks)), out_shape=[j...  2.06 us
    ppermute x1, starting transfers between devices, shards(): near_halo = lax.ppermute(to_near, ('tm', 'space'), near_pairs)  1.81 us
    pallas_call x1, Pallas kernels, shards(): pl.pallas_call(functools.partial(near_kernel, paired, len(near_halos)), o...  1.5 us
    pallas_call x1, Pallas kernels, shards(): pl.pallas_call(functools.partial(prepare_kernel, paired, slot_of), out_sh...  1.43 us
    ppermute x1, waiting for transfers between devices, shards(): near_other = lax.ppermute(near_halo, 'tm', beside)  0.75 us
  transfers between devices with their start and end apart: 7, of which 1 were waited for; matrix products, arithmetic and copies ran while one was open for 4% of the time, Pallas kernels for 28%

profile of v1, /device:TPU:0, one launch (start us, length us, event | category | flops | bytes accessed | tf_op | source)
XLA Modules:
  0.0 18.0 jit_solution(12134284389226114706)
XLA Ops:
  0.0 0.5 %collective-permute-start = (bf16[2,4,4,512]{3,2,1,0:T(4,128)(2,1)}, bf16[2,4,4,512]{3,2,1,0:T(4,128)(2,1)S(1)}, u32[]{:S(2)}, u32[]{:S(2)}) collective-permute-start(bf16[2,4,4,512]{3,2,1,0:T(4,128)(2,1)} %refs_0_.1), channel_id=1, source_target_pairs={{0,8},{8,0},{16,24},{24,16},{1,9},{9,1},{17,25},{25,17},{2,10},{10... | collective-permute-start | bytes 98312 | tf_op jit(solution)/shard_map/ppermute | solution.py:330
  0.5 2.5 %collective-permute-start.2 = (bf16[2,4,4,512]{3,2,1,0:T(4,128)(2,1)}, bf16[2,4,4,512]{3,2,1,0:T(4,128)(2,1)S(1)}, u32[]{:S(2)}, u32[]{:S(2)}) collective-permute-start(bf16[2,4,4,512]{3,2,1,0:T(4,128)(2,1)} %refs_0_.1), channel_id=1, source_target_pairs={{0,16},{8,24},{16,0},{24,8},{1,17},{9,25},{17,1},{25,9},{2,18},{10... | collective-permute-start | bytes 98312 | tf_op jit(solution)/shard_map/ppermute | solution.py:331
  2.9 0.1 collective-permute-start.3
  3.1 0.7 %fusion = (bf16[2,1,4,512]{3,2,1,0:T(4,128)(2,1)S(1)}, bf16[2,1,4,512]{3,2,1,0:T(4,128)(2,1)S(1)}) fusion(bf16[2,4,4,512]{3,2,1,0:T(4,128)(2,1)} %refs_0_.1), kind=kLoop, calls=%fused_computation.1 | loop fusion | bytes 32768 | tf_op jit(solution)/shard_map/slice | solution.py:334
  3.9 0.0 collective-permute-done.near.rest_2_
  3.9 1.8 %collective-permute-start.5 = (bf16[16,512]{1,0:T(8,128)(2,1)S(1)}, bf16[16,512]{1,0:T(8,128)(2,1)S(1)}, u32[]{:S(2)}, u32[]{:S(2)}) collective-permute-start(bf16[16,512]{1,0:T(8,128)(2,1)S(1)} %get-tuple-element.38), channel_id=1, source_target_pairs={{0,1},{1,0},{2,3},{3,2},{4,5},{5,4},{6,7},{7,6},{8,25},{9,24},{10,... | collective-permute-start | bytes 49160 | tf_op jit(solution)/shard_map/ppermute | solution.py:352
  5.7 3.5 %collective-permute-start.1 = (bf16[16,512]{1,0:T(8,128)(2,1)S(1)}, bf16[16,512]{1,0:T(8,128)(2,1)S(1)}, u32[]{:S(2)}, u32[]{:S(2)}) collective-permute-start(bf16[16,512]{1,0:T(8,128)(2,1)S(1)} %get-tuple-element.23), channel_id=1, source_target_pairs={{0,7},{1,2},{2,1},{3,4},{4,3},{5,6},{6,5},{7,0},{8,31},{9,26},{10,... | collective-permute-start | bytes 49160 | tf_op jit(solution)/shard_map/ppermute | solution.py:353
  9.3 1.4 %prepare.1 = (bf16[2,4,4,512]{3,2,1,0:T(4,128)(2,1)S(1)}, bf16[128,432]{1,0:T(8,128)(2,1)S(1)}, bf16[128,432]{1,0:T(8,128)(2,1)S(1)}, bf16[128,432]{1,0:T(8,128)...) custom-call(bf16[2,4,4,512]{3,2,1,0:T(4,128)(2,1)} %refs_0_.1, ...), custom_call_target="tpu_custom_call" | custom-call | flops 1 | bytes 1 | tf_op jit(solution)/shard_map/prepare/pallas_call | solution.py:375
  10.7 0.0 collective-permute-done.2.rest_1_
  10.7 0.0 collective-permute-done.3.rest_3_
  10.7 2.1 %inner.1 = (bf16[4,9,32,512]{3,2,1,0:T(8,128)(2,1)S(1)}, bf16[2,2,32,512]{3,2,1,0:T(8,128)(2,1)S(1)}) custom-call(bf16[2,4,4,512]{3,2,1,0:T(4,128)(2,1)S(1)} %get-tuple-element.24.rest_0_, bf16[2,4,4,512]{3,2,1,0:T(4,128)(2,1)S(1)} %collective-permute-done.2.rest_1_, bf16[2,4,4,512]{3,2,1,0:T(4,128)(2,1)S(1)} %collective-permute-done.near.rest_2_, ...), custom_call_target="tpu_custom_call" | custom-call | flops 1 | bytes 1 | tf_op jit(solution)/shard_map/inner/pallas_call | solution.py:400
  12.8 0.0 collective-permute-done.5.refs_0_
  12.8 0.7 %collective-permute-start.6 = (bf16[16,512]{1,0:T(8,128)(2,1)S(1)}, bf16[16,512]{1,0:T(8,128)(2,1)S(1)}, u32[]{:S(2)}, u32[]{:S(2)}) collective-permute-start(bf16[16,512]{1,0:T(8,128)(2,1)S(1)} %collective-permute-done.5.refs_0_), channel_id=1, source_target_pairs={{0,8},{8,0},{16,24},{24,16},{1,9},{9,1},{17,25},{25,17},{2,10},{10... | collective-permute-start | bytes 49160 | tf_op jit(solution)/shard_map/ppermute | solution.py:354
  13.5 0.0 collective-permute-done.1.refs_0_
  13.5 0.1 collective-permute-start.4
  13.6 0.7 %collective-permute-done.6.refs_1_ = bf16[16,512]{1,0:T(8,128)(2,1)S(1)} collective-permute-done((bf16[16,512]{1,0:T(8,128)(2,1)S(1)}, bf16[16,512]{1,0:T(8,128)(2,1)S(1)}, u32[]{:S(2)}, u32[]{:S(2)}) %collective-permute-start.6) | collective-permute-done | bytes 16416 | tf_op jit(solution)/shard_map/ppermute | solution.py:354
  14.3 1.5 %near.1.refs_4_ = bf16[2,32,512]{2,1,0:T(8,128)(2,1)S(1)} custom-call(bf16[16,512]{1,0:T(8,128)(2,1)S(1)} %collective-permute-done.5.refs_0_, bf16[16,512]{1,0:T(8,128)(2,1)S(1)} %collective-permute-done.6.refs_1_, bf16[4,9,32,512]{3,2,1,0:T(8,128)(2,1)S(1)} %get-tuple-element.36.refs_2_, bf16[128,432]{1,0:T(8,128)(2,1)S(1)} %get-tuple-element.39.refs_3_, ...), custom_call_target="tpu_custom_call" | custom-call | flops 1 | bytes 1 | tf_op jit(solution)/shard_map/near/pallas_call | solution.py:418
  15.8 0.0 collective-permute-done.4.refs_1_
  15.8 2.2 %far.1 = bf16[2,4,32,512]{3,2,1,0:T(8,128)(2,1)} custom-call(bf16[16,512]{1,0:T(8,128)(2,1)S(1)} %collective-permute-done.1.refs_0_, bf16[16,512]{1,0:T(8,128)(2,1)S(1)} %collective-permute-done.4.refs_1_, bf16[4,9,32,512]{3,2,1,0:T(8,128)(2,1)S(1)} %get-tuple-element.36.refs_2_, bf16[2,2,32,512]{3,2,1,0:T(8,128)(2,1)S(1)} %get-tuple-element.37.refs_3_, ...), custom_call_target="tpu_custom_call" | custom-call | flops 1 | bytes 1 | tf_op jit(solution)/shard_map/far/pallas_call | solution.py:429
  (2 shorter events, 0.0 us)
Async XLA Ops:
  0.0 3.9 %collective-permute-start = (bf16[2,4,4,512]{3,2,1,0:T(4,128)(2,1)}, bf16[2,4,4,512]{3,2,1,0:T(4,128)(2,1)S(1)}, u32[]{:S(2)}, u32[]{:S(2)}) collective-permute-start(bf16[2,4,4,512]{3,2,1,0:T(4,128)(2,1)} %refs_0_.1), channel_id=1, source_target_pairs={{0,8},{8,0},{16,24},{24,16},{1,9},{9,1},{17,25},{25,17},{2,10},{10... | collective-permute-start | bytes 98312 | tf_op jit(solution)/shard_map/ppermute | solution.py:330
  0.5 10.2 %collective-permute-start.2 = (bf16[2,4,4,512]{3,2,1,0:T(4,128)(2,1)}, bf16[2,4,4,512]{3,2,1,0:T(4,128)(2,1)S(1)}, u32[]{:S(2)}, u32[]{:S(2)}) collective-permute-start(bf16[2,4,4,512]{3,2,1,0:T(4,128)(2,1)} %refs_0_.1), channel_id=1, source_target_pairs={{0,16},{8,24},{16,0},{24,8},{1,17},{9,25},{17,1},{25,9},{2,18},{10... | collective-permute-start | bytes 98312 | tf_op jit(solution)/shard_map/ppermute | solution.py:331
  2.9 7.8 %collective-permute-start.3 = (bf16[2,4,4,512]{3,2,1,0:T(4,128)(2,1)}, bf16[2,4,4,512]{3,2,1,0:T(4,128)(2,1)S(1)}, u32[]{:S(2)}, u32[]{:S(2)}) collective-permute-start(bf16[2,4,4,512]{3,2,1,0:T(4,128)(2,1)} %refs_0_.1), channel_id=1, source_target_pairs={{0,24},{8,16},{16,8},{24,0},{1,25},{9,17},{17,9},{25,1},{2,26},{10... | collective-permute-start | bytes 98312 | tf_op jit(solution)/shard_map/ppermute | solution.py:332
  3.9 8.9 %collective-permute-start.5 = (bf16[16,512]{1,0:T(8,128)(2,1)S(1)}, bf16[16,512]{1,0:T(8,128)(2,1)S(1)}, u32[]{:S(2)}, u32[]{:S(2)}) collective-permute-start(bf16[16,512]{1,0:T(8,128)(2,1)S(1)} %get-tuple-element.38), channel_id=1, source_target_pairs={{0,1},{1,0},{2,3},{3,2},{4,5},{5,4},{6,7},{7,6},{8,25},{9,24},{10,... | collective-permute-start | bytes 49160 | tf_op jit(solution)/shard_map/ppermute | solution.py:352
  5.7 7.8 %collective-permute-start.1 = (bf16[16,512]{1,0:T(8,128)(2,1)S(1)}, bf16[16,512]{1,0:T(8,128)(2,1)S(1)}, u32[]{:S(2)}, u32[]{:S(2)}) collective-permute-start(bf16[16,512]{1,0:T(8,128)(2,1)S(1)} %get-tuple-element.23), channel_id=1, source_target_pairs={{0,7},{1,2},{2,1},{3,4},{4,3},{5,6},{6,5},{7,0},{8,31},{9,26},{10,... | collective-permute-start | bytes 49160 | tf_op jit(solution)/shard_map/ppermute | solution.py:353
  12.8 1.5 %collective-permute-start.6 = (bf16[16,512]{1,0:T(8,128)(2,1)S(1)}, bf16[16,512]{1,0:T(8,128)(2,1)S(1)}, u32[]{:S(2)}, u32[]{:S(2)}) collective-permute-start(bf16[16,512]{1,0:T(8,128)(2,1)S(1)} %collective-permute-done.5.refs_0_), channel_id=1, source_target_pairs={{0,8},{8,0},{16,24},{24,16},{1,9},{9,1},{17,25},{25,17},{2,10},{10... | collective-permute-start | bytes 49160 | tf_op jit(solution)/shard_map/ppermute | solution.py:354
  13.5 2.3 %collective-permute-start.4 = (bf16[16,512]{1,0:T(8,128)(2,1)S(1)}, bf16[16,512]{1,0:T(8,128)(2,1)S(1)}, u32[]{:S(2)}, u32[]{:S(2)}) collective-permute-start(bf16[16,512]{1,0:T(8,128)(2,1)S(1)} %collective-permute-done.1.refs_0_), channel_id=1, source_target_pairs={{0,8},{8,0},{16,24},{24,16},{1,9},{9,1},{17,25},{25,17},{2,10},{10... | collective-permute-start | bytes 49160 | tf_op jit(solution)/shard_map/ppermute | solution.py:415

commit v2 on v1

--- a/solution.py
+++ b/solution.py
@@ -57,21 +57,31 @@
     return jnp.dot(tall, pick, preferred_element_type=F32)
 
 
-def prepare_kernel(paired, slot_of, *refs):
-    sources, outs, landed, sems = refs[:7], refs[7:-7], refs[-7:-1], refs[-1]
+def fetch_kernel(*refs):
+    count = len(refs) // 2
+    sems = refs[-1]
     copies = [
-        pltpu.make_async_copy(source, target, sems.at[index])
-        for index, (source, target) in enumerate(zip(sources, (outs[0], *landed)))
+        pltpu.make_async_copy(refs[index], refs[count + index], sems.at[index])
+        for index in range(count)
     ]
     for copy in copies:
         copy.start()
     for copy in copies:
         copy.wait()
-    conv, conv_shift, taps, tap_shift, mix, mix_shift = landed
-    frames = outs[0].shape[0]
-    conv_outs, conv_shift_out = outs[1:4], outs[4]
-    tap_outs = outs[5 : 5 + LEVELS]
-    tap_shift_out, mix_out, mix_shift_out = outs[5 + LEVELS :]
+
+
+def prepare_kernel(paired, slot_of, count, *refs):
+    blocks, outs = refs[:count], refs[count + 6 :]
+    conv, conv_shift, taps, tap_shift, mix, mix_shift = refs[count : count + 6]
+    frames, row_count = blocks[0].shape[:2]
+    patches, outs = outs[0], outs[1:]
+    for row in range(row_count):
+        lines = [block[frame, row] for block in blocks for frame in range(frames)]
+        for place, piece in enumerate(shifted(jnp.concatenate(lines, axis=0))):
+            patches[row, place] = piece
+    conv_outs, conv_shift_out = outs[:3], outs[3]
+    tap_outs = outs[4 : 4 + LEVELS]
+    tap_shift_out, mix_out, mix_shift_out = outs[4 + LEVELS :]
     places, fields, channels = conv.shape
     depth = places * fields
     wide = depth * GROUP
@@ -144,14 +154,14 @@
 
 
 def encode(windows, weights, frames, store):
-    conv, conv_shift = weights[:2]
-    taps = weights[2 : 2 + LEVELS]
-    tap_shift, mix, mix_shift = weights[2 + LEVELS :]
-    tall = conv.shape[0]
+    conv_shift = weights[0]
+    taps = weights[1 : 1 + LEVELS]
+    tap_shift, mix, mix_shift = weights[1 + LEVELS :]
+    tall = conv_shift.shape[0]
     channels = tall // GROUP
     groups = taps[0].shape[1] // tall
     hidden = []
-    for window in windows:
+    for conv, window in windows:
         parts = []
         for group in range(groups):
             summed = jnp.dot(conv[...], window(group), preferred_element_type=F32)
@@ -185,40 +195,41 @@
     )
 
 
-def pack_kernel(edges, near, *outs):
+def pack_kernel(own, near, *outs):
     frames, row_count = near.shape[:2]
     even = parity(True) == 0
     first = lax.rem(lax.axis_index("tm"), 2) == 0
-    for place, (out, row, other) in enumerate(
-        zip(outs, (0, row_count - 1), (row_count - 1, 0))
-    ):
-        mine = jnp.concatenate([edges[frame, place] for frame in range(frames)], axis=0)
-        beside = jnp.concatenate(
-            [jnp.where(even, near[frame, row], near[frame, other]) for frame in range(frames)],
-            axis=0,
+    rows = []
+    for row in (0, row_count - 1):
+        mine, beside = [
+            jnp.concatenate([block[frame, row] for frame in range(frames)], axis=0)
+            for block in (own, near)
+        ]
+        rows.append(
+            jnp.concatenate(
+                [jnp.where(first, mine, beside), jnp.where(first, beside, mine)], axis=0
+            )
         )
-        out[...] = jnp.concatenate(
-            [jnp.where(first, mine, beside), jnp.where(first, beside, mine)], axis=0
-        )
-
-
-def inner_kernel(count, *rest):
-    blocks, weights, (patches, out) = rest[:count], rest[count:-2], rest[-2:]
-    frames, row_count, _, plane = blocks[0].shape
-    depth = weights[0].shape[1] // 27
+    outs[0][...] = jnp.where(even, rows[0], rows[1])
+    outs[1][...] = jnp.where(even, rows[1], rows[0])
+
+
+def inner_kernel(patches, conv, *rest):
+    weights, out = rest[:-1], rest[-1]
+    row_count, _, _, plane = patches.shape
+    depth = conv.shape[1] // 27
     width = math.gcd(plane, CELLS)
-    for index in range(row_count):
-        lines = [block[frame, index] for block in blocks for frame in range(frames)]
-        for place, piece in enumerate(shifted(jnp.concatenate(lines, axis=0))):
-            patches[index, place] = piece
     places = [
         (row, slice(start, start + width))
         for row in range(1, row_count - 1)
         for start in range(0, plane, width)
     ]
     windows = [
-        functools.partial(
-            stack, [patches.at[row + step] for step in (-1, 0, 1)], depth=depth, cells=cells
+        (
+            conv,
+            functools.partial(
+                stack, [patches.at[row + step] for step in (-1, 0, 1)], depth=depth, cells=cells
+            ),
         )
         for row, cells in places
     ]
@@ -249,54 +260,48 @@
     return jnp.where(top, 0, row_count - 1), jnp.where(top, 1, row_count - 2)
 
 
-def encode_edge(paired, far, halos, patches, weights, border, frames, store):
+def outer_kernel(paired, count, *refs):
+    halos = refs[count : 2 * count], refs[:count]
+    patches, inner, *convs = refs[2 * count : 2 * count + 4]
+    weights, (out, borders, done, sems) = refs[2 * count + 4 : -4], refs[-4:]
     row_count, _, _, plane = patches.shape
-    depth = weights[0].shape[1] // 27
+    depth = convs[0].shape[1] // 27
     width = math.gcd(plane, CELLS)
-    for place, piece in enumerate(shifted(halo_lines(halos))):
-        border[place] = piece
-    edge, inside = edge_row(paired, far, row_count)
-    cells = [slice(start, start + width) for start in range(0, plane, width)]
-    sources = [border, patches.at[edge], patches.at[inside]]
-    windows = [functools.partial(stack, sources, depth=depth, cells=part) for part in cells]
-    encode(windows, weights, frames, lambda index, frame, final: store(frame, cells[index], final))
-
-
-def near_kernel(paired, count, *refs):
-    halos, patches, weights, (out, border) = refs[:count], refs[count], refs[count + 1 : -2], refs[-2:]
-
-    def store(frame, cells, final):
-        out[frame, :, cells] = final
-
-    encode_edge(paired, False, halos, patches, weights, border, out.shape[0], store)
-
-
-def far_kernel(paired, count, *refs):
-    halos, patches, inner, near = refs[:count], *refs[count : count + 3]
-    weights, (out, border, done, sems) = refs[count + 3 : -4], refs[-4:]
-    row_count = patches.shape[0]
-    far_row, _ = edge_row(paired, True, row_count)
-    near_row, _ = edge_row(paired, False, row_count)
-    copies = [
-        pltpu.make_async_copy(inner, out.at[:, 1 : row_count - 1], sems.at[0]),
-        pltpu.make_async_copy(near, out.at[:, near_row], sems.at[1]),
-    ]
-    for copy in copies:
-        copy.start()
-
-    def store(frame, cells, final):
-        done[frame, :, cells] = final
-
-    encode_edge(paired, True, halos, patches, weights, border, out.shape[0], store)
-    copies.append(pltpu.make_async_copy(done, out.at[:, far_row], sems.at[2]))
-    copies[-1].start()
+    rows = [edge_row(paired, far, row_count) for far in (True, False)]
+    copies = [pltpu.make_async_copy(inner, out.at[:, 1 : row_count - 1], sems.at[0])]
+    copies[0].start()
+    windows = []
+    places = []
+    for side, (edge, inside) in enumerate(rows):
+        for place, piece in enumerate(shifted(halo_lines(halos[side]))):
+            borders[side, place] = piece
+        sources = [borders.at[side], patches.at[edge], patches.at[inside]]
+        for start in range(0, plane, width):
+            cells = slice(start, start + width)
+            places.append((side, cells))
+            windows.append(
+                (convs[side], functools.partial(stack, sources, depth=depth, cells=cells))
+            )
+
+    def store(index, frame, final):
+        side, cells = places[index]
+        done[side, frame, :, cells] = final
+
+    encode(windows, weights, out.shape[0], store)
+    for side, (edge, _) in enumerate(rows):
+        copies.append(pltpu.make_async_copy(done.at[side], out.at[:, edge], sems.at[side + 1]))
+        copies[-1].start()
     for copy in copies:
         copy.wait()
 
 
 VMEM = pl.BlockSpec(memory_space=pltpu.VMEM)
-CHEAP = pl.CostEstimate(flops=1, bytes_accessed=1, transcendentals=0)
 PARAMS = pltpu.CompilerParams(vmem_limit_bytes=40 * 2**20)
+
+
+def cost(microseconds):
+    size = int(microseconds * 3.7e6)
+    return pl.CostEstimate(flops=0, bytes_accessed=size, transcendentals=0)
 
 
 def ring(count, step):
@@ -322,26 +327,35 @@
         mix_weight,
         mix_bias,
     ]
+    sources = [pltpu.with_memory_space_constraint(source, pltpu.HBM) for source in sources]
+    own, *sources = pl.pallas_call(
+        fetch_kernel,
+        out_shape=[jax.ShapeDtypeStruct(source.shape, source.dtype) for source in sources],
+        in_specs=[pl.BlockSpec(memory_space=pl.ANY)] * len(sources),
+        out_specs=[VMEM] * len(sources),
+        scratch_shapes=[pltpu.SemaphoreType.DMA((len(sources),))],
+        compiler_params=PARAMS,
+        cost_estimate=cost(0.8),
+        name="fetch",
+    )(*sources)
+
     if paired:
         offsets = [0, 2, 1, 3]
         slot_of = lambda index: [index ^ offset for offset in offsets]
         across = [(index, index ^ 2) for index in range(times)]
         beside = [(index, index ^ 1) for index in range(times)]
         near = lax.ppermute(snapshots, "tm", beside)
+        both = lax.ppermute(snapshots, "tm", [(index, index ^ 3) for index in range(times)])
         far = lax.ppermute(snapshots, "tm", across)
-        both = lax.ppermute(snapshots, "tm", [(index, index ^ 3) for index in range(times)])
-        even = parity(True) == 0
-        low, high = snapshots[:, 0], snapshots[:, -1]
-        edges = jnp.where(even, jnp.stack([low, high], axis=1), jnp.stack([high, low], axis=1))
         to_far, to_near = pl.pallas_call(
             pack_kernel,
             out_shape=[jax.ShapeDtypeStruct((total // 2, plane), BF16)] * 2,
             in_specs=[VMEM] * 2,
             out_specs=[VMEM] * 2,
             compiler_params=PARAMS,
-            cost_estimate=CHEAP,
+            cost_estimate=cost(0.05),
             name="pack",
-        )(edges, near)
+        )(own, near)
         far_pairs, near_pairs = [], []
         for time in range(times):
             for space in range(spaces):
@@ -351,13 +365,11 @@
                 near_pairs.append((time * spaces + space, target + space - step))
         near_halo = lax.ppermute(to_near, ("tm", "space"), near_pairs)
         far_halo = lax.ppermute(to_far, ("tm", "space"), far_pairs)
-        near_other = lax.ppermute(near_halo, "tm", beside)
-        near_halos = [near_halo, near_other]
     else:
         slot_of = lambda index: [(index + offset) % times for offset in offsets]
 
     shapes = [
-        jax.ShapeDtypeStruct(snapshots.shape, BF16),
+        jax.ShapeDtypeStruct((row_count, 9, total, plane), BF16),
         *[jax.ShapeDtypeStruct((tall, 27 * GROUP * fields), BF16)] * 3,
         jax.ShapeDtypeStruct((tall, 128), F32),
     ]
@@ -371,19 +383,6 @@
         jax.ShapeDtypeStruct((LEVELS, tall, tall), BF16),
         jax.ShapeDtypeStruct((LEVELS, tall, 128), F32),
     ]
-    sources = [pltpu.with_memory_space_constraint(source, pltpu.HBM) for source in sources]
-    own, conv, conv_far, conv_near, *weights = pl.pallas_call(
-        functools.partial(prepare_kernel, paired, slot_of),
-        out_shape=shapes,
-        in_specs=[pl.BlockSpec(memory_space=pl.ANY)] * len(sources),
-        out_specs=[VMEM] * len(shapes),
-        scratch_shapes=[pltpu.VMEM(source.shape, source.dtype) for source in sources[1:]]
-        + [pltpu.SemaphoreType.DMA((len(sources),))],
-        compiler_params=PARAMS,
-        cost_estimate=CHEAP,
-        name="prepare",
-    )(*sources)
-
     if paired:
         blocks = [own, far, near, both]
     else:
@@ -397,49 +396,45 @@
         far_halos = [lax.ppermute(high, "space", ring(spaces, 1))]
         near_halos = [lax.ppermute(low, "space", ring(spaces, -1))]
 
-    patches, inner = pl.pallas_call(
-        functools.partial(inner_kernel, len(blocks)),
-        out_shape=[
-            jax.ShapeDtypeStruct((row_count, 9, total, plane), BF16),
-            jax.ShapeDtypeStruct((frames, row_count - 2, channels, plane), BF16),
-        ],
-        in_specs=[VMEM] * (len(blocks) + 1 + len(weights)),
-        out_specs=[VMEM] * 2,
+    patches, conv, conv_far, conv_near, *weights = pl.pallas_call(
+        functools.partial(prepare_kernel, paired, slot_of, len(blocks)),
+        out_shape=shapes,
+        in_specs=[VMEM] * (len(blocks) + len(sources)),
+        out_specs=[VMEM] * len(shapes),
         compiler_params=PARAMS,
-        cost_estimate=CHEAP,
+        cost_estimate=cost(0.9),
+        name="prepare",
+    )(*blocks, *sources)
+
+    inner = pl.pallas_call(
+        inner_kernel,
+        out_shape=jax.ShapeDtypeStruct((frames, row_count - 2, channels, plane), BF16),
+        in_specs=[VMEM] * (2 + len(weights)),
+        out_specs=VMEM,
+        compiler_params=PARAMS,
+        cost_estimate=cost(1.8),
         name="inner",
-    )(*blocks, conv, *weights)
+    )(patches, conv, *weights)
 
     if paired:
-        far_halo, patches, inner = lax.optimization_barrier((far_halo, patches, inner))
-        far_other = lax.ppermute(far_halo, "tm", beside)
-        far_halos = [far_halo, far_other]
-
-    near = pl.pallas_call(
-        functools.partial(near_kernel, paired, len(near_halos)),
-        out_shape=jax.ShapeDtypeStruct((frames, channels, plane), BF16),
-        in_specs=[VMEM] * (len(near_halos) + 2 + len(weights)),
-        out_specs=VMEM,
-        scratch_shapes=[pltpu.VMEM((9, total, plane), BF16)],
-        compiler_params=PARAMS,
-        cost_estimate=CHEAP,
-        name="near",
-    )(*near_halos, patches, conv_near, *weights)
+        near_halo, far_halo, inner = lax.optimization_barrier((near_halo, far_halo, inner))
+        near_halos = [near_halo, lax.ppermute(near_halo, "tm", beside)]
+        far_halos = [far_halo, lax.ppermute(far_halo, "tm", beside)]
 
     return pl.pallas_call(
-        functools.partial(far_kernel, paired, len(far_halos)),
+        functools.partial(outer_kernel, paired, len(far_halos)),
         out_shape=jax.ShapeDtypeStruct((frames, row_count, channels, plane), BF16),
-        in_specs=[VMEM] * (len(far_halos) + 4 + len(weights)),
+        in_specs=[VMEM] * (len(far_halos) + len(near_halos) + 4 + len(weights)),
         out_specs=pl.BlockSpec(memory_space=pl.ANY),
         scratch_shapes=[
-            pltpu.VMEM((9, total, plane), BF16),
-            pltpu.VMEM((frames, channels, plane), BF16),
+            pltpu.VMEM((2, 9, total, plane), BF16),
+            pltpu.VMEM((2, frames, channels, plane), BF16),
             pltpu.SemaphoreType.DMA((3,)),
         ],
         compiler_params=PARAMS,
-        cost_estimate=CHEAP,
-        name="far",
-    )(*far_halos, patches, inner, near, conv_far, *weights)
+        cost_estimate=cost(2.5),
+        name="outer",
+    )(*near_halos, *far_halos, patches, inner, conv_far, conv_near, *weights)
 
 
 def solution(mesh):

time: 18.2 us -> 16.9 us (0.929)
  Pallas kernels: 7.19 us -> 6.43 us
  local copies, waits for them, and re-layouts: 0.74 us -> 0 us
  waiting for transfers between devices: 0.77 us -> 1.03 us
    ppermute x1, starting transfers between devices: 2.49 us -> 0.01 us  [shards(): far = lax.ppermute(snapshots, 'tm', across)]
    ppermute x1, starting transfers between devices: 0.15 us -> 2.6 us  [shards(): lax.ppermute(snapshots, 'tm', [(index, index ^ 3) for index in range(time...]
    pallas_call x4, Pallas kernels: 7.16 us -> 6.41 us  [the longest x1 2.72 us: shards(): pl.pallas_call(functools.partial(outer_kernel, paired, len(far_halos)), o...]
    slice x1 -> x0, local copies, waits for them, and re-layouts: 0.74 us -> none  [shards(): low, high = (snapshots[:, 0], snapshots[:, -1])]
    ppermute x1, starting transfers between devices: 1.81 us -> 2.12 us  [shards(): near_halo = lax.ppermute(to_near, ('tm', 'space'), near_pairs)]
    ppermute x2, starting transfers between devices: 0.77 us -> 0.51 us  [the longest x1 0.39 us: shards(): far_halos = [far_halo, lax.ppermute(far_halo, 'tm', beside)]]
  transfers between devices with their start and end apart: 7 -> 7, of which waited for: 1 -> 3; matrix products, arithmetic and copies ran while one was open for 4% -> 0% of each run, Pallas kernels for 28% -> 22%
where the time goes in v2:
time: 16.9 us; the launch traced here: 16.7 us
  starting transfers between devices  9.23 us (55%)
  Pallas kernels  6.43 us (38%)
  waiting for transfers between devices  1.03 us (6%)
    ppermute x1, starting transfers between devices, shards(): far_halo = lax.ppermute(to_far, ('tm', 'space'), far_pairs)  3.54 us
    pallas_call x1, Pallas kernels, shards(): pl.pallas_call(functools.partial(outer_kernel, paired, len(far_halos)), o...  2.72 us
    ppermute x1, starting transfers between devices, shards(): lax.ppermute(snapshots, 'tm', [(index, index ^ 3) for index in range(time...  2.6 us
    ppermute x1, starting transfers between devices, shards(): near_halo = lax.ppermute(to_near, ('tm', 'space'), near_pairs)  2.12 us
    pallas_call x1, Pallas kernels, shards(): pl.pallas_call(inner_kernel, out_shape=jax.ShapeDtypeStruct((frames, row_...  1.84 us
    pallas_call x1, Pallas kernels, shards(): pl.pallas_call(fetch_kernel, out_shape=[jax.ShapeDtypeStruct(source.shape...  1 us
    pallas_call x1, Pallas kernels, shards(): pl.pallas_call(functools.partial(prepare_kernel, paired, slot_of, len(blo...  0.84 us
    ppermute x1, waiting for transfers between devices, shards(): near_halos = [near_halo, lax.ppermute(near_halo, 'tm', beside)]  0.67 us
  transfers between devices with their start and end apart: 7, of which 3 were waited for; matrix products, arithmetic and copies ran while one was open for 0% of the time, Pallas kernels for 22%

profile of v2, /device:TPU:0, one launch (start us, length us, event | category | flops | bytes accessed | tf_op | source)
XLA Modules:
  0.0 16.7 jit_solution(6654969561706329363)
XLA Ops:
  0.0 0.5 %collective-permute-start = (bf16[2,4,4,512]{3,2,1,0:T(4,128)(2,1)}, bf16[2,4,4,512]{3,2,1,0:T(4,128)(2,1)S(1)}, u32[]{:S(2)}, u32[]{:S(2)}) collective-permute-start(bf16[2,4,4,512]{3,2,1,0:T(4,128)(2,1)} %refs_0_.1), channel_id=1, source_target_pairs={{0,8},{8,0},{16,24},{24,16},{1,9},{9,1},{17,25},{25,17},{2,10},{10... | collective-permute-start | bytes 98312 | tf_op jit(solution)/shard_map/ppermute | solution.py:347
  0.5 2.6 %collective-permute-start.4 = (bf16[2,4,4,512]{3,2,1,0:T(4,128)(2,1)}, bf16[2,4,4,512]{3,2,1,0:T(4,128)(2,1)S(1)}, u32[]{:S(2)}, u32[]{:S(2)}) collective-permute-start(bf16[2,4,4,512]{3,2,1,0:T(4,128)(2,1)} %refs_0_.1), channel_id=1, source_target_pairs={{0,24},{8,16},{16,8},{24,0},{1,25},{9,17},{17,9},{25,1},{2,26},{10... | collective-permute-start | bytes 98312 | tf_op jit(solution)/shard_map/ppermute | solution.py:348
  3.1 0.0 collective-permute-start.3
  3.1 1.0 %fetch.1 = (bf16[2,4,4,512]{3,2,1,0:T(4,128)(2,1)S(1)}, bf16[27,4,32]{2,1,0:T(4,128)(2,1)S(1)}, f32[1,32]{1,0:T(1,128)S(1)}, bf16[3,3,32,32]{3,2,1,0:T(8,128)(2,...) custom-call(bf16[2,4,4,512]{3,2,1,0:T(4,128)(2,1)} %refs_0_.1, ...), custom_call_target="tpu_custom_call" | custom-call | bytes 2960000 | tf_op jit(solution)/shard_map/fetch/pallas_call | solution.py:331
  4.1 0.0 collective-permute-done.near.refs_2_
  4.1 2.1 %collective-permute-start.1 = (bf16[16,512]{1,0:T(8,128)(2,1)S(1)}, bf16[16,512]{1,0:T(8,128)(2,1)S(1)}, u32[]{:S(2)}, u32[]{:S(2)}) collective-permute-start(bf16[16,512]{1,0:T(8,128)(2,1)S(1)} %get-tuple-element.29), channel_id=1, source_target_pairs={{0,1},{1,0},{2,3},{3,2},{4,5},{5,4},{6,7},{7,6},{8,25},{9,24},{10,... | collective-permute-start | bytes 49160 | tf_op jit(solution)/shard_map/ppermute | solution.py:366
  6.2 3.5 %collective-permute-start.2 = (bf16[16,512]{1,0:T(8,128)(2,1)S(1)}, bf16[16,512]{1,0:T(8,128)(2,1)S(1)}, u32[]{:S(2)}, u32[]{:S(2)}) collective-permute-start(bf16[16,512]{1,0:T(8,128)(2,1)S(1)} %get-tuple-element.30), channel_id=1, source_target_pairs={{0,7},{1,2},{2,1},{3,4},{4,3},{5,6},{6,5},{7,0},{8,31},{9,26},{10,... | collective-permute-start | bytes 49160 | tf_op jit(solution)/shard_map/ppermute | solution.py:367
  9.8 0.0 collective-permute-done.4.refs_3_
  9.8 0.0 collective-permute-done.3.refs_1_
  9.8 0.8 %prepare.1 = (bf16[4,9,32,512]{3,2,1,0:T(8,128)(2,1)S(1)}, bf16[128,432]{1,0:T(8,128)(2,1)S(1)}, bf16[128,432]{1,0:T(8,128)(2,1)S(1)}, bf16[128,432]{1,0:T(8,128...) custom-call(bf16[2,4,4,512]{3,2,1,0:T(4,128)(2,1)S(1)} %get-tuple-el, ...), custom_call_target="tpu_custom_call" | custom-call | bytes 3330000 | tf_op jit(solution)/shard_map/prepare/pallas_call | solution.py:399
  10.6 1.8 %inner.1.refs_5_ = bf16[2,2,32,512]{3,2,1,0:T(8,128)(2,1)S(1)} custom-call(bf16[4,9,32,512]{3,2,1,0:T(8,128)(2,1)S(1)} %get-tuple-element.37.patches.refs_4_, bf16[128,432]{1,0:T(8,128)(2,1)S(1)} %get-tuple-element.38.conv, f32[128,128]{1,0:T(8,128)S(1)} %get-tuple-element.39.rest_0_.refs_8_, bf16[256,256]{1,0:T(8,128)(2,1)S(1)} %get-tuple-element.40.rest_1_.refs_9_, ...), custom_call_target="tpu_custom_call" | custom-call | bytes 6660000 | tf_op jit(solution)/shard_map/inner/pallas_call | solution.py:409
  12.5 0.0 collective-permute-done.1.refs_0_
  12.5 0.2 %collective-permute-done.2.refs_2_ = bf16[16,512]{1,0:T(8,128)(2,1)S(1)} collective-permute-done((bf16[16,512]{1,0:T(8,128)(2,1)S(1)}, bf16[16,512]{1,0:T(8,128)(2,1)S(1)}, u32[]{:S(2)}, u32[]{:S(2)}) %collective-permute-start.2) | collective-permute-done | bytes 16416 | tf_op jit(solution)/shard_map/ppermute | solution.py:367
  12.7 0.1 collective-permute-start.5
  12.8 0.4 %collective-permute-start.6 = (bf16[16,512]{1,0:T(8,128)(2,1)S(1)}, bf16[16,512]{1,0:T(8,128)(2,1)S(1)}, u32[]{:S(2)}, u32[]{:S(2)}) collective-permute-start(bf16[16,512]{1,0:T(8,128)(2,1)S(1)} %collective-permute-done.2.refs_2_), channel_id=1, source_target_pairs={{0,8},{8,0},{16,24},{24,16},{1,9},{9,1},{17,25},{25,17},{2,10},{10... | collective-permute-start | bytes 49160 | tf_op jit(solution)/shard_map/ppermute | solution.py:422
  13.2 0.7 %collective-permute-done.5.refs_1_ = bf16[16,512]{1,0:T(8,128)(2,1)S(1)} collective-permute-done((bf16[16,512]{1,0:T(8,128)(2,1)S(1)}, bf16[16,512]{1,0:T(8,128)(2,1)S(1)}, u32[]{:S(2)}, u32[]{:S(2)}) %collective-permute-start.5) | collective-permute-done | bytes 16416 | tf_op jit(solution)/shard_map/ppermute | solution.py:421
  13.9 0.2 collective-permute-done.6.refs_3_
  14.0 2.7 %outer.1 = bf16[2,4,32,512]{3,2,1,0:T(8,128)(2,1)} custom-call(bf16[16,512]{1,0:T(8,128)(2,1)S(1)} %collective-permute-done.1.refs_0_, bf16[16,512]{1,0:T(8,128)(2,1)S(1)} %collective-permute-done.5.refs_1_, bf16[16,512]{1,0:T(8,128)(2,1)S(1)} %collective-permute-done.2.refs_2_, bf16[16,512]{1,0:T(8,128)(2,1)S(1)} %collective-permute-done.6.refs_3_, ...), custom_call_target="tpu_custom_call" | custom-call | bytes 9250000 | tf_op jit(solution)/shard_map/outer/pallas_call | solution.py:424
  (1 shorter events, 0.0 us)
Async XLA Ops:
  0.0 4.1 %collective-permute-start = (bf16[2,4,4,512]{3,2,1,0:T(4,128)(2,1)}, bf16[2,4,4,512]{3,2,1,0:T(4,128)(2,1)S(1)}, u32[]{:S(2)}, u32[]{:S(2)}) collective-permute-start(bf16[2,4,4,512]{3,2,1,0:T(4,128)(2,1)} %refs_0_.1), channel_id=1, source_target_pairs={{0,8},{8,0},{16,24},{24,16},{1,9},{9,1},{17,25},{25,17},{2,10},{10... | collective-permute-start | bytes 98312 | tf_op jit(solution)/shard_map/ppermute | solution.py:347
  0.5 9.3 %collective-permute-start.4 = (bf16[2,4,4,512]{3,2,1,0:T(4,128)(2,1)}, bf16[2,4,4,512]{3,2,1,0:T(4,128)(2,1)S(1)}, u32[]{:S(2)}, u32[]{:S(2)}) collective-permute-start(bf16[2,4,4,512]{3,2,1,0:T(4,128)(2,1)} %refs_0_.1), channel_id=1, source_target_pairs={{0,24},{8,16},{16,8},{24,0},{1,25},{9,17},{17,9},{25,1},{2,26},{10... | collective-permute-start | bytes 98312 | tf_op jit(solution)/shard_map/ppermute | solution.py:348
  3.1 6.7 %collective-permute-start.3 = (bf16[2,4,4,512]{3,2,1,0:T(4,128)(2,1)}, bf16[2,4,4,512]{3,2,1,0:T(4,128)(2,1)S(1)}, u32[]{:S(2)}, u32[]{:S(2)}) collective-permute-start(bf16[2,4,4,512]{3,2,1,0:T(4,128)(2,1)} %refs_0_.1), channel_id=1, source_target_pairs={{0,16},{8,24},{16,0},{24,8},{1,17},{9,25},{17,1},{25,9},{2,18},{10... | collective-permute-start | bytes 98312 | tf_op jit(solution)/shard_map/ppermute | solution.py:349
  4.1 8.4 %collective-permute-start.1 = (bf16[16,512]{1,0:T(8,128)(2,1)S(1)}, bf16[16,512]{1,0:T(8,128)(2,1)S(1)}, u32[]{:S(2)}, u32[]{:S(2)}) collective-permute-start(bf16[16,512]{1,0:T(8,128)(2,1)S(1)} %get-tuple-element.29), channel_id=1, source_target_pairs={{0,1},{1,0},{2,3},{3,2},{4,5},{5,4},{6,7},{7,6},{8,25},{9,24},{10,... | collective-permute-start | bytes 49160 | tf_op jit(solution)/shard_map/ppermute | solution.py:366
  6.2 6.4 %collective-permute-start.2 = (bf16[16,512]{1,0:T(8,128)(2,1)S(1)}, bf16[16,512]{1,0:T(8,128)(2,1)S(1)}, u32[]{:S(2)}, u32[]{:S(2)}) collective-permute-start(bf16[16,512]{1,0:T(8,128)(2,1)S(1)} %get-tuple-element.30), channel_id=1, source_target_pairs={{0,7},{1,2},{2,1},{3,4},{4,3},{5,6},{6,5},{7,0},{8,31},{9,26},{10,... | collective-permute-start | bytes 49160 | tf_op jit(solution)/shard_map/ppermute | solution.py:367
  12.7 1.2 %collective-permute-start.5 = (bf16[16,512]{1,0:T(8,128)(2,1)S(1)}, bf16[16,512]{1,0:T(8,128)(2,1)S(1)}, u32[]{:S(2)}, u32[]{:S(2)}) collective-permute-start(bf16[16,512]{1,0:T(8,128)(2,1)S(1)} %collective-permute-done.1.refs_0_), channel_id=1, source_target_pairs={{0,8},{8,0},{16,24},{24,16},{1,9},{9,1},{17,25},{25,17},{2,10},{10... | collective-permute-start | bytes 49160 | tf_op jit(solution)/shard_map/ppermute | solution.py:421
  12.8 1.2 %collective-permute-start.6 = (bf16[16,512]{1,0:T(8,128)(2,1)S(1)}, bf16[16,512]{1,0:T(8,128)(2,1)S(1)}, u32[]{:S(2)}, u32[]{:S(2)}) collective-permute-start(bf16[16,512]{1,0:T(8,128)(2,1)S(1)} %collective-permute-done.2.refs_2_), channel_id=1, source_target_pairs={{0,8},{8,0},{16,24},{24,16},{1,9},{9,1},{17,25},{25,17},{2,10},{10... | collective-permute-start | bytes 49160 | tf_op jit(solution)/shard_map/ppermute | solution.py:422

commit v3 on v2

--- a/solution.py
+++ b/solution.py
@@ -35,9 +35,17 @@
     return needed, counts[::-1]
 
 
-def gelu(value):
-    half = 0.5 * value
-    return (half + half * jnp.tanh(value * (SLOPE + CUBIC * (value * value)))).astype(BF16)
+def gelu_of_double(half):
+    inner = half * (2 * SLOPE + 8 * CUBIC * (half * half))
+    return (half + half * jnp.tanh(inner)).astype(BF16)
+
+
+def joined(parts, axis):
+    return parts[0] if len(parts) == 1 else jnp.concatenate(parts, axis=axis)
+
+
+def wide(shift, cells):
+    return joined([shift] * (cells // 128), 1)
 
 
 def column(row, copies):
@@ -45,16 +53,20 @@
     down = lax.broadcasted_iota(jnp.int32, (count, count), 0)
     across = lax.broadcasted_iota(jnp.int32, (count, count), 1)
     tall = jnp.sum(jnp.where(down == across, row, 0.0), axis=1, keepdims=True)
-    return jnp.broadcast_to(jnp.concatenate([tall] * copies, axis=0), (count * copies, 128))
+    return joined([tall] * copies, 0)
+
+
+def lanes(value):
+    return jnp.broadcast_to(value, (value.shape[0], 128))
 
 
 def spread(block, rows, columns):
-    channels = block.shape[0]
-    tall = jnp.concatenate([block] * (rows // channels), axis=0)
-    down = lax.broadcasted_iota(jnp.int32, (channels, columns), 0)
-    across = lax.broadcasted_iota(jnp.int32, (channels, columns), 1)
-    pick = jnp.where(across % channels == down, 1.0, 0.0).astype(BF16)
-    return jnp.dot(tall, pick, preferred_element_type=F32)
+    height, width = block.shape
+    tile = jnp.concatenate([block] * (128 // width), axis=1)
+    parts = [tile] * (columns // 128)
+    if columns % 128:
+        parts.append(tile[:, : columns % 128])
+    return joined([joined(parts, 1)] * (rows // height), 0)
 
 
 def fetch_kernel(*refs):
@@ -81,7 +93,8 @@
             patches[row, place] = piece
     conv_outs, conv_shift_out = outs[:3], outs[3]
     tap_outs = outs[4 : 4 + LEVELS]
-    tap_shift_out, mix_out, mix_shift_out = outs[4 + LEVELS :]
+    tap_shift_outs = outs[4 + LEVELS : 4 + 2 * LEVELS]
+    mix_out, mix_shift_out = outs[4 + 2 * LEVELS :]
     places, fields, channels = conv.shape
     depth = places * fields
     wide = depth * GROUP
@@ -95,17 +108,18 @@
     down = lax.broadcasted_iota(jnp.int32, full.shape, 0)
     across = lax.broadcasted_iota(jnp.int32, full.shape, 1)
     keep = down // channels == across // fields % GROUP
-    full = jnp.where(keep, full, 0.0)
+    full = jnp.where(keep, 0.5 * full, 0.0)
     third = wide // 3
     turned = jnp.concatenate([full[:, 2 * third :], full[:, third : -third], full[:, :third]], axis=1)
     even = parity(paired) == 0
     conv_outs[0][...] = full.astype(BF16)
     conv_outs[1][...] = jnp.where(even, full, turned).astype(BF16)
     conv_outs[2][...] = jnp.where(even, turned, full).astype(BF16)
-    conv_shift_out[...] = column(conv_shift[...], GROUP)
+    conv_shift_out[...] = lanes(0.5 * column(conv_shift[...], GROUP))
     slots = slot_of(lax.axis_index("tm"))
     for level in range(LEVELS):
         rows, columns = tap_outs[level].shape
+        columns //= level + 1
 
         def frame_of(axis):
             place = lax.broadcasted_iota(jnp.int32, (rows, columns), axis) // channels
@@ -116,18 +130,36 @@
             return start + place % frames
 
         gap = frame_of(1) - frame_of(0)
-        total = jnp.zeros((rows, columns), F32)
-        for tap in range(3):
-            block = spread(taps[level, tap], rows, columns)
-            total = jnp.where(gap == (tap - 1) * 2**level, block, total)
-        tap_outs[level][...] = total.astype(BF16)
-        tap_shift_out[level] = column(tap_shift[level : level + 1], GROUP)
-        size = GROUP * channels
-        down = lax.broadcasted_iota(jnp.int32, (size, size), 0)
-        across = lax.broadcasted_iota(jnp.int32, (size, size), 1)
-        full = spread(mix[level], size, size)
-        mix_out[level] = jnp.where(down // channels == across // channels, full, 0.0).astype(BF16)
-        mix_shift_out[level] = column(mix_shift[level : level + 1], GROUP)
+        for source in range(level + 1):
+            total = jnp.zeros((rows, columns), F32)
+            for tap in range(3):
+                block = taps[level, tap]
+                if source:
+                    block = jnp.dot(block, mix[source - 1], preferred_element_type=F32)
+                block = spread(block.astype(F32), rows, columns)
+                total = jnp.where(gap == (tap - 1) * 2**level, block, total)
+            if not source:
+                shift = column(tap_shift[level : level + 1], rows // channels)
+                if level:
+                    held = jnp.sum(mix_shift[:level], axis=0, keepdims=True)
+                    held = total * spread(held, 1, columns)
+                    shift = shift + jnp.sum(held, axis=1, keepdims=True)
+                tap_shift_outs[level][...] = lanes(0.5 * shift)
+            part = slice(source * columns, (source + 1) * columns)
+            tap_outs[level][:, part] = (0.5 * total).astype(BF16)
+    size = mix_out.shape[0]
+    down = lax.broadcasted_iota(jnp.int32, (size, size), 0)
+    across = lax.broadcasted_iota(jnp.int32, (size, size), 1)
+    same = down // channels == across // channels
+    mix_out[...] = jnp.concatenate(
+        [
+            jnp.where(same, spread(mix[level].astype(F32), size, size), 0.0).astype(BF16)
+            for level in range(LEVELS)
+        ],
+        axis=1,
+    )
+    held = jnp.sum(mix_shift[...], axis=0, keepdims=True)
+    mix_shift_out[...] = lanes(column(held, size // channels))
 
 
 def shifted(lines):
@@ -145,45 +177,30 @@
     return lax.rem(lax.axis_index("space"), 2) if paired else 0
 
 
-def joined(parts, axis):
-    return parts[0] if len(parts) == 1 else jnp.concatenate(parts, axis=axis)
-
-
-def wide(shift, cells):
-    return joined([shift] * (cells // 128), 1)
-
-
 def encode(windows, weights, frames, store):
-    conv_shift = weights[0]
-    taps = weights[1 : 1 + LEVELS]
-    tap_shift, mix, mix_shift = weights[1 + LEVELS :]
-    tall = conv_shift.shape[0]
-    channels = tall // GROUP
-    groups = taps[0].shape[1] // tall
-    hidden = []
+    conv_shift, mix, mix_shift = weights[0], *weights[-2:]
+    taps, tap_shifts = weights[1 : 1 + LEVELS], weights[1 + LEVELS : 1 + 2 * LEVELS]
+    channels = conv_shift.shape[0] // GROUP
+    groups = -(-taps[0].shape[1] // conv_shift.shape[0])
+    held = []
     for conv, window in windows:
         parts = []
         for group in range(groups):
             summed = jnp.dot(conv[...], window(group), preferred_element_type=F32)
-            parts.append(gelu(summed + wide(conv_shift[...], summed.shape[1])))
-        hidden.append(joined(parts, 0))
-    for level, tap in enumerate(taps):
-        rows, columns = tap.shape
-        later = []
-        for current in hidden:
-            cells = current.shape[1]
-            summed = jnp.dot(tap[...], current[:columns], preferred_element_type=F32)
-            parts = []
-            for first in range(0, rows, tall):
-                size = min(tall, rows - first)
-                piece = summed[first : first + size]
-                gated = gelu(piece + wide(tap_shift[level, :size], cells))
-                mixed = jnp.dot(mix[level, :size, :size], gated, preferred_element_type=F32)
-                kept = current[first : first + size].astype(F32)
-                parts.append((kept + mixed + wide(mix_shift[level, :size], cells)).astype(BF16))
-            later.append(joined(parts, 0))
-        hidden = later
-    for index, final in enumerate(hidden):
+            parts.append(gelu_of_double(summed + wide(conv_shift[...], summed.shape[1])))
+        held.append([joined(parts, 0)])
+    for level, (tap, shift) in enumerate(zip(taps, tap_shifts)):
+        columns = tap.shape[1] // (level + 1)
+        for parts in held:
+            read = joined([part[:columns] for part in parts], 0)
+            summed = jnp.dot(tap[...], read, preferred_element_type=F32)
+            parts.append(gelu_of_double(summed + wide(shift[...], summed.shape[1])))
+    size = mix.shape[0]
+    for index, (first, *gated) in enumerate(held):
+        read = joined([part[:size] for part in gated], 0)
+        mixed = jnp.dot(mix[...], read, preferred_element_type=F32)
+        mixed = mixed + wide(mix_shift[...], mixed.shape[1])
+        final = (first[:size].astype(F32) + mixed).astype(BF16)
         for frame in range(frames):
             store(index, frame, final[frame * channels : (frame + 1) * channels])
 
@@ -241,11 +258,12 @@
     encode(windows, weights, out.shape[0], store)
 
 
-def halo_lines(halos):
-    if len(halos) == 1:
-        return halos[0][...]
+def merge_kernel(near, far, out):
+    out[...] = jnp.concatenate([near[...], far[...]], axis=0)
+
+
+def halo_lines(got, other):
     first = lax.rem(lax.axis_index("tm"), 2) == 0
-    got, other = halos[0][...], halos[1][...]
     half = got.shape[0] // 2
     parts = [[], []]
     for held in (jnp.where(first, got, other), jnp.where(first, other, got)):
@@ -260,10 +278,16 @@
     return jnp.where(top, 0, row_count - 1), jnp.where(top, 1, row_count - 2)
 
 
-def outer_kernel(paired, count, *refs):
-    halos = refs[count : 2 * count], refs[:count]
-    patches, inner, *convs = refs[2 * count : 2 * count + 4]
-    weights, (out, borders, done, sems) = refs[2 * count + 4 : -4], refs[-4:]
+def outer_kernel(paired, near, far, *refs):
+    near, far = near[...], far[...]
+    if paired:
+        half = refs[0].shape[0] // 2
+        near = halo_lines(near, refs[0][:half])
+        far = halo_lines(far, refs[0][half:])
+        refs = refs[1:]
+    halos = far, near
+    patches, inner, *convs = refs[:4]
+    weights, (out, borders, done, sems) = refs[4:-4], refs[-4:]
     row_count, _, _, plane = patches.shape
     depth = convs[0].shape[1] // 27
     width = math.gcd(plane, CELLS)
@@ -273,7 +297,7 @@
     windows = []
     places = []
     for side, (edge, inside) in enumerate(rows):
-        for place, piece in enumerate(shifted(halo_lines(halos[side]))):
+        for place, piece in enumerate(shifted(halos[side])):
             borders[side, place] = piece
         sources = [borders.at[side], patches.at[edge], patches.at[inside]]
         for start in range(0, plane, width):
@@ -373,16 +397,17 @@
         *[jax.ShapeDtypeStruct((tall, 27 * GROUP * fields), BF16)] * 3,
         jax.ShapeDtypeStruct((tall, 128), F32),
     ]
+    wide_of = [count * frames * channels for count in counts]
     for level in range(LEVELS):
-        rows, columns = counts[level + 1], counts[level]
-        shapes.append(
-            jax.ShapeDtypeStruct((rows * frames * channels, columns * frames * channels), BF16)
-        )
+        shape = wide_of[level + 1], wide_of[level] * (level + 1)
+        shapes.append(jax.ShapeDtypeStruct(shape, BF16))
+    for level in range(LEVELS):
+        shapes.append(jax.ShapeDtypeStruct((wide_of[level + 1], 128), F32))
     shapes += [
-        jax.ShapeDtypeStruct((LEVELS, tall, 128), F32),
-        jax.ShapeDtypeStruct((LEVELS, tall, tall), BF16),
-        jax.ShapeDtypeStruct((LEVELS, tall, 128), F32),
-    ]
+        jax.ShapeDtypeStruct((wide_of[LEVELS], wide_of[LEVELS] * LEVELS), BF16),
+        jax.ShapeDtypeStruct((wide_of[LEVELS], 128), F32),
+    ]
+
     if paired:
         blocks = [own, far, near, both]
     else:
@@ -393,8 +418,10 @@
             jnp.concatenate([block[:, row] for block in blocks], axis=0).reshape(total, plane)
             for row in (0, row_count - 1)
         ]
-        far_halos = [lax.ppermute(high, "space", ring(spaces, 1))]
-        near_halos = [lax.ppermute(low, "space", ring(spaces, -1))]
+        halos = [
+            lax.ppermute(low, "space", ring(spaces, -1)),
+            lax.ppermute(high, "space", ring(spaces, 1)),
+        ]
 
     patches, conv, conv_far, conv_near, *weights = pl.pallas_call(
         functools.partial(prepare_kernel, paired, slot_of, len(blocks)),
@@ -418,13 +445,21 @@
 
     if paired:
         near_halo, far_halo, inner = lax.optimization_barrier((near_halo, far_halo, inner))
-        near_halos = [near_halo, lax.ppermute(near_halo, "tm", beside)]
-        far_halos = [far_halo, lax.ppermute(far_halo, "tm", beside)]
+        merged = pl.pallas_call(
+            merge_kernel,
+            out_shape=jax.ShapeDtypeStruct((total, plane), BF16),
+            in_specs=[VMEM] * 2,
+            out_specs=VMEM,
+            compiler_params=PARAMS,
+            cost_estimate=cost(0.05),
+            name="merge",
+        )(near_halo, far_halo)
+        halos = [near_halo, far_halo, lax.ppermute(merged, "tm", beside)]
 
     return pl.pallas_call(
-        functools.partial(outer_kernel, paired, len(far_halos)),
+        functools.partial(outer_kernel, paired),
         out_shape=jax.ShapeDtypeStruct((frames, row_count, channels, plane), BF16),
-        in_specs=[VMEM] * (len(far_halos) + len(near_halos) + 4 + len(weights)),
+        in_specs=[VMEM] * (len(halos) + 4 + len(weights)),
         out_specs=pl.BlockSpec(memory_space=pl.ANY),
         scratch_shapes=[
             pltpu.VMEM((2, 9, total, plane), BF16),
@@ -434,7 +469,7 @@
         compiler_params=PARAMS,
         cost_estimate=cost(2.5),
         name="outer",
-    )(*near_halos, *far_halos, patches, inner, conv_far, conv_near, *weights)
+    )(*halos, patches, inner, conv_far, conv_near, *weights)
 
 
 def solution(mesh):

time: 16.9 us -> 16.2 us (0.959)
  Pallas kernels: 6.43 us -> 5.87 us
  starting transfers between devices: 9.23 us -> 8.84 us
  waiting for transfers between devices: 1.03 us -> 1.33 us
    pallas_call x1 -> x2, Pallas kernels: 2.72 us -> 2.21 us  [the longest x1 2.21 us: shards(): pl.pallas_call(functools.partial(outer_kernel, paired), out_shape=jax.Sha...]
    pallas_call x1, Pallas kernels: 1.84 us -> 1.39 us  [shards(): pl.pallas_call(inner_kernel, out_shape=jax.ShapeDtypeStruct((frames, row_...]
    pallas_call x1, Pallas kernels: 0.84 us -> 1.25 us  [shards(): pl.pallas_call(functools.partial(prepare_kernel, paired, slot_of, len(blo...]
    ppermute x2 -> x1, starting transfers between devices: 0.51 us -> 0.12 us  [shards(): halos = [near_halo, far_halo, lax.ppermute(merged, 'tm', beside)]]
    ppermute x2 -> x1, waiting for transfers between devices: 0.84 us -> 1.09 us  [shards(): halos = [near_halo, far_halo, lax.ppermute(merged, 'tm', beside)]]
  transfers between devices with their start and end apart: 7 -> 6, of which waited for: 3 -> 2; matrix products, arithmetic and copies ran while one was open for 0% -> 0% of each run, Pallas kernels for 22% -> 23%
where the time goes in v3:
time: 16.2 us; the launch traced here: 16.1 us
  starting transfers between devices  8.84 us (55%)
  Pallas kernels  5.87 us (36%)
  waiting for transfers between devices  1.33 us (8%)
    ppermute x1, starting transfers between devices, shards(): far_halo = lax.ppermute(to_far, ('tm', 'space'), far_pairs)  3.54 us
    ppermute x1, starting transfers between devices, shards(): lax.ppermute(snapshots, 'tm', [(index, index ^ 3) for index in range(time...  2.6 us
    pallas_call x1, Pallas kernels, shards(): pl.pallas_call(functools.partial(outer_kernel, paired), out_shape=jax.Sha...  2.21 us
    ppermute x1, starting transfers between devices, shards(): near_halo = lax.ppermute(to_near, ('tm', 'space'), near_pairs)  2.12 us
    pallas_call x1, Pallas kernels, shards(): pl.pallas_call(inner_kernel, out_shape=jax.ShapeDtypeStruct((frames, row_...  1.39 us
    pallas_call x1, Pallas kernels, shards(): pl.pallas_call(functools.partial(prepare_kernel, paired, slot_of, len(blo...  1.25 us
    ppermute x1, waiting for transfers between devices, shards(): halos = [near_halo, far_halo, lax.ppermute(merged, 'tm', beside)]  1.09 us
    pallas_call x1, Pallas kernels, shards(): pl.pallas_call(fetch_kernel, out_shape=[jax.ShapeDtypeStruct(source.shape...  1 us
  transfers between devices with their start and end apart: 6, of which 2 were waited for; matrix products, arithmetic and copies ran while one was open for 0% of the time, Pallas kernels for 23%

profile of v3, /device:TPU:0, one launch (start us, length us, event | category | flops | bytes accessed | tf_op | source)
XLA Modules:
  0.0 16.1 jit_solution(9788811389420303201)
XLA Ops:
  0.0 0.5 %collective-permute-start = (bf16[2,4,4,512]{3,2,1,0:T(4,128)(2,1)}, bf16[2,4,4,512]{3,2,1,0:T(4,128)(2,1)S(1)}, u32[]{:S(2)}, u32[]{:S(2)}) collective-permute-start(bf16[2,4,4,512]{3,2,1,0:T(4,128)(2,1)} %refs_0_.1), channel_id=1, source_target_pairs={{0,8},{8,0},{16,24},{24,16},{1,9},{9,1},{17,25},{25,17},{2,10},{10... | collective-permute-start | bytes 98312 | tf_op jit(solution)/shard_map/ppermute | solution.py:371
  0.5 2.6 %collective-permute-start.4 = (bf16[2,4,4,512]{3,2,1,0:T(4,128)(2,1)}, bf16[2,4,4,512]{3,2,1,0:T(4,128)(2,1)S(1)}, u32[]{:S(2)}, u32[]{:S(2)}) collective-permute-start(bf16[2,4,4,512]{3,2,1,0:T(4,128)(2,1)} %refs_0_.1), channel_id=1, source_target_pairs={{0,24},{8,16},{16,8},{24,0},{1,25},{9,17},{17,9},{25,1},{2,26},{10... | collective-permute-start | bytes 98312 | tf_op jit(solution)/shard_map/ppermute | solution.py:372
  3.1 0.0 collective-permute-start.3
  3.1 1.0 %fetch.1 = (bf16[2,4,4,512]{3,2,1,0:T(4,128)(2,1)S(1)}, bf16[27,4,32]{2,1,0:T(4,128)(2,1)S(1)}, f32[1,32]{1,0:T(1,128)S(1)}, bf16[3,3,32,32]{3,2,1,0:T(8,128)(2,...) custom-call(bf16[2,4,4,512]{3,2,1,0:T(4,128)(2,1)} %refs_0_.1, ...), custom_call_target="tpu_custom_call" | custom-call | bytes 2960000 | tf_op jit(solution)/shard_map/fetch/pallas_call | solution.py:355
  4.1 0.0 collective-permute-done.near.refs_2_
  4.1 2.1 %collective-permute-start.1 = (bf16[16,512]{1,0:T(8,128)(2,1)S(1)}, bf16[16,512]{1,0:T(8,128)(2,1)S(1)}, u32[]{:S(2)}, u32[]{:S(2)}) collective-permute-start(bf16[16,512]{1,0:T(8,128)(2,1)S(1)} %get-tuple-element.31), channel_id=1, source_target_pairs={{0,1},{1,0},{2,3},{3,2},{4,5},{5,4},{6,7},{7,6},{8,25},{9,24},{10,... | collective-permute-start | bytes 49160 | tf_op jit(solution)/shard_map/ppermute | solution.py:390
  6.2 3.5 %collective-permute-start.2 = (bf16[16,512]{1,0:T(8,128)(2,1)S(1)}, bf16[16,512]{1,0:T(8,128)(2,1)S(1)}, u32[]{:S(2)}, u32[]{:S(2)}) collective-permute-start(bf16[16,512]{1,0:T(8,128)(2,1)S(1)} %get-tuple-element.32), channel_id=1, source_target_pairs={{0,7},{1,2},{2,1},{3,4},{4,3},{5,6},{6,5},{7,0},{8,31},{9,26},{10,... | collective-permute-start | bytes 49160 | tf_op jit(solution)/shard_map/ppermute | solution.py:391
  9.8 0.0 collective-permute-done.4.refs_3_
  9.8 0.0 collective-permute-done.3.refs_1_
  9.8 1.2 %prepare.1 = (bf16[4,9,32,512]{3,2,1,0:T(8,128)(2,1)S(1)}, bf16[128,432]{1,0:T(8,128)(2,1)S(1)}, bf16[128,432]{1,0:T(8,128)(2,1)S(1)}, bf16[128,432]{1,0:T(8,128...) custom-call(bf16[2,4,4,512]{3,2,1,0:T(4,128)(2,1)S(1)} %get-tuple-el, ...), custom_call_target="tpu_custom_call" | custom-call | bytes 3330000 | tf_op jit(solution)/shard_map/prepare/pallas_call | solution.py:426
  11.0 1.4 %inner.1.refs_2_ = bf16[2,2,32,512]{3,2,1,0:T(8,128)(2,1)S(1)} custom-call(bf16[4,9,32,512]{3,2,1,0:T(8,128)(2,1)S(1)} %get-tuple-element.39.patches.refs_1_, bf16[128,432]{1,0:T(8,128)(2,1)S(1)} %get-tuple-element.40.conv, f32[128,128]{1,0:T(8,128)S(1)} %get-tuple-element.41.rest_0_.refs_5_, bf16[256,256]{1,0:T(8,128)(2,1)S(1)} %get-tuple-element.42.rest_1_.refs_6_, ...), custom_call_target="tpu_custom_call" | custom-call | bytes 6660000 | tf_op jit(solution)/shard_map/inner/pallas_call | solution.py:436
  12.4 0.0 collective-permute-done.1.near
  12.4 0.2 %collective-permute-done.2.far = bf16[16,512]{1,0:T(8,128)(2,1)S(1)} collective-permute-done((bf16[16,512]{1,0:T(8,128)(2,1)S(1)}, bf16[16,512]{1,0:T(8,128)(2,1)S(1)}, u32[]{:S(2)}, u32[]{:S(2)}) %collective-permute-start.2) | collective-permute-done | bytes 16416 | tf_op jit(solution)/shard_map/ppermute | solution.py:391
  12.7 0.1 collective-permute-start.5
  12.8 1.1 %collective-permute-done.5.refs_0_ = bf16[32,512]{1,0:T(8,128)(2,1)S(1)} collective-permute-done((bf16[32,512]{1,0:T(8,128)(2,1)S(1)}, bf16[32,512]{1,0:T(8,128)(2,1)S(1)}, u32[]{:S(2)}, u32[]{:S(2)}) %collective-permute-start.5) | collective-permute-done | bytes 32800 | tf_op jit(solution)/shard_map/ppermute | solution.py:457
  13.9 2.2 %outer.1 = bf16[2,4,32,512]{3,2,1,0:T(8,128)(2,1)} custom-call(bf16[16,512]{1,0:T(8,128)(2,1)S(1)} %collective-permute-done.1.near, bf16[16,512]{1,0:T(8,128)(2,1)S(1)} %collective-permute-done.2.far, bf16[32,512]{1,0:T(8,128)(2,1)S(1)} %collective-permute-done.5.refs_0_, bf16[4,9,32,512]{3,2,1,0:T(8,128)(2,1)S(1)} %get-tuple-element.39.patches.refs_1_, ...), custom_call_target="tpu_custom_call" | custom-call | bytes 9250000 | tf_op jit(solution)/shard_map/outer/pallas_call | solution.py:459
  (2 shorter events, 0.0 us)
Async XLA Ops:
  0.0 4.1 %collective-permute-start = (bf16[2,4,4,512]{3,2,1,0:T(4,128)(2,1)}, bf16[2,4,4,512]{3,2,1,0:T(4,128)(2,1)S(1)}, u32[]{:S(2)}, u32[]{:S(2)}) collective-permute-start(bf16[2,4,4,512]{3,2,1,0:T(4,128)(2,1)} %refs_0_.1), channel_id=1, source_target_pairs={{0,8},{8,0},{16,24},{24,16},{1,9},{9,1},{17,25},{25,17},{2,10},{10... | collective-permute-start | bytes 98312 | tf_op jit(solution)/shard_map/ppermute | solution.py:371
  0.5 9.3 %collective-permute-start.4 = (bf16[2,4,4,512]{3,2,1,0:T(4,128)(2,1)}, bf16[2,4,4,512]{3,2,1,0:T(4,128)(2,1)S(1)}, u32[]{:S(2)}, u32[]{:S(2)}) collective-permute-start(bf16[2,4,4,512]{3,2,1,0:T(4,128)(2,1)} %refs_0_.1), channel_id=1, source_target_pairs={{0,24},{8,16},{16,8},{24,0},{1,25},{9,17},{17,9},{25,1},{2,26},{10... | collective-permute-start | bytes 98312 | tf_op jit(solution)/shard_map/ppermute | solution.py:372
  3.1 6.7 %collective-permute-start.3 = (bf16[2,4,4,512]{3,2,1,0:T(4,128)(2,1)}, bf16[2,4,4,512]{3,2,1,0:T(4,128)(2,1)S(1)}, u32[]{:S(2)}, u32[]{:S(2)}) collective-permute-start(bf16[2,4,4,512]{3,2,1,0:T(4,128)(2,1)} %refs_0_.1), channel_id=1, source_target_pairs={{0,16},{8,24},{16,0},{24,8},{1,17},{9,25},{17,1},{25,9},{2,18},{10... | collective-permute-start | bytes 98312 | tf_op jit(solution)/shard_map/ppermute | solution.py:373
  4.1 8.3 %collective-permute-start.1 = (bf16[16,512]{1,0:T(8,128)(2,1)S(1)}, bf16[16,512]{1,0:T(8,128)(2,1)S(1)}, u32[]{:S(2)}, u32[]{:S(2)}) collective-permute-start(bf16[16,512]{1,0:T(8,128)(2,1)S(1)} %get-tuple-element.31), channel_id=1, source_target_pairs={{0,1},{1,0},{2,3},{3,2},{4,5},{5,4},{6,7},{7,6},{8,25},{9,24},{10,... | collective-permute-start | bytes 49160 | tf_op jit(solution)/shard_map/ppermute | solution.py:390
  6.2 6.4 %collective-permute-start.2 = (bf16[16,512]{1,0:T(8,128)(2,1)S(1)}, bf16[16,512]{1,0:T(8,128)(2,1)S(1)}, u32[]{:S(2)}, u32[]{:S(2)}) collective-permute-start(bf16[16,512]{1,0:T(8,128)(2,1)S(1)} %get-tuple-element.32), channel_id=1, source_target_pairs={{0,7},{1,2},{2,1},{3,4},{4,3},{5,6},{6,5},{7,0},{8,31},{9,26},{10,... | collective-permute-start | bytes 49160 | tf_op jit(solution)/shard_map/ppermute | solution.py:391
  12.7 1.2 %collective-permute-start.5 = (bf16[32,512]{1,0:T(8,128)(2,1)S(1)}, bf16[32,512]{1,0:T(8,128)(2,1)S(1)}, u32[]{:S(2)}, u32[]{:S(2)}) collective-permute-start(bf16[32,512]{1,0:T(8,128)(2,1)S(1)} %merge.1), channel_id=1, source_target_pairs={{0,8},{8,0},{16,24},{24,16},{1,9},{9,1},{17,25},{25,17},{2,10},{10... | collective-permute-start | bytes 98312 | tf_op jit(solution)/shard_map/ppermute | solution.py:457

commit v4 on v3

--- a/solution.py
+++ b/solution.py
@@ -82,19 +82,7 @@
         copy.wait()
 
 
-def prepare_kernel(paired, slot_of, count, *refs):
-    blocks, outs = refs[:count], refs[count + 6 :]
-    conv, conv_shift, taps, tap_shift, mix, mix_shift = refs[count : count + 6]
-    frames, row_count = blocks[0].shape[:2]
-    patches, outs = outs[0], outs[1:]
-    for row in range(row_count):
-        lines = [block[frame, row] for block in blocks for frame in range(frames)]
-        for place, piece in enumerate(shifted(jnp.concatenate(lines, axis=0))):
-            patches[row, place] = piece
-    conv_outs, conv_shift_out = outs[:3], outs[3]
-    tap_outs = outs[4 : 4 + LEVELS]
-    tap_shift_outs = outs[4 + LEVELS : 4 + 2 * LEVELS]
-    mix_out, mix_shift_out = outs[4 + 2 * LEVELS :]
+def conv_kernel(paired, conv, conv_shift, *outs):
     places, fields, channels = conv.shape
     depth = places * fields
     wide = depth * GROUP
@@ -112,10 +100,16 @@
     third = wide // 3
     turned = jnp.concatenate([full[:, 2 * third :], full[:, third : -third], full[:, :third]], axis=1)
     even = parity(paired) == 0
-    conv_outs[0][...] = full.astype(BF16)
-    conv_outs[1][...] = jnp.where(even, full, turned).astype(BF16)
-    conv_outs[2][...] = jnp.where(even, turned, full).astype(BF16)
-    conv_shift_out[...] = lanes(0.5 * column(conv_shift[...], GROUP))
+    outs[0][...] = full.astype(BF16)
+    outs[1][...] = jnp.where(even, full, turned).astype(BF16)
+    outs[2][...] = jnp.where(even, turned, full).astype(BF16)
+    outs[3][...] = lanes(0.5 * column(conv_shift[...], GROUP))
+
+
+def levels_kernel(slot_of, frames, taps, tap_shift, mix, mix_shift, *outs):
+    tap_outs, tap_shift_outs = outs[:LEVELS], outs[LEVELS : 2 * LEVELS]
+    mix_out, mix_shift_out = outs[2 * LEVELS :]
+    channels = mix.shape[-1]
     slots = slot_of(lax.axis_index("tm"))
     for level in range(LEVELS):
         rows, columns = tap_outs[level].shape
@@ -227,13 +221,23 @@
                 [jnp.where(first, mine, beside), jnp.where(first, beside, mine)], axis=0
             )
         )
+    outs[2][0] = own[...]
+    outs[2][1] = near[...]
     outs[0][...] = jnp.where(even, rows[0], rows[1])
     outs[1][...] = jnp.where(even, rows[1], rows[0])
 
 
-def inner_kernel(patches, conv, *rest):
-    weights, out = rest[:-1], rest[-1]
-    row_count, _, _, plane = patches.shape
+def inner_kernel(paired, count, *refs):
+    blocks, conv, weights, (patches, out) = refs[:count], refs[count], refs[count + 1 : -2], refs[-2:]
+    if paired:
+        own, near, beyond = blocks
+        blocks = own, beyond.at[0], near, beyond.at[1]
+    frames, row_count = blocks[0].shape[:2]
+    plane = patches.shape[-1]
+    for row in range(row_count):
+        lines = [block[frame, row] for block in blocks for frame in range(frames)]
+        for place, piece in enumerate(shifted(jnp.concatenate(lines, axis=0))):
+            patches[row, place] = piece
     depth = conv.shape[1] // 27
     width = math.gcd(plane, CELLS)
     places = [
@@ -352,7 +356,7 @@
         mix_bias,
     ]
     sources = [pltpu.with_memory_space_constraint(source, pltpu.HBM) for source in sources]
-    own, *sources = pl.pallas_call(
+    sources = pl.pallas_call(
         fetch_kernel,
         out_shape=[jax.ShapeDtypeStruct(source.shape, source.dtype) for source in sources],
         in_specs=[pl.BlockSpec(memory_space=pl.ANY)] * len(sources),
@@ -369,17 +373,16 @@
         across = [(index, index ^ 2) for index in range(times)]
         beside = [(index, index ^ 1) for index in range(times)]
         near = lax.ppermute(snapshots, "tm", beside)
-        both = lax.ppermute(snapshots, "tm", [(index, index ^ 3) for index in range(times)])
-        far = lax.ppermute(snapshots, "tm", across)
-        to_far, to_near = pl.pallas_call(
+        to_far, to_near, pair = pl.pallas_call(
             pack_kernel,
-            out_shape=[jax.ShapeDtypeStruct((total // 2, plane), BF16)] * 2,
+            out_shape=[jax.ShapeDtypeStruct((total // 2, plane), BF16)] * 2
+            + [jax.ShapeDtypeStruct((2,) + snapshots.shape, BF16)],
             in_specs=[VMEM] * 2,
-            out_specs=[VMEM] * 2,
+            out_specs=[VMEM] * 3,
             compiler_params=PARAMS,
             cost_estimate=cost(0.05),
             name="pack",
-        )(own, near)
+        )(sources[0], near)
         far_pairs, near_pairs = [], []
         for time in range(times):
             for space in range(spaces):
@@ -387,17 +390,26 @@
                 step = 2 * (space % 2) - 1
                 far_pairs.append((time * spaces + space, target + (space + step) % spaces))
                 near_pairs.append((time * spaces + space, target + space - step))
+        beyond = lax.ppermute(pair, "tm", across)
         near_halo = lax.ppermute(to_near, ("tm", "space"), near_pairs)
         far_halo = lax.ppermute(to_far, ("tm", "space"), far_pairs)
     else:
         slot_of = lambda index: [(index + offset) % times for offset in offsets]
 
-    shapes = [
-        jax.ShapeDtypeStruct((row_count, 9, total, plane), BF16),
-        *[jax.ShapeDtypeStruct((tall, 27 * GROUP * fields), BF16)] * 3,
-        jax.ShapeDtypeStruct((tall, 128), F32),
-    ]
+    own, conv, conv_shift, *levels = sources
+    *convs, conv_shift = pl.pallas_call(
+        functools.partial(conv_kernel, paired),
+        out_shape=[jax.ShapeDtypeStruct((tall, 27 * GROUP * fields), BF16)] * 3
+        + [jax.ShapeDtypeStruct((tall, 128), F32)],
+        in_specs=[VMEM] * 2,
+        out_specs=[VMEM] * 4,
+        compiler_params=PARAMS,
+        cost_estimate=cost(0.3),
+        name="conv",
+    )(conv, conv_shift)
+
     wide_of = [count * frames * channels for count in counts]
+    shapes = []
     for level in range(LEVELS):
         shape = wide_of[level + 1], wide_of[level] * (level + 1)
         shapes.append(jax.ShapeDtypeStruct(shape, BF16))
@@ -407,9 +419,19 @@
         jax.ShapeDtypeStruct((wide_of[LEVELS], wide_of[LEVELS] * LEVELS), BF16),
         jax.ShapeDtypeStruct((wide_of[LEVELS], 128), F32),
     ]
+    weights = pl.pallas_call(
+        functools.partial(levels_kernel, slot_of, frames),
+        out_shape=shapes,
+        in_specs=[VMEM] * 4,
+        out_specs=[VMEM] * len(shapes),
+        compiler_params=PARAMS,
+        cost_estimate=cost(0.7),
+        name="levels",
+    )(*levels)
+    weights = [conv_shift, *weights]
 
     if paired:
-        blocks = [own, far, near, both]
+        blocks = [own, near, beyond]
     else:
         blocks = [own] + [
             lax.ppermute(snapshots, "tm", ring(times, -offset)) for offset in offsets[1:]
@@ -423,25 +445,18 @@
             lax.ppermute(high, "space", ring(spaces, 1)),
         ]
 
-    patches, conv, conv_far, conv_near, *weights = pl.pallas_call(
-        functools.partial(prepare_kernel, paired, slot_of, len(blocks)),
-        out_shape=shapes,
-        in_specs=[VMEM] * (len(blocks) + len(sources)),
-        out_specs=[VMEM] * len(shapes),
-        compiler_params=PARAMS,
-        cost_estimate=cost(0.9),
-        name="prepare",
-    )(*blocks, *sources)
-
-    inner = pl.pallas_call(
-        inner_kernel,
-        out_shape=jax.ShapeDtypeStruct((frames, row_count - 2, channels, plane), BF16),
-        in_specs=[VMEM] * (2 + len(weights)),
-        out_specs=VMEM,
+    patches, inner = pl.pallas_call(
+        functools.partial(inner_kernel, paired, len(blocks)),
+        out_shape=[
+            jax.ShapeDtypeStruct((row_count, 9, total, plane), BF16),
+            jax.ShapeDtypeStruct((frames, row_count - 2, channels, plane), BF16),
+        ],
+        in_specs=[VMEM] * (len(blocks) + 1 + len(weights)),
+        out_specs=[VMEM] * 2,
         compiler_params=PARAMS,
         cost_estimate=cost(1.8),
         name="inner",
-    )(patches, conv, *weights)
+    )(*blocks, convs[0], *weights)
 
     if paired:
         near_halo, far_halo, inner = lax.optimization_barrier((near_halo, far_halo, inner))
@@ -469,7 +484,7 @@
         compiler_params=PARAMS,
         cost_estimate=cost(2.5),
         name="outer",
-    )(*halos, patches, inner, conv_far, conv_near, *weights)
+    )(*halos, patches, inner, *convs[1:], *weights)
 
 
 def solution(mesh):

time: 16.2 us -> 16 us (0.988)
  starting transfers between devices: 8.84 us -> 8.42 us
  waiting for transfers between devices: 1.33 us -> 1.63 us
    ppermute x1, starting transfers between devices: 2.12 us -> 1.52 us  [shards(): near_halo = lax.ppermute(to_near, ('tm', 'space'), near_pairs)]
    ppermute x2 -> x1, starting transfers between devices: 2.6 us -> 2.9 us  [shards(): beyond = lax.ppermute(pair, 'tm', across)]
    pallas_call x2 -> x3, Pallas kernels: 2.63 us -> 2.5 us  [the longest x1 1.55 us: shards(): pl.pallas_call(functools.partial(inner_kernel, paired, len(blocks)), out_...]
  transfers between devices with their start and end apart: 6 -> 5, of which waited for: 2 -> 3; matrix products, arithmetic and copies ran while one was open for 0% -> 0% of each run, Pallas kernels for 23% -> 22%
where the time goes in v4:
time: 16 us; the launch traced here: 15.8 us
  starting transfers between devices  8.42 us (53%)
  Pallas kernels  5.71 us (36%)
  waiting for transfers between devices  1.63 us (10%)
    ppermute x1, starting transfers between devices, shards(): far_halo = lax.ppermute(to_far, ('tm', 'space'), far_pairs)  3.54 us
    ppermute x1, starting transfers between devices, shards(): beyond = lax.ppermute(pair, 'tm', across)  2.9 us
    pallas_call x1, Pallas kernels, shards(): pl.pallas_call(functools.partial(outer_kernel, paired), out_shape=jax.Sha...  2.18 us
    pallas_call x1, Pallas kernels, shards(): pl.pallas_call(functools.partial(inner_kernel, paired, len(blocks)), out_...  1.55 us
    ppermute x1, starting transfers between devices, shards(): near_halo = lax.ppermute(to_near, ('tm', 'space'), near_pairs)  1.52 us
    ppermute x1, waiting for transfers between devices, shards(): halos = [near_halo, far_halo, lax.ppermute(merged, 'tm', beside)]  1.2 us
    pallas_call x1, Pallas kernels, shards(): pl.pallas_call(fetch_kernel, out_shape=[jax.ShapeDtypeStruct(source.shape...  1 us
    pallas_call x1, Pallas kernels, shards(): pl.pallas_call(functools.partial(levels_kernel, slot_of, frames), out_sha...  0.66 us
  transfers between devices with their start and end apart: 5, of which 3 were waited for; matrix products, arithmetic and copies ran while one was open for 0% of the time, Pallas kernels for 22%

profile of v4, /device:TPU:0, one launch (start us, length us, event | category | flops | bytes accessed | tf_op | source)
XLA Modules:
  0.0 15.8 jit_solution(10006641887894846587)
XLA Ops:
  0.0 0.5 %collective-permute-start = (bf16[2,4,4,512]{3,2,1,0:T(4,128)(2,1)}, bf16[2,4,4,512]{3,2,1,0:T(4,128)(2,1)S(1)}, u32[]{:S(2)}, u32[]{:S(2)}) collective-permute-start(bf16[2,4,4,512]{3,2,1,0:T(4,128)(2,1)} %refs_0_.1), channel_id=1, source_target_pairs={{0,8},{8,0},{16,24},{24,16},{1,9},{9,1},{17,25},{25,17},{2,10},{10... | collective-permute-start | bytes 98312 | tf_op jit(solution)/shard_map/ppermute | solution.py:375
  0.5 1.0 %fetch.1 = (bf16[2,4,4,512]{3,2,1,0:T(4,128)(2,1)S(1)}, bf16[27,4,32]{2,1,0:T(4,128)(2,1)S(1)}, f32[1,32]{1,0:T(1,128)S(1)}, bf16[3,3,32,32]{3,2,1,0:T(8,128)(2,...) custom-call(bf16[2,4,4,512]{3,2,1,0:T(4,128)(2,1)} %refs_0_.1, ...), custom_call_target="tpu_custom_call" | custom-call | bytes 2960000 | tf_op jit(solution)/shard_map/fetch/pallas_call | solution.py:359
  1.5 0.1 collective-permute-done.near.refs_1_
  1.6 2.9 %collective-permute-start.3 = (bf16[2,2,4,4,512]{4,3,2,1,0:T(4,128)(2,1)S(1)}, bf16[2,2,4,4,512]{4,3,2,1,0:T(4,128)(2,1)S(1)}, u32[]{:S(2)}, u32[]{:S(2)}) collective-permute-start(bf16[2,2,4,4,512]{4,3,2,1,0:T(4,128)(2,1)S(1)} %get-tuple-element.35), channel_id=1, source_target_pairs={{0,16},{8,24},{16,0},{24,8},{1,17},{9,25},{17,1},{25,9},{2,18},{10... | collective-permute-start | bytes 196616 | tf_op jit(solution)/shard_map/ppermute | solution.py:393
  4.5 1.5 %collective-permute-start.1 = (bf16[16,512]{1,0:T(8,128)(2,1)S(1)}, bf16[16,512]{1,0:T(8,128)(2,1)S(1)}, u32[]{:S(2)}, u32[]{:S(2)}) collective-permute-start(bf16[16,512]{1,0:T(8,128)(2,1)S(1)} %get-tuple-element.33), channel_id=1, source_target_pairs={{0,1},{1,0},{2,3},{3,2},{4,5},{5,4},{6,7},{7,6},{8,25},{9,24},{10,... | collective-permute-start | bytes 49160 | tf_op jit(solution)/shard_map/ppermute | solution.py:394
  6.0 3.5 %collective-permute-start.2 = (bf16[16,512]{1,0:T(8,128)(2,1)S(1)}, bf16[16,512]{1,0:T(8,128)(2,1)S(1)}, u32[]{:S(2)}, u32[]{:S(2)}) collective-permute-start(bf16[16,512]{1,0:T(8,128)(2,1)S(1)} %get-tuple-element.34), channel_id=1, source_target_pairs={{0,7},{1,2},{2,1},{3,4},{4,3},{5,6},{6,5},{7,0},{8,31},{9,26},{10,... | collective-permute-start | bytes 49160 | tf_op jit(solution)/shard_map/ppermute | solution.py:395
  9.5 0.3 %conv.1 = (bf16[128,432]{1,0:T(8,128)(2,1)S(1)}, bf16[128,432]{1,0:T(8,128)(2,1)S(1)}, bf16[128,432]{1,0:T(8,128)(2,1)S(1)}, f32[128,128]{1,0:T(8,128)S(1)}) custom-call(bf16[27,4,32]{2,1,0:T(4,128)(2,1)S(1)} %get-tuple-element.36.conv, f32[1,32]{1,0:T(1,128)S(1)} %get-tuple-element.37.conv_shift), custom_call_target="tpu_custom_call" | custom-call | bytes 1110000 | tf_op jit(solution)/shard_map/conv/pallas_call | solution.py:400
  9.8 0.7 %levels.1 = (bf16[256,256]{1,0:T(8,128)(2,1)S(1)}, bf16[128,512]{1,0:T(8,128)(2,1)S(1)}, bf16[64,384]{1,0:T(8,128)(2,1)S(1)}, f32[256,128]{1,0:T(8,128)S(1)}, f3...) custom-call(bf16[3,3,32,32]{3,2,1,0:T(8,128)(2,1)S(1)} %get-tuple-element.40., ...), custom_call_target="tpu_custom_call" | custom-call | bytes 2590000 | tf_op jit(solution)/shard_map/levels/pallas_call | solution.py:422
  10.5 0.0 collective-permute-done.3.refs_2_
  10.5 1.6 %inner.1 = (bf16[4,9,32,512]{3,2,1,0:T(8,128)(2,1)S(1)}, bf16[2,2,32,512]{3,2,1,0:T(8,128)(2,1)S(1)}) custom-call(bf16[2,4,4,512]{3,2,1,0:T(4,128)(2,1)S(1)} %get-tuple-element.32.own.refs_0_, bf16[2,4,4,512]{3,2,1,0:T(4,128)(2,1)S(1)} %collective-permute-done.near.refs_1_, bf16[2,2,4,4,512]{4,3,2,1,0:T(4,128)(2,1)S(1)} %collective-permute-done.3.refs_2_, ...), custom_call_target="tpu_custom_call" | custom-call | bytes 6660000 | tf_op jit(solution)/shard_map/inner/pallas_call | solution.py:448
  12.0 0.0 collective-permute-done.1.near
  12.0 0.4 %collective-permute-done.2.far = bf16[16,512]{1,0:T(8,128)(2,1)S(1)} collective-permute-done((bf16[16,512]{1,0:T(8,128)(2,1)S(1)}, bf16[16,512]{1,0:T(8,128)(2,1)S(1)}, u32[]{:S(2)}, u32[]{:S(2)}) %collective-permute-start.2) | collective-permute-done | bytes 16416 | tf_op jit(solution)/shard_map/ppermute | solution.py:395
  12.4 0.0 collective-permute-start.4
  12.4 1.2 %collective-permute-done.4.refs_0_ = bf16[32,512]{1,0:T(8,128)(2,1)S(1)} collective-permute-done((bf16[32,512]{1,0:T(8,128)(2,1)S(1)}, bf16[32,512]{1,0:T(8,128)(2,1)S(1)}, u32[]{:S(2)}, u32[]{:S(2)}) %collective-permute-start.4) | collective-permute-done | bytes 32800 | tf_op jit(solution)/shard_map/ppermute | solution.py:472
  13.6 2.2 %outer.1 = bf16[2,4,32,512]{3,2,1,0:T(8,128)(2,1)} custom-call(bf16[16,512]{1,0:T(8,128)(2,1)S(1)} %collective-permute-done.1.near, bf16[16,512]{1,0:T(8,128)(2,1)S(1)} %collective-permute-done.2.far, bf16[32,512]{1,0:T(8,128)(2,1)S(1)} %collective-permute-done.4.refs_0_, bf16[4,9,32,512]{3,2,1,0:T(8,128)(2,1)S(1)} %get-tuple-element.55.refs_1_, ...), custom_call_target="tpu_custom_call" | custom-call | bytes 9250000 | tf_op jit(solution)/shard_map/outer/pallas_call | solution.py:474
  (2 shorter events, 0.0 us)
Async XLA Ops:
  0.0 1.5 %collective-permute-start = (bf16[2,4,4,512]{3,2,1,0:T(4,128)(2,1)}, bf16[2,4,4,512]{3,2,1,0:T(4,128)(2,1)S(1)}, u32[]{:S(2)}, u32[]{:S(2)}) collective-permute-start(bf16[2,4,4,512]{3,2,1,0:T(4,128)(2,1)} %refs_0_.1), channel_id=1, source_target_pairs={{0,8},{8,0},{16,24},{24,16},{1,9},{9,1},{17,25},{25,17},{2,10},{10... | collective-permute-start | bytes 98312 | tf_op jit(solution)/shard_map/ppermute | solution.py:375
  1.6 8.9 %collective-permute-start.3 = (bf16[2,2,4,4,512]{4,3,2,1,0:T(4,128)(2,1)S(1)}, bf16[2,2,4,4,512]{4,3,2,1,0:T(4,128)(2,1)S(1)}, u32[]{:S(2)}, u32[]{:S(2)}) collective-permute-start(bf16[2,2,4,4,512]{4,3,2,1,0:T(4,128)(2,1)S(1)} %get-tuple-element.35), channel_id=1, source_target_pairs={{0,16},{8,24},{16,0},{24,8},{1,17},{9,25},{17,1},{25,9},{2,18},{10... | collective-permute-start | bytes 196616 | tf_op jit(solution)/shard_map/ppermute | solution.py:393
  4.5 7.6 %collective-permute-start.1 = (bf16[16,512]{1,0:T(8,128)(2,1)S(1)}, bf16[16,512]{1,0:T(8,128)(2,1)S(1)}, u32[]{:S(2)}, u32[]{:S(2)}) collective-permute-start(bf16[16,512]{1,0:T(8,128)(2,1)S(1)} %get-tuple-element.33), channel_id=1, source_target_pairs={{0,1},{1,0},{2,3},{3,2},{4,5},{5,4},{6,7},{7,6},{8,25},{9,24},{10,... | collective-permute-start | bytes 49160 | tf_op jit(solution)/shard_map/ppermute | solution.py:394
  6.0 6.4 %collective-permute-start.2 = (bf16[16,512]{1,0:T(8,128)(2,1)S(1)}, bf16[16,512]{1,0:T(8,128)(2,1)S(1)}, u32[]{:S(2)}, u32[]{:S(2)}) collective-permute-start(bf16[16,512]{1,0:T(8,128)(2,1)S(1)} %get-tuple-element.34), channel_id=1, source_target_pairs={{0,7},{1,2},{2,1},{3,4},{4,3},{5,6},{6,5},{7,0},{8,31},{9,26},{10,... | collective-permute-start | bytes 49160 | tf_op jit(solution)/shard_map/ppermute | solution.py:395
  12.4 1.2 %collective-permute-start.4 = (bf16[32,512]{1,0:T(8,128)(2,1)S(1)}, bf16[32,512]{1,0:T(8,128)(2,1)S(1)}, u32[]{:S(2)}, u32[]{:S(2)}) collective-permute-start(bf16[32,512]{1,0:T(8,128)(2,1)S(1)} %merge.1), channel_id=1, source_target_pairs={{0,8},{8,0},{16,24},{24,16},{1,9},{9,1},{17,25},{25,17},{2,10},{10... | collective-permute-start | bytes 98312 | tf_op jit(solution)/shard_map/ppermute | solution.py:472

commit v5 on v4

--- a/solution.py
+++ b/solution.py
@@ -328,8 +328,9 @@
 
 
 def cost(microseconds):
-    size = int(microseconds * 3.7e6)
-    return pl.CostEstimate(flops=0, bytes_accessed=size, transcendentals=0)
+    size = int(microseconds * 3.7e6 * 0.5)
+    flops = int(microseconds * 1.15e9 * 0.5)
+    return pl.CostEstimate(flops=flops, bytes_accessed=size, transcendentals=0)
 
 
 def ring(count, step):
@@ -397,6 +398,10 @@
         slot_of = lambda index: [(index + offset) % times for offset in offsets]
 
     own, conv, conv_shift, *levels = sources
+    if paired:
+        near_halo, conv, conv_shift, *levels = lax.optimization_barrier(
+            (near_halo, conv, conv_shift, *levels)
+        )
     *convs, conv_shift = pl.pallas_call(
         functools.partial(conv_kernel, paired),
         out_shape=[jax.ShapeDtypeStruct((tall, 27 * GROUP * fields), BF16)] * 3

time: 16 us -> 16 us (level)
    ppermute x1, starting transfers between devices: 2.9 us -> 1.49 us  [shards(): beyond = lax.ppermute(pair, 'tm', across)]
    ppermute x1, starting transfers between devices: 1.52 us -> 2.93 us  [shards(): near_halo = lax.ppermute(to_near, ('tm', 'space'), near_pairs)]
where the time goes in v5:
time: 16 us; the launch traced here: 15.8 us
  starting transfers between devices  8.42 us (53%)
  Pallas kernels  5.75 us (36%)
  waiting for transfers between devices  1.62 us (10%)
    ppermute x1, starting transfers between devices, shards(): far_halo = lax.ppermute(to_far, ('tm', 'space'), far_pairs)  3.54 us
    ppermute x1, starting transfers between devices, shards(): near_halo = lax.ppermute(to_near, ('tm', 'space'), near_pairs)  2.93 us
    pallas_call x1, Pallas kernels, shards(): pl.pallas_call(functools.partial(outer_kernel, paired), out_shape=jax.Sha...  2.2 us
    pallas_call x1, Pallas kernels, shards(): pl.pallas_call(functools.partial(inner_kernel, paired, len(blocks)), out_...  1.57 us
    ppermute x1, starting transfers between devices, shards(): beyond = lax.ppermute(pair, 'tm', across)  1.49 us
    ppermute x1, waiting for transfers between devices, shards(): halos = [near_halo, far_halo, lax.ppermute(merged, 'tm', beside)]  1.2 us
    pallas_call x1, Pallas kernels, shards(): pl.pallas_call(fetch_kernel, out_shape=[jax.ShapeDtypeStruct(source.shape...  1 us
    pallas_call x1, Pallas kernels, shards(): pl.pallas_call(functools.partial(levels_kernel, slot_of, frames), out_sha...  0.66 us
  transfers between devices with their start and end apart: 5, of which 3 were waited for; matrix products, arithmetic and copies ran while one was open for 0% of the time, Pallas kernels for 22%

profile of v5, /device:TPU:0, one launch (start us, length us, event | category | flops | bytes accessed | tf_op | source)
XLA Modules:
  0.0 15.8 jit_solution(17276212315047729078)
XLA Ops:
  0.0 0.5 %collective-permute-start = (bf16[2,4,4,512]{3,2,1,0:T(4,128)(2,1)}, bf16[2,4,4,512]{3,2,1,0:T(4,128)(2,1)S(1)}, u32[]{:S(2)}, u32[]{:S(2)}) collective-permute-start(bf16[2,4,4,512]{3,2,1,0:T(4,128)(2,1)} %refs_0_.1), channel_id=1, source_target_pairs={{0,8},{8,0},{16,24},{24,16},{1,9},{9,1},{17,25},{25,17},{2,10},{10... | collective-permute-start | bytes 98312 | tf_op jit(solution)/shard_map/ppermute | solution.py:376
  0.5 1.0 %fetch.1 = (bf16[2,4,4,512]{3,2,1,0:T(4,128)(2,1)S(1)}, bf16[27,4,32]{2,1,0:T(4,128)(2,1)S(1)}, f32[1,32]{1,0:T(1,128)S(1)}, bf16[3,3,32,32]{3,2,1,0:T(8,128)(2,...) custom-call(bf16[2,4,4,512]{3,2,1,0:T(4,128)(2,1)} %refs_0_.1, ...), custom_call_target="tpu_custom_call" | custom-call | flops 460000000 | bytes 1480000 | tf_op jit(solution)/shard_map/fetch/pallas_call | solution.py:360
  1.5 0.1 collective-permute-done.near.refs_1_
  1.6 2.9 %collective-permute-start.1 = (bf16[16,512]{1,0:T(8,128)(2,1)S(1)}, bf16[16,512]{1,0:T(8,128)(2,1)S(1)}, u32[]{:S(2)}, u32[]{:S(2)}) collective-permute-start(bf16[16,512]{1,0:T(8,128)(2,1)S(1)} %get-tuple-element.40), channel_id=1, source_target_pairs={{0,1},{1,0},{2,3},{3,2},{4,5},{5,4},{6,7},{7,6},{8,25},{9,24},{10,... | collective-permute-start | bytes 49160 | tf_op jit(solution)/shard_map/ppermute | solution.py:395
  4.5 1.5 %collective-permute-start.3 = (bf16[2,2,4,4,512]{4,3,2,1,0:T(4,128)(2,1)S(1)}, bf16[2,2,4,4,512]{4,3,2,1,0:T(4,128)(2,1)S(1)}, u32[]{:S(2)}, u32[]{:S(2)}) collective-permute-start(bf16[2,2,4,4,512]{4,3,2,1,0:T(4,128)(2,1)S(1)} %get-tuple-element.49), channel_id=1, source_target_pairs={{0,16},{8,24},{16,0},{24,8},{1,17},{9,25},{17,1},{25,9},{2,18},{10... | collective-permute-start | bytes 196616 | tf_op jit(solution)/shard_map/ppermute | solution.py:394
  6.0 3.5 %collective-permute-start.2 = (bf16[16,512]{1,0:T(8,128)(2,1)S(1)}, bf16[16,512]{1,0:T(8,128)(2,1)S(1)}, u32[]{:S(2)}, u32[]{:S(2)}) collective-permute-start(bf16[16,512]{1,0:T(8,128)(2,1)S(1)} %get-tuple-element.48), channel_id=1, source_target_pairs={{0,7},{1,2},{2,1},{3,4},{4,3},{5,6},{6,5},{7,0},{8,31},{9,26},{10,... | collective-permute-start | bytes 49160 | tf_op jit(solution)/shard_map/ppermute | solution.py:396
  9.5 0.0 collective-permute-done.1.near
  9.5 0.3 %conv.1 = (bf16[128,432]{1,0:T(8,128)(2,1)S(1)}, bf16[128,432]{1,0:T(8,128)(2,1)S(1)}, bf16[128,432]{1,0:T(8,128)(2,1)S(1)}, f32[128,128]{1,0:T(8,128)S(1)}) custom-call(bf16[27,4,32]{2,1,0:T(4,128)(2,1)S(1)} %get-tuple-element.50.conv, f32[1,32]{1,0:T(1,128)S(1)} %get-tuple-element.51.conv_shift), custom_call_target="tpu_custom_call" | custom-call | flops 172500000 | bytes 555000 | tf_op jit(solution)/shard_map/conv/pallas_call | solution.py:405
  9.8 0.7 %levels.1 = (bf16[256,256]{1,0:T(8,128)(2,1)S(1)}, bf16[128,512]{1,0:T(8,128)(2,1)S(1)}, bf16[64,384]{1,0:T(8,128)(2,1)S(1)}, f32[256,128]{1,0:T(8,128)S(1)}, f3...) custom-call(bf16[3,3,32,32]{3,2,1,0:T(8,128)(2,1)S(1)} %get-tuple-element.54., ...), custom_call_target="tpu_custom_call" | custom-call | flops 402500000 | bytes 1295000 | tf_op jit(solution)/shard_map/levels/pallas_call | solution.py:427
  10.5 0.0 collective-permute-done.3.refs_2_
  10.5 1.6 %inner.1 = (bf16[4,9,32,512]{3,2,1,0:T(8,128)(2,1)S(1)}, bf16[2,2,32,512]{3,2,1,0:T(8,128)(2,1)S(1)}) custom-call(bf16[2,4,4,512]{3,2,1,0:T(4,128)(2,1)S(1)} %get-tuple-element.39.own.refs_0_, bf16[2,4,4,512]{3,2,1,0:T(4,128)(2,1)S(1)} %collective-permute-done.near.refs_1_, bf16[2,2,4,4,512]{4,3,2,1,0:T(4,128)(2,1)S(1)} %collective-permute-done.3.refs_2_, ...), custom_call_target="tpu_custom_call" | custom-call | flops 1035000000 | bytes 3330000 | tf_op jit(solution)/shard_map/inner/pallas_call | solution.py:453
  12.1 0.4 %collective-permute-done.2.far = bf16[16,512]{1,0:T(8,128)(2,1)S(1)} collective-permute-done((bf16[16,512]{1,0:T(8,128)(2,1)S(1)}, bf16[16,512]{1,0:T(8,128)(2,1)S(1)}, u32[]{:S(2)}, u32[]{:S(2)}) %collective-permute-start.2) | collective-permute-done | bytes 16416 | tf_op jit(solution)/shard_map/ppermute | solution.py:396
  12.4 0.0 collective-permute-start.4
  12.4 1.2 %collective-permute-done.4.refs_0_ = bf16[32,512]{1,0:T(8,128)(2,1)S(1)} collective-permute-done((bf16[32,512]{1,0:T(8,128)(2,1)S(1)}, bf16[32,512]{1,0:T(8,128)(2,1)S(1)}, u32[]{:S(2)}, u32[]{:S(2)}) %collective-permute-start.4) | collective-permute-done | bytes 32800 | tf_op jit(solution)/shard_map/ppermute | solution.py:477
  13.6 2.2 %outer.1 = bf16[2,4,32,512]{3,2,1,0:T(8,128)(2,1)} custom-call(bf16[16,512]{1,0:T(8,128)(2,1)S(1)} %collective-permute-done.1.near, bf16[16,512]{1,0:T(8,128)(2,1)S(1)} %collective-permute-done.2.far, bf16[32,512]{1,0:T(8,128)(2,1)S(1)} %collective-permute-done.4.refs_0_, bf16[4,9,32,512]{3,2,1,0:T(8,128)(2,1)S(1)} %get-tuple-element.69.refs_1_, ...), custom_call_target="tpu_custom_call" | custom-call | flops 1437500032 | bytes 4625000 | tf_op jit(solution)/shard_map/outer/pallas_call | solution.py:479
  (2 shorter events, 0.0 us)
Async XLA Ops:
  0.0 1.5 %collective-permute-start = (bf16[2,4,4,512]{3,2,1,0:T(4,128)(2,1)}, bf16[2,4,4,512]{3,2,1,0:T(4,128)(2,1)S(1)}, u32[]{:S(2)}, u32[]{:S(2)}) collective-permute-start(bf16[2,4,4,512]{3,2,1,0:T(4,128)(2,1)} %refs_0_.1), channel_id=1, source_target_pairs={{0,8},{8,0},{16,24},{24,16},{1,9},{9,1},{17,25},{25,17},{2,10},{10... | collective-permute-start | bytes 98312 | tf_op jit(solution)/shard_map/ppermute | solution.py:376
  1.6 8.0 %collective-permute-start.1 = (bf16[16,512]{1,0:T(8,128)(2,1)S(1)}, bf16[16,512]{1,0:T(8,128)(2,1)S(1)}, u32[]{:S(2)}, u32[]{:S(2)}) collective-permute-start(bf16[16,512]{1,0:T(8,128)(2,1)S(1)} %get-tuple-element.40), channel_id=1, source_target_pairs={{0,1},{1,0},{2,3},{3,2},{4,5},{5,4},{6,7},{7,6},{8,25},{9,24},{10,... | collective-permute-start | bytes 49160 | tf_op jit(solution)/shard_map/ppermute | solution.py:395
  4.5 6.0 %collective-permute-start.3 = (bf16[2,2,4,4,512]{4,3,2,1,0:T(4,128)(2,1)S(1)}, bf16[2,2,4,4,512]{4,3,2,1,0:T(4,128)(2,1)S(1)}, u32[]{:S(2)}, u32[]{:S(2)}) collective-permute-start(bf16[2,2,4,4,512]{4,3,2,1,0:T(4,128)(2,1)S(1)} %get-tuple-element.49), channel_id=1, source_target_pairs={{0,16},{8,24},{16,0},{24,8},{1,17},{9,25},{17,1},{25,9},{2,18},{10... | collective-permute-start | bytes 196616 | tf_op jit(solution)/shard_map/ppermute | solution.py:394
  6.0 6.4 %collective-permute-start.2 = (bf16[16,512]{1,0:T(8,128)(2,1)S(1)}, bf16[16,512]{1,0:T(8,128)(2,1)S(1)}, u32[]{:S(2)}, u32[]{:S(2)}) collective-permute-start(bf16[16,512]{1,0:T(8,128)(2,1)S(1)} %get-tuple-element.48), channel_id=1, source_target_pairs={{0,7},{1,2},{2,1},{3,4},{4,3},{5,6},{6,5},{7,0},{8,31},{9,26},{10,... | collective-permute-start | bytes 49160 | tf_op jit(solution)/shard_map/ppermute | solution.py:396
  12.4 1.2 %collective-permute-start.4 = (bf16[32,512]{1,0:T(8,128)(2,1)S(1)}, bf16[32,512]{1,0:T(8,128)(2,1)S(1)}, u32[]{:S(2)}, u32[]{:S(2)}) collective-permute-start(bf16[32,512]{1,0:T(8,128)(2,1)S(1)} %merge.1), channel_id=1, source_target_pairs={{0,8},{8,0},{16,24},{24,16},{1,9},{9,1},{17,25},{25,17},{2,10},{10... | collective-permute-start | bytes 98312 | tf_op jit(solution)/shard_map/ppermute | solution.py:477

commit v6 on v5

--- a/solution.py
+++ b/solution.py
@@ -262,10 +262,6 @@
     encode(windows, weights, out.shape[0], store)
 
 
-def merge_kernel(near, far, out):
-    out[...] = jnp.concatenate([near[...], far[...]], axis=0)
-
-
 def halo_lines(got, other):
     first = lax.rem(lax.axis_index("tm"), 2) == 0
     half = got.shape[0] // 2
@@ -282,43 +278,50 @@
     return jnp.where(top, 0, row_count - 1), jnp.where(top, 1, row_count - 2)
 
 
-def outer_kernel(paired, near, far, *refs):
-    near, far = near[...], far[...]
-    if paired:
-        half = refs[0].shape[0] // 2
-        near = halo_lines(near, refs[0][:half])
-        far = halo_lines(far, refs[0][half:])
-        refs = refs[1:]
-    halos = far, near
-    patches, inner, *convs = refs[:4]
-    weights, (out, borders, done, sems) = refs[4:-4], refs[-4:]
+def encode_edge(paired, far, halos, patches, conv, weights, border, frames, store):
     row_count, _, _, plane = patches.shape
-    depth = convs[0].shape[1] // 27
+    depth = conv.shape[1] // 27
     width = math.gcd(plane, CELLS)
-    rows = [edge_row(paired, far, row_count) for far in (True, False)]
-    copies = [pltpu.make_async_copy(inner, out.at[:, 1 : row_count - 1], sems.at[0])]
-    copies[0].start()
-    windows = []
-    places = []
-    for side, (edge, inside) in enumerate(rows):
-        for place, piece in enumerate(shifted(halos[side])):
-            borders[side, place] = piece
-        sources = [borders.at[side], patches.at[edge], patches.at[inside]]
-        for start in range(0, plane, width):
-            cells = slice(start, start + width)
-            places.append((side, cells))
-            windows.append(
-                (convs[side], functools.partial(stack, sources, depth=depth, cells=cells))
-            )
-
-    def store(index, frame, final):
-        side, cells = places[index]
-        done[side, frame, :, cells] = final
-
-    encode(windows, weights, out.shape[0], store)
-    for side, (edge, _) in enumerate(rows):
-        copies.append(pltpu.make_async_copy(done.at[side], out.at[:, edge], sems.at[side + 1]))
-        copies[-1].start()
+    halo = halo_lines(halos[0][...], halos[1][...]) if paired else halos[0][...]
+    for place, piece in enumerate(shifted(halo)):
+        border[place] = piece
+    edge, inside = edge_row(paired, far, row_count)
+    sources = [border, patches.at[edge], patches.at[inside]]
+    places = [slice(start, start + width) for start in range(0, plane, width)]
+    windows = [
+        (conv, functools.partial(stack, sources, depth=depth, cells=cells)) for cells in places
+    ]
+    encode(windows, weights, frames, lambda index, *result: store(places[index], *result))
+
+
+def near_kernel(paired, count, *refs):
+    halos, patches, conv = refs[:count], refs[count], refs[count + 1]
+    weights, (out, border) = refs[count + 2 : -2], refs[-2:]
+
+    def store(cells, frame, final):
+        out[frame, :, cells] = final
+
+    encode_edge(paired, False, halos, patches, conv, weights, border, out.shape[0], store)
+
+
+def far_kernel(paired, count, *refs):
+    halos, patches, inner, near, conv = refs[:count], *refs[count : count + 4]
+    weights, (out, border, done, sems) = refs[count + 4 : -4], refs[-4:]
+    row_count = patches.shape[0]
+    far_row, near_row = [edge_row(paired, far, row_count)[0] for far in (True, False)]
+    copies = [
+        pltpu.make_async_copy(inner, out.at[:, 1 : row_count - 1], sems.at[0]),
+        pltpu.make_async_copy(near, out.at[:, near_row], sems.at[1]),
+    ]
+    for copy in copies:
+        copy.start()
+
+    def store(cells, frame, final):
+        done[frame, :, cells] = final
+
+    encode_edge(paired, True, halos, patches, conv, weights, border, out.shape[0], store)
+    copies.append(pltpu.make_async_copy(done, out.at[:, far_row], sems.at[2]))
+    copies[-1].start()
     for copy in copies:
         copy.wait()
 
@@ -328,8 +331,7 @@
 
 
 def cost(microseconds):
-    size = int(microseconds * 3.7e6 * 0.5)
-    flops = int(microseconds * 1.15e9 * 0.5)
+    size, flops = int(microseconds * 3.7e6), int(microseconds * 1.15e9)
     return pl.CostEstimate(flops=flops, bytes_accessed=size, transcendentals=0)
 
 
@@ -409,7 +411,7 @@
         in_specs=[VMEM] * 2,
         out_specs=[VMEM] * 4,
         compiler_params=PARAMS,
-        cost_estimate=cost(0.3),
+        cost_estimate=cost(0.05),
         name="conv",
     )(conv, conv_shift)
 
@@ -430,12 +432,14 @@
         in_specs=[VMEM] * 4,
         out_specs=[VMEM] * len(shapes),
         compiler_params=PARAMS,
-        cost_estimate=cost(0.7),
+        cost_estimate=cost(0.1),
         name="levels",
     )(*levels)
     weights = [conv_shift, *weights]
 
     if paired:
+        near_halos = [near_halo, lax.ppermute(near_halo, "tm", beside)]
+        near_halos[1], own = lax.optimization_barrier((near_halos[1], own))
         blocks = [own, near, beyond]
     else:
         blocks = [own] + [
@@ -445,10 +449,8 @@
             jnp.concatenate([block[:, row] for block in blocks], axis=0).reshape(total, plane)
             for row in (0, row_count - 1)
         ]
-        halos = [
-            lax.ppermute(low, "space", ring(spaces, -1)),
-            lax.ppermute(high, "space", ring(spaces, 1)),
-        ]
+        near_halos = [lax.ppermute(low, "space", ring(spaces, -1))]
+        far_halos = [lax.ppermute(high, "space", ring(spaces, 1))]
 
     patches, inner = pl.pallas_call(
         functools.partial(inner_kernel, paired, len(blocks)),
@@ -459,37 +461,39 @@
         in_specs=[VMEM] * (len(blocks) + 1 + len(weights)),
         out_specs=[VMEM] * 2,
         compiler_params=PARAMS,
-        cost_estimate=cost(1.8),
+        cost_estimate=cost(0.01),
         name="inner",
     )(*blocks, convs[0], *weights)
 
     if paired:
-        near_halo, far_halo, inner = lax.optimization_barrier((near_halo, far_halo, inner))
-        merged = pl.pallas_call(
-            merge_kernel,
-            out_shape=jax.ShapeDtypeStruct((total, plane), BF16),
-            in_specs=[VMEM] * 2,
-            out_specs=VMEM,
-            compiler_params=PARAMS,
-            cost_estimate=cost(0.05),
-            name="merge",
-        )(near_halo, far_halo)
-        halos = [near_halo, far_halo, lax.ppermute(merged, "tm", beside)]
+        far_halo, patches, inner = lax.optimization_barrier((far_halo, patches, inner))
+        far_halos = [far_halo, lax.ppermute(far_halo, "tm", beside)]
+
+    near_row = pl.pallas_call(
+        functools.partial(near_kernel, paired, len(near_halos)),
+        out_shape=jax.ShapeDtypeStruct((frames, channels, plane), BF16),
+        in_specs=[VMEM] * (len(near_halos) + 2 + len(weights)),
+        out_specs=VMEM,
+        scratch_shapes=[pltpu.VMEM((9, total, plane), BF16)],
+        compiler_params=PARAMS,
+        cost_estimate=cost(1.0),
+        name="near",
+    )(*near_halos, patches, convs[2], *weights)
 
     return pl.pallas_call(
-        functools.partial(outer_kernel, paired),
+        functools.partial(far_kernel, paired, len(far_halos)),
         out_shape=jax.ShapeDtypeStruct((frames, row_count, channels, plane), BF16),
-        in_specs=[VMEM] * (len(halos) + 4 + len(weights)),
+        in_specs=[VMEM] * (len(far_halos) + 4 + len(weights)),
         out_specs=pl.BlockSpec(memory_space=pl.ANY),
         scratch_shapes=[
-            pltpu.VMEM((2, 9, total, plane), BF16),
-            pltpu.VMEM((2, frames, channels, plane), BF16),
+            pltpu.VMEM((9, total, plane), BF16),
+            pltpu.VMEM((frames, channels, plane), BF16),
             pltpu.SemaphoreType.DMA((3,)),
         ],
         compiler_params=PARAMS,
-        cost_estimate=cost(2.5),
-        name="outer",
-    )(*halos, patches, inner, *convs[1:], *weights)
+        cost_estimate=cost(1.7),
+        name="far",
+    )(*far_halos, patches, inner, near_row, convs[1], *weights)
 
 
 def solution(mesh):

time: 16 us -> 15.8 us (0.988)
  waiting for transfers between devices: 1.62 us -> 0.22 us
  Pallas kernels: 5.75 us -> 6.5 us
  starting transfers between devices: 8.42 us -> 8.86 us
    ppermute x1, starting transfers between devices: 1.49 us -> 2.9 us  [shards(): beyond = lax.ppermute(pair, 'tm', across)]
    ppermute x1, starting transfers between devices: 2.93 us -> 1.52 us  [shards(): near_halo = lax.ppermute(to_near, ('tm', 'space'), near_pairs)]
    ppermute x1 -> x2, waiting for transfers between devices: 1.2 us -> 0.01 us  [the longest x1 0.01 us: shards(): near_halos = [near_halo, lax.ppermute(near_halo, 'tm', beside)]]
    pallas_call x2, Pallas kernels: 2.21 us -> 2.98 us  [the longest x1 1.83 us: shards(): pl.pallas_call(functools.partial(far_kernel, paired, len(far_halos)), out...]
    ppermute x1 -> x2, starting transfers between devices: 0.01 us -> 0.44 us  [the longest x1 0.22 us: shards(): near_halos = [near_halo, lax.ppermute(near_halo, 'tm', beside)]]
    ppermute x1, waiting for transfers between devices: 0.35 us -> 0.15 us  [shards(): far_halo = lax.ppermute(to_far, ('tm', 'space'), far_pairs)]
  transfers between devices with their start and end apart: 5 -> 6, of which waited for: 3 -> 2; matrix products, arithmetic and copies ran while one was open for 0% -> 0% of each run, Pallas kernels for 22% -> 30%
where the time goes in v6:
time: 15.8 us; the launch traced here: 15.6 us
  starting transfers between devices  8.86 us (56%)
  Pallas kernels  6.5 us (41%)
  waiting for transfers between devices  0.22 us (1%)
    ppermute x1, starting transfers between devices, shards(): far_halo = lax.ppermute(to_far, ('tm', 'space'), far_pairs)  3.54 us
    ppermute x1, starting transfers between devices, shards(): beyond = lax.ppermute(pair, 'tm', across)  2.9 us
    pallas_call x1, Pallas kernels, shards(): pl.pallas_call(functools.partial(far_kernel, paired, len(far_halos)), out...  1.83 us
    pallas_call x1, Pallas kernels, shards(): pl.pallas_call(functools.partial(inner_kernel, paired, len(blocks)), out_...  1.54 us
    ppermute x1, starting transfers between devices, shards(): near_halo = lax.ppermute(to_near, ('tm', 'space'), near_pairs)  1.52 us
    pallas_call x1, Pallas kernels, shards(): pl.pallas_call(functools.partial(near_kernel, paired, len(near_halos)), o...  1.15 us
    pallas_call x1, Pallas kernels, shards(): pl.pallas_call(fetch_kernel, out_shape=[jax.ShapeDtypeStruct(source.shape...  1 us
    pallas_call x1, Pallas kernels, shards(): pl.pallas_call(functools.partial(levels_kernel, slot_of, frames), out_sha...  0.66 us
  transfers between devices with their start and end apart: 6, of which 2 were waited for; matrix products, arithmetic and copies ran while one was open for 0% of the time, Pallas kernels for 30%

profile of v6, /device:TPU:0, one launch (start us, length us, event | category | flops | bytes accessed | tf_op | source)
XLA Modules:
  0.0 15.6 jit_solution(10198463494731172435)
XLA Ops:
  0.0 0.5 %collective-permute-start = (bf16[2,4,4,512]{3,2,1,0:T(4,128)(2,1)}, bf16[2,4,4,512]{3,2,1,0:T(4,128)(2,1)S(1)}, u32[]{:S(2)}, u32[]{:S(2)}) collective-permute-start(bf16[2,4,4,512]{3,2,1,0:T(4,128)(2,1)} %refs_0_.1), channel_id=1, source_target_pairs={{0,8},{8,0},{16,24},{24,16},{1,9},{9,1},{17,25},{25,17},{2,10},{10... | collective-permute-start | bytes 98312 | tf_op jit(solution)/shard_map/ppermute | solution.py:378
  0.5 1.0 %fetch.1 = (bf16[2,4,4,512]{3,2,1,0:T(4,128)(2,1)S(1)}, bf16[27,4,32]{2,1,0:T(4,128)(2,1)S(1)}, f32[1,32]{1,0:T(1,128)S(1)}, bf16[3,3,32,32]{3,2,1,0:T(8,128)(2,...) custom-call(bf16[2,4,4,512]{3,2,1,0:T(4,128)(2,1)} %refs_0_.1, ...), custom_call_target="tpu_custom_call" | custom-call | flops 920000000 | bytes 2960000 | tf_op jit(solution)/shard_map/fetch/pallas_call | solution.py:362
  1.5 0.1 collective-permute-done.near.refs_1_
  1.6 2.9 %collective-permute-start.4 = (bf16[2,2,4,4,512]{4,3,2,1,0:T(4,128)(2,1)S(1)}, bf16[2,2,4,4,512]{4,3,2,1,0:T(4,128)(2,1)S(1)}, u32[]{:S(2)}, u32[]{:S(2)}) collective-permute-start(bf16[2,2,4,4,512]{4,3,2,1,0:T(4,128)(2,1)S(1)} %get-tuple-element.52), channel_id=1, source_target_pairs={{0,16},{8,24},{16,0},{24,8},{1,17},{9,25},{17,1},{25,9},{2,18},{10... | collective-permute-start | bytes 196616 | tf_op jit(solution)/shard_map/ppermute | solution.py:396
  4.5 1.5 %collective-permute-start.2 = (bf16[16,512]{1,0:T(8,128)(2,1)S(1)}, bf16[16,512]{1,0:T(8,128)(2,1)S(1)}, u32[]{:S(2)}, u32[]{:S(2)}) collective-permute-start(bf16[16,512]{1,0:T(8,128)(2,1)S(1)} %get-tuple-element.43), channel_id=1, source_target_pairs={{0,1},{1,0},{2,3},{3,2},{4,5},{5,4},{6,7},{7,6},{8,25},{9,24},{10,... | collective-permute-start | bytes 49160 | tf_op jit(solution)/shard_map/ppermute | solution.py:397
  6.0 3.5 %collective-permute-start.1 = (bf16[16,512]{1,0:T(8,128)(2,1)S(1)}, bf16[16,512]{1,0:T(8,128)(2,1)S(1)}, u32[]{:S(2)}, u32[]{:S(2)}) collective-permute-start(bf16[16,512]{1,0:T(8,128)(2,1)S(1)} %get-tuple-element.42), channel_id=1, source_target_pairs={{0,7},{1,2},{2,1},{3,4},{4,3},{5,6},{6,5},{7,0},{8,31},{9,26},{10,... | collective-permute-start | bytes 49160 | tf_op jit(solution)/shard_map/ppermute | solution.py:398
  9.5 0.0 collective-permute-done.2.refs_0_
  9.5 0.2 %collective-permute-start.3 = (bf16[16,512]{1,0:T(8,128)(2,1)S(1)}, bf16[16,512]{1,0:T(8,128)(2,1)S(1)}, u32[]{:S(2)}, u32[]{:S(2)}) collective-permute-start(bf16[16,512]{1,0:T(8,128)(2,1)S(1)} %collective-permute-done.2.refs_0_), channel_id=1, source_target_pairs={{0,8},{8,0},{16,24},{24,16},{1,9},{9,1},{17,25},{25,17},{2,10},{10... | collective-permute-start | bytes 49160 | tf_op jit(solution)/shard_map/ppermute | solution.py:441
  9.7 0.3 %conv.1 = (bf16[128,432]{1,0:T(8,128)(2,1)S(1)}, bf16[128,432]{1,0:T(8,128)(2,1)S(1)}, bf16[128,432]{1,0:T(8,128)(2,1)S(1)}, f32[128,128]{1,0:T(8,128)S(1)}) custom-call(bf16[27,4,32]{2,1,0:T(4,128)(2,1)S(1)} %get-tuple-element.53.conv, f32[1,32]{1,0:T(1,128)S(1)} %get-tuple-element.54.conv_shift), custom_call_target="tpu_custom_call" | custom-call | flops 57500000 | bytes 185000 | tf_op jit(solution)/shard_map/conv/pallas_call | solution.py:407
  10.0 0.7 %levels.1 = (bf16[256,256]{1,0:T(8,128)(2,1)S(1)}, bf16[128,512]{1,0:T(8,128)(2,1)S(1)}, bf16[64,384]{1,0:T(8,128)(2,1)S(1)}, f32[256,128]{1,0:T(8,128)S(1)}, f3...) custom-call(bf16[3,3,32,32]{3,2,1,0:T(8,128)(2,1)S(1)} %get-tuple-element.57., ...), custom_call_target="tpu_custom_call" | custom-call | flops 115000000 | bytes 370000 | tf_op jit(solution)/shard_map/levels/pallas_call | solution.py:429
  10.7 0.0 collective-permute-done.3.refs_1_
  10.7 0.0 collective-permute-done.4.refs_2_
  10.7 1.5 %inner.1 = (bf16[4,9,32,512]{3,2,1,0:T(8,128)(2,1)S(1)}, bf16[2,2,32,512]{3,2,1,0:T(8,128)(2,1)S(1)}) custom-call(bf16[2,4,4,512]{3,2,1,0:T(4,128)(2,1)S(1)} %get-tuple-element.51.own.refs_0_, bf16[2,4,4,512]{3,2,1,0:T(4,128)(2,1)S(1)} %collective-permute-done.near.refs_1_, bf16[2,2,4,4,512]{4,3,2,1,0:T(4,128)(2,1)S(1)} %collective-permute-done.4.refs_2_, ...), custom_call_target="tpu_custom_call" | custom-call | flops 11500000 | bytes 37000 | tf_op jit(solution)/shard_map/inner/pallas_call | solution.py:455
  12.3 0.1 collective-permute-done.1.refs_0_
  12.4 0.2 %collective-permute-start.5 = (bf16[16,512]{1,0:T(8,128)(2,1)S(1)}, bf16[16,512]{1,0:T(8,128)(2,1)S(1)}, u32[]{:S(2)}, u32[]{:S(2)}) collective-permute-start(bf16[16,512]{1,0:T(8,128)(2,1)S(1)} %collective-permute-done.1.refs_0_), channel_id=1, source_target_pairs={{0,8},{8,0},{16,24},{24,16},{1,9},{9,1},{17,25},{25,17},{2,10},{10... | collective-permute-start | bytes 49160 | tf_op jit(solution)/shard_map/ppermute | solution.py:470
  12.6 1.2 %near.1.refs_4_ = bf16[2,32,512]{2,1,0:T(8,128)(2,1)S(1)} custom-call(bf16[16,512]{1,0:T(8,128)(2,1)S(1)} %collective-permute-done.2.refs_0_, bf16[16,512]{1,0:T(8,128)(2,1)S(1)} %collective-permute-done.3.refs_1_, bf16[4,9,32,512]{3,2,1,0:T(8,128)(2,1)S(1)} %get-tuple-element.72.refs_2_, bf16[128,432]{1,0:T(8,128)(2,1)S(1)} %get-tuple-element.75.refs_3_, ...), custom_call_target="tpu_custom_call" | custom-call | flops 1150000000 | bytes 3700000 | tf_op jit(solution)/shard_map/near/pallas_call | solution.py:472
  13.8 0.0 collective-permute-done.5.refs_1_
  13.8 1.8 %far.1 = bf16[2,4,32,512]{3,2,1,0:T(8,128)(2,1)} custom-call(bf16[16,512]{1,0:T(8,128)(2,1)S(1)} %collective-permute-done.1.refs_0_, bf16[16,512]{1,0:T(8,128)(2,1)S(1)} %collective-permute-done.5.refs_1_, bf16[4,9,32,512]{3,2,1,0:T(8,128)(2,1)S(1)} %get-tuple-element.72.refs_2_, bf16[2,2,32,512]{3,2,1,0:T(8,128)(2,1)S(1)} %get-tuple-element.73.refs_3_, ...), custom_call_target="tpu_custom_call" | custom-call | flops 1955000064 | bytes 6290000 | tf_op jit(solution)/shard_map/far/pallas_call | solution.py:483
  (1 shorter events, 0.0 us)
Async XLA Ops:
  0.0 1.5 %collective-permute-start = (bf16[2,4,4,512]{3,2,1,0:T(4,128)(2,1)}, bf16[2,4,4,512]{3,2,1,0:T(4,128)(2,1)S(1)}, u32[]{:S(2)}, u32[]{:S(2)}) collective-permute-start(bf16[2,4,4,512]{3,2,1,0:T(4,128)(2,1)} %refs_0_.1), channel_id=1, source_target_pairs={{0,8},{8,0},{16,24},{24,16},{1,9},{9,1},{17,25},{25,17},{2,10},{10... | collective-permute-start | bytes 98312 | tf_op jit(solution)/shard_map/ppermute | solution.py:378
  1.6 9.2 %collective-permute-start.4 = (bf16[2,2,4,4,512]{4,3,2,1,0:T(4,128)(2,1)S(1)}, bf16[2,2,4,4,512]{4,3,2,1,0:T(4,128)(2,1)S(1)}, u32[]{:S(2)}, u32[]{:S(2)}) collective-permute-start(bf16[2,2,4,4,512]{4,3,2,1,0:T(4,128)(2,1)S(1)} %get-tuple-element.52), channel_id=1, source_target_pairs={{0,16},{8,24},{16,0},{24,8},{1,17},{9,25},{17,1},{25,9},{2,18},{10... | collective-permute-start | bytes 196616 | tf_op jit(solution)/shard_map/ppermute | solution.py:396
  4.5 5.1 %collective-permute-start.2 = (bf16[16,512]{1,0:T(8,128)(2,1)S(1)}, bf16[16,512]{1,0:T(8,128)(2,1)S(1)}, u32[]{:S(2)}, u32[]{:S(2)}) collective-permute-start(bf16[16,512]{1,0:T(8,128)(2,1)S(1)} %get-tuple-element.43), channel_id=1, source_target_pairs={{0,1},{1,0},{2,3},{3,2},{4,5},{5,4},{6,7},{7,6},{8,25},{9,24},{10,... | collective-permute-start | bytes 49160 | tf_op jit(solution)/shard_map/ppermute | solution.py:397
  6.0 6.4 %collective-permute-start.1 = (bf16[16,512]{1,0:T(8,128)(2,1)S(1)}, bf16[16,512]{1,0:T(8,128)(2,1)S(1)}, u32[]{:S(2)}, u32[]{:S(2)}) collective-permute-start(bf16[16,512]{1,0:T(8,128)(2,1)S(1)} %get-tuple-element.42), channel_id=1, source_target_pairs={{0,7},{1,2},{2,1},{3,4},{4,3},{5,6},{6,5},{7,0},{8,31},{9,26},{10,... | collective-permute-start | bytes 49160 | tf_op jit(solution)/shard_map/ppermute | solution.py:398
  9.5 1.2 %collective-permute-start.3 = (bf16[16,512]{1,0:T(8,128)(2,1)S(1)}, bf16[16,512]{1,0:T(8,128)(2,1)S(1)}, u32[]{:S(2)}, u32[]{:S(2)}) collective-permute-start(bf16[16,512]{1,0:T(8,128)(2,1)S(1)} %collective-permute-done.2.refs_0_), channel_id=1, source_target_pairs={{0,8},{8,0},{16,24},{24,16},{1,9},{9,1},{17,25},{25,17},{2,10},{10... | collective-permute-start | bytes 49160 | tf_op jit(solution)/shard_map/ppermute | solution.py:441
  12.4 1.4 %collective-permute-start.5 = (bf16[16,512]{1,0:T(8,128)(2,1)S(1)}, bf16[16,512]{1,0:T(8,128)(2,1)S(1)}, u32[]{:S(2)}, u32[]{:S(2)}) collective-permute-start(bf16[16,512]{1,0:T(8,128)(2,1)S(1)} %collective-permute-done.1.refs_0_), channel_id=1, source_target_pairs={{0,8},{8,0},{16,24},{24,16},{1,9},{9,1},{17,25},{25,17},{2,10},{10... | collective-permute-start | bytes 49160 | tf_op jit(solution)/shard_map/ppermute | solution.py:470

commit v7 on v6

--- a/solution.py
+++ b/solution.py
@@ -221,17 +221,12 @@
                 [jnp.where(first, mine, beside), jnp.where(first, beside, mine)], axis=0
             )
         )
-    outs[2][0] = own[...]
-    outs[2][1] = near[...]
     outs[0][...] = jnp.where(even, rows[0], rows[1])
     outs[1][...] = jnp.where(even, rows[1], rows[0])
 
 
-def inner_kernel(paired, count, *refs):
+def inner_kernel(count, *refs):
     blocks, conv, weights, (patches, out) = refs[:count], refs[count], refs[count + 1 : -2], refs[-2:]
-    if paired:
-        own, near, beyond = blocks
-        blocks = own, beyond.at[0], near, beyond.at[1]
     frames, row_count = blocks[0].shape[:2]
     plane = patches.shape[-1]
     for row in range(row_count):
@@ -366,7 +361,7 @@
         out_specs=[VMEM] * len(sources),
         scratch_shapes=[pltpu.SemaphoreType.DMA((len(sources),))],
         compiler_params=PARAMS,
-        cost_estimate=cost(0.8),
+        cost_estimate=cost(0.01),
         name="fetch",
     )(*sources)
 
@@ -376,14 +371,14 @@
         across = [(index, index ^ 2) for index in range(times)]
         beside = [(index, index ^ 1) for index in range(times)]
         near = lax.ppermute(snapshots, "tm", beside)
-        to_far, to_near, pair = pl.pallas_call(
+        far = lax.ppermute(snapshots, "tm", across)
+        to_far, to_near = pl.pallas_call(
             pack_kernel,
-            out_shape=[jax.ShapeDtypeStruct((total // 2, plane), BF16)] * 2
-            + [jax.ShapeDtypeStruct((2,) + snapshots.shape, BF16)],
+            out_shape=[jax.ShapeDtypeStruct((total // 2, plane), BF16)] * 2,
             in_specs=[VMEM] * 2,
-            out_specs=[VMEM] * 3,
+            out_specs=[VMEM] * 2,
             compiler_params=PARAMS,
-            cost_estimate=cost(0.05),
+            cost_estimate=cost(0.3),
             name="pack",
         )(sources[0], near)
         far_pairs, near_pairs = [], []
@@ -393,7 +388,6 @@
                 step = 2 * (space % 2) - 1
                 far_pairs.append((time * spaces + space, target + (space + step) % spaces))
                 near_pairs.append((time * spaces + space, target + space - step))
-        beyond = lax.ppermute(pair, "tm", across)
         near_halo = lax.ppermute(to_near, ("tm", "space"), near_pairs)
         far_halo = lax.ppermute(to_far, ("tm", "space"), far_pairs)
     else:
@@ -401,8 +395,8 @@
 
     own, conv, conv_shift, *levels = sources
     if paired:
-        near_halo, conv, conv_shift, *levels = lax.optimization_barrier(
-            (near_halo, conv, conv_shift, *levels)
+        near_halo, far, conv, conv_shift, *levels = lax.optimization_barrier(
+            (near_halo, far, conv, conv_shift, *levels)
         )
     *convs, conv_shift = pl.pallas_call(
         functools.partial(conv_kernel, paired),
@@ -411,7 +405,7 @@
         in_specs=[VMEM] * 2,
         out_specs=[VMEM] * 4,
         compiler_params=PARAMS,
-        cost_estimate=cost(0.05),
+        cost_estimate=cost(0.3),
         name="conv",
     )(conv, conv_shift)
 
@@ -432,15 +426,16 @@
         in_specs=[VMEM] * 4,
         out_specs=[VMEM] * len(shapes),
         compiler_params=PARAMS,
-        cost_estimate=cost(0.1),
+        cost_estimate=cost(0.7),
         name="levels",
     )(*levels)
     weights = [conv_shift, *weights]
 
     if paired:
+        both = lax.ppermute(far, "tm", beside)
         near_halos = [near_halo, lax.ppermute(near_halo, "tm", beside)]
         near_halos[1], own = lax.optimization_barrier((near_halos[1], own))
-        blocks = [own, near, beyond]
+        blocks = [own, far, near, both]
     else:
         blocks = [own] + [
             lax.ppermute(snapshots, "tm", ring(times, -offset)) for offset in offsets[1:]
@@ -453,7 +448,7 @@
         far_halos = [lax.ppermute(high, "space", ring(spaces, 1))]
 
     patches, inner = pl.pallas_call(
-        functools.partial(inner_kernel, paired, len(blocks)),
+        functools.partial(inner_kernel, len(blocks)),
         out_shape=[
             jax.ShapeDtypeStruct((row_count, 9, total, plane), BF16),
             jax.ShapeDtypeStruct((frames, row_count - 2, channels, plane), BF16),
@@ -476,7 +471,7 @@
         out_specs=VMEM,
         scratch_shapes=[pltpu.VMEM((9, total, plane), BF16)],
         compiler_params=PARAMS,
-        cost_estimate=cost(1.0),
+        cost_estimate=cost(1),
         name="near",
     )(*near_halos, patches, convs[2], *weights)
 

time: 15.8 us -> 16 us (1.013)
  starting transfers between devices: 8.86 us -> 9.06 us
    ppermute x1, starting transfers between devices: 0.22 us -> 0.57 us  [shards(): near_halos = [near_halo, lax.ppermute(near_halo, 'tm', beside)]]
    ppermute x1 -> x2, starting transfers between devices: 2.9 us -> 2.56 us  [the longest x1 2.49 us: shards(): far = lax.ppermute(snapshots, 'tm', across)]
    ppermute x1 -> x2, waiting for transfers between devices: 0.01 us -> 0.17 us  [the longest x1 0.17 us: shards(): both = lax.ppermute(far, 'tm', beside)]
  transfers between devices with their start and end apart: 6 -> 7, of which waited for: 2 -> 1; matrix products, arithmetic and copies ran while one was open for 0% -> 0% of each run, Pallas kernels for 30% -> 30%
where the time goes in v7:
time: 16 us; the launch traced here: 15.8 us
  starting transfers between devices  9.06 us (57%)
  Pallas kernels  6.5 us (41%)
  waiting for transfers between devices  0.18 us (1%)
    ppermute x1, starting transfers between devices, shards(): far_halo = lax.ppermute(to_far, ('tm', 'space'), far_pairs)  3.54 us
    ppermute x1, starting transfers between devices, shards(): far = lax.ppermute(snapshots, 'tm', across)  2.49 us
    pallas_call x1, Pallas kernels, shards(): pl.pallas_call(functools.partial(far_kernel, paired, len(far_halos)), out...  1.83 us
    ppermute x1, starting transfers between devices, shards(): near_halo = lax.ppermute(to_near, ('tm', 'space'), near_pairs)  1.58 us
    pallas_call x1, Pallas kernels, shards(): pl.pallas_call(functools.partial(inner_kernel, len(blocks)), out_shape=[j...  1.54 us
    pallas_call x1, Pallas kernels, shards(): pl.pallas_call(functools.partial(near_kernel, paired, len(near_halos)), o...  1.15 us
    pallas_call x1, Pallas kernels, shards(): pl.pallas_call(fetch_kernel, out_shape=[jax.ShapeDtypeStruct(source.shape...  1 us
    pallas_call x1, Pallas kernels, shards(): pl.pallas_call(functools.partial(levels_kernel, slot_of, frames), out_sha...  0.65 us
  transfers between devices with their start and end apart: 7, of which 1 were waited for; matrix products, arithmetic and copies ran while one was open for 0% of the time, Pallas kernels for 30%

profile of v7, /device:TPU:0, one launch (start us, length us, event | category | flops | bytes accessed | tf_op | source)
XLA Modules:
  0.0 15.8 jit_solution(886710548540799794)
XLA Ops:
  0.0 0.5 %collective-permute-start = (bf16[2,4,4,512]{3,2,1,0:T(4,128)(2,1)}, bf16[2,4,4,512]{3,2,1,0:T(4,128)(2,1)S(1)}, u32[]{:S(2)}, u32[]{:S(2)}) collective-permute-start(bf16[2,4,4,512]{3,2,1,0:T(4,128)(2,1)} %refs_0_.1), channel_id=1, source_target_pairs={{0,8},{8,0},{16,24},{24,16},{1,9},{9,1},{17,25},{25,17},{2,10},{10... | collective-permute-start | bytes 98312 | tf_op jit(solution)/shard_map/ppermute | solution.py:373
  0.5 2.5 %collective-permute-start.3 = (bf16[2,4,4,512]{3,2,1,0:T(4,128)(2,1)}, bf16[2,4,4,512]{3,2,1,0:T(4,128)(2,1)S(1)}, u32[]{:S(2)}, u32[]{:S(2)}) collective-permute-start(bf16[2,4,4,512]{3,2,1,0:T(4,128)(2,1)} %refs_0_.1), channel_id=1, source_target_pairs={{0,16},{8,24},{16,0},{24,8},{1,17},{9,25},{17,1},{25,9},{2,18},{10... | collective-permute-start | bytes 98312 | tf_op jit(solution)/shard_map/ppermute | solution.py:374
  2.9 1.0 %fetch.1 = (bf16[2,4,4,512]{3,2,1,0:T(4,128)(2,1)S(1)}, bf16[27,4,32]{2,1,0:T(4,128)(2,1)S(1)}, f32[1,32]{1,0:T(1,128)S(1)}, bf16[3,3,32,32]{3,2,1,0:T(8,128)(2,...) custom-call(bf16[2,4,4,512]{3,2,1,0:T(4,128)(2,1)} %refs_0_.1, ...), custom_call_target="tpu_custom_call" | custom-call | flops 11500000 | bytes 37000 | tf_op jit(solution)/shard_map/fetch/pallas_call | solution.py:357
  4.0 0.0 collective-permute-done.near.refs_2_
  4.0 1.6 %collective-permute-start.2 = (bf16[16,512]{1,0:T(8,128)(2,1)S(1)}, bf16[16,512]{1,0:T(8,128)(2,1)S(1)}, u32[]{:S(2)}, u32[]{:S(2)}) collective-permute-start(bf16[16,512]{1,0:T(8,128)(2,1)S(1)} %get-tuple-element.43), channel_id=1, source_target_pairs={{0,1},{1,0},{2,3},{3,2},{4,5},{5,4},{6,7},{7,6},{8,25},{9,24},{10,... | collective-permute-start | bytes 49160 | tf_op jit(solution)/shard_map/ppermute | solution.py:391
  5.6 3.5 %collective-permute-start.1 = (bf16[16,512]{1,0:T(8,128)(2,1)S(1)}, bf16[16,512]{1,0:T(8,128)(2,1)S(1)}, u32[]{:S(2)}, u32[]{:S(2)}) collective-permute-start(bf16[16,512]{1,0:T(8,128)(2,1)S(1)} %get-tuple-element.42), channel_id=1, source_target_pairs={{0,7},{1,2},{2,1},{3,4},{4,3},{5,6},{6,5},{7,0},{8,31},{9,26},{10,... | collective-permute-start | bytes 49160 | tf_op jit(solution)/shard_map/ppermute | solution.py:392
  9.1 0.0 collective-permute-done.3.refs_1_
  9.1 0.0 collective-permute-done.2.refs_0_
  9.1 0.6 %collective-permute-start.4 = (bf16[16,512]{1,0:T(8,128)(2,1)S(1)}, bf16[16,512]{1,0:T(8,128)(2,1)S(1)}, u32[]{:S(2)}, u32[]{:S(2)}) collective-permute-start(bf16[16,512]{1,0:T(8,128)(2,1)S(1)} %collective-permute-done.2.refs_0_), channel_id=1, source_target_pairs={{0,8},{8,0},{16,24},{24,16},{1,9},{9,1},{17,25},{25,17},{2,10},{10... | collective-permute-start | bytes 49160 | tf_op jit(solution)/shard_map/ppermute | solution.py:436
  9.7 0.1 collective-permute-start.5
  9.8 0.7 %levels.1 = (bf16[256,256]{1,0:T(8,128)(2,1)S(1)}, bf16[128,512]{1,0:T(8,128)(2,1)S(1)}, bf16[64,384]{1,0:T(8,128)(2,1)S(1)}, f32[256,128]{1,0:T(8,128)S(1)}, f3...) custom-call(bf16[3,3,32,32]{3,2,1,0:T(8,128)(2,1)S(1)} %get-tuple-element.57., ...), custom_call_target="tpu_custom_call" | custom-call | flops 805000000 | bytes 2590000 | tf_op jit(solution)/shard_map/levels/pallas_call | solution.py:423
  10.4 0.3 %conv.1 = (bf16[128,432]{1,0:T(8,128)(2,1)S(1)}, bf16[128,432]{1,0:T(8,128)(2,1)S(1)}, bf16[128,432]{1,0:T(8,128)(2,1)S(1)}, f32[128,128]{1,0:T(8,128)S(1)}) custom-call(bf16[27,4,32]{2,1,0:T(4,128)(2,1)S(1)} %get-tuple-element.53.conv, f32[1,32]{1,0:T(1,128)S(1)} %get-tuple-element.54.conv_shift), custom_call_target="tpu_custom_call" | custom-call | flops 345000000 | bytes 1110000 | tf_op jit(solution)/shard_map/conv/pallas_call | solution.py:401
  10.7 0.0 collective-permute-done.4.refs_1_
  10.7 0.2 %collective-permute-done.5.refs_3_ = bf16[2,4,4,512]{3,2,1,0:T(4,128)(2,1)S(1)} collective-permute-done((bf16[2,4,4,512]{3,2,1,0:T(4,128)(2,1)S(1)}, bf16[2,4,4,512]{3,2,1,0:T(4,128)(2,1)S(1)}, u32[]{:S(2)}, u32[]{:S(2)}) %collective-permute-start.5) | collective-permute-done | bytes 32800 | tf_op jit(solution)/shard_map/ppermute | solution.py:435
  10.9 1.5 %inner.1 = (bf16[4,9,32,512]{3,2,1,0:T(8,128)(2,1)S(1)}, bf16[2,2,32,512]{3,2,1,0:T(8,128)(2,1)S(1)}) custom-call(bf16[2,4,4,512]{3,2,1,0:T(4,128)(2,1)S(1)} %get-tuple-element.51.own.refs_0_, bf16[2,4,4,512]{3,2,1,0:T(4,128)(2,1)S(1)} %collective-permute-done.3.refs_1_, bf16[2,4,4,512]{3,2,1,0:T(4,128)(2,1)S(1)} %collective-permute-done.near.refs_2_, ...), custom_call_target="tpu_custom_call" | custom-call | flops 11500000 | bytes 37000 | tf_op jit(solution)/shard_map/inner/pallas_call | solution.py:450
  12.5 0.0 collective-permute-done.1.refs_0_
  12.5 0.4 %collective-permute-start.6 = (bf16[16,512]{1,0:T(8,128)(2,1)S(1)}, bf16[16,512]{1,0:T(8,128)(2,1)S(1)}, u32[]{:S(2)}, u32[]{:S(2)}) collective-permute-start(bf16[16,512]{1,0:T(8,128)(2,1)S(1)} %collective-permute-done.1.refs_0_), channel_id=1, source_target_pairs={{0,8},{8,0},{16,24},{24,16},{1,9},{9,1},{17,25},{25,17},{2,10},{10... | collective-permute-start | bytes 49160 | tf_op jit(solution)/shard_map/ppermute | solution.py:465
  12.8 1.2 %near.1.refs_4_ = bf16[2,32,512]{2,1,0:T(8,128)(2,1)S(1)} custom-call(bf16[16,512]{1,0:T(8,128)(2,1)S(1)} %collective-permute-done.2.refs_0_, bf16[16,512]{1,0:T(8,128)(2,1)S(1)} %collective-permute-done.4.refs_1_, bf16[4,9,32,512]{3,2,1,0:T(8,128)(2,1)S(1)} %get-tuple-element.72.refs_2_, bf16[128,432]{1,0:T(8,128)(2,1)S(1)} %get-tuple-element.75.refs_3_, ...), custom_call_target="tpu_custom_call" | custom-call | flops 1150000000 | bytes 3700000 | tf_op jit(solution)/shard_map/near/pallas_call | solution.py:467
  14.0 0.0 collective-permute-done.6.refs_1_
  14.0 1.8 %far.1 = bf16[2,4,32,512]{3,2,1,0:T(8,128)(2,1)} custom-call(bf16[16,512]{1,0:T(8,128)(2,1)S(1)} %collective-permute-done.1.refs_0_, bf16[16,512]{1,0:T(8,128)(2,1)S(1)} %collective-permute-done.6.refs_1_, bf16[4,9,32,512]{3,2,1,0:T(8,128)(2,1)S(1)} %get-tuple-element.72.refs_2_, bf16[2,2,32,512]{3,2,1,0:T(8,128)(2,1)S(1)} %get-tuple-element.73.refs_3_, ...), custom_call_target="tpu_custom_call" | custom-call | flops 1955000064 | bytes 6290000 | tf_op jit(solution)/shard_map/far/pallas_call | solution.py:478
  (1 shorter events, 0.0 us)
Async XLA Ops:
  0.0 4.0 %collective-permute-start = (bf16[2,4,4,512]{3,2,1,0:T(4,128)(2,1)}, bf16[2,4,4,512]{3,2,1,0:T(4,128)(2,1)S(1)}, u32[]{:S(2)}, u32[]{:S(2)}) collective-permute-start(bf16[2,4,4,512]{3,2,1,0:T(4,128)(2,1)} %refs_0_.1), channel_id=1, source_target_pairs={{0,8},{8,0},{16,24},{24,16},{1,9},{9,1},{17,25},{25,17},{2,10},{10... | collective-permute-start | bytes 98312 | tf_op jit(solution)/shard_map/ppermute | solution.py:373
  0.5 8.7 %collective-permute-start.3 = (bf16[2,4,4,512]{3,2,1,0:T(4,128)(2,1)}, bf16[2,4,4,512]{3,2,1,0:T(4,128)(2,1)S(1)}, u32[]{:S(2)}, u32[]{:S(2)}) collective-permute-start(bf16[2,4,4,512]{3,2,1,0:T(4,128)(2,1)} %refs_0_.1), channel_id=1, source_target_pairs={{0,16},{8,24},{16,0},{24,8},{1,17},{9,25},{17,1},{25,9},{2,18},{10... | collective-permute-start | bytes 98312 | tf_op jit(solution)/shard_map/ppermute | solution.py:374
  4.0 5.1 %collective-permute-start.2 = (bf16[16,512]{1,0:T(8,128)(2,1)S(1)}, bf16[16,512]{1,0:T(8,128)(2,1)S(1)}, u32[]{:S(2)}, u32[]{:S(2)}) collective-permute-start(bf16[16,512]{1,0:T(8,128)(2,1)S(1)} %get-tuple-element.43), channel_id=1, source_target_pairs={{0,1},{1,0},{2,3},{3,2},{4,5},{5,4},{6,7},{7,6},{8,25},{9,24},{10,... | collective-permute-start | bytes 49160 | tf_op jit(solution)/shard_map/ppermute | solution.py:391
  5.6 6.9 %collective-permute-start.1 = (bf16[16,512]{1,0:T(8,128)(2,1)S(1)}, bf16[16,512]{1,0:T(8,128)(2,1)S(1)}, u32[]{:S(2)}, u32[]{:S(2)}) collective-permute-start(bf16[16,512]{1,0:T(8,128)(2,1)S(1)} %get-tuple-element.42), channel_id=1, source_target_pairs={{0,7},{1,2},{2,1},{3,4},{4,3},{5,6},{6,5},{7,0},{8,31},{9,26},{10,... | collective-permute-start | bytes 49160 | tf_op jit(solution)/shard_map/ppermute | solution.py:392
  9.1 1.6 %collective-permute-start.4 = (bf16[16,512]{1,0:T(8,128)(2,1)S(1)}, bf16[16,512]{1,0:T(8,128)(2,1)S(1)}, u32[]{:S(2)}, u32[]{:S(2)}) collective-permute-start(bf16[16,512]{1,0:T(8,128)(2,1)S(1)} %collective-permute-done.2.refs_0_), channel_id=1, source_target_pairs={{0,8},{8,0},{16,24},{24,16},{1,9},{9,1},{17,25},{25,17},{2,10},{10... | collective-permute-start | bytes 49160 | tf_op jit(solution)/shard_map/ppermute | solution.py:436
  9.7 1.2 %collective-permute-start.5 = (bf16[2,4,4,512]{3,2,1,0:T(4,128)(2,1)S(1)}, bf16[2,4,4,512]{3,2,1,0:T(4,128)(2,1)S(1)}, u32[]{:S(2)}, u32[]{:S(2)}) collective-permute-start(bf16[2,4,4,512]{3,2,1,0:T(4,128)(2,1)S(1)} %collective-permute-done.3.refs_1_), channel_id=1, source_target_pairs={{0,8},{8,0},{16,24},{24,16},{1,9},{9,1},{17,25},{25,17},{2,10},{10... | collective-permute-start | bytes 98312 | tf_op jit(solution)/shard_map/ppermute | solution.py:435
  12.5 1.5 %collective-permute-start.6 = (bf16[16,512]{1,0:T(8,128)(2,1)S(1)}, bf16[16,512]{1,0:T(8,128)(2,1)S(1)}, u32[]{:S(2)}, u32[]{:S(2)}) collective-permute-start(bf16[16,512]{1,0:T(8,128)(2,1)S(1)} %collective-permute-done.1.refs_0_), channel_id=1, source_target_pairs={{0,8},{8,0},{16,24},{24,16},{1,9},{9,1},{17,25},{25,17},{2,10},{10... | collective-permute-start | bytes 49160 | tf_op jit(solution)/shard_map/ppermute | solution.py:465

commit v8 on v6

--- a/solution.py
+++ b/solution.py
@@ -88,14 +88,14 @@
     wide = depth * GROUP
     flat = conv[...].astype(F32).reshape(depth, channels).astype(BF16)
     down = lax.broadcasted_iota(jnp.int32, (depth, wide), 0)
-    across = lax.broadcasted_iota(jnp.int32, (depth, wide), 1)
-    same = (down // fields == across // (GROUP * fields)) & (down % fields == across % fields)
+    across = lax.broadcasted_iota(jnp.int32, (1, wide), 1)
+    field, group = lax.rem(across, fields), lax.rem(lax.div(across, fields), GROUP)
+    same = down == lax.div(across, GROUP * fields) * fields + field
     pick = jnp.where(same, 1.0, 0.0).astype(BF16)
     full = lax.dot_general(flat, pick, (((0,), (0,)), ((), ())), preferred_element_type=F32)
     full = jnp.concatenate([full] * GROUP, axis=0)
     down = lax.broadcasted_iota(jnp.int32, full.shape, 0)
-    across = lax.broadcasted_iota(jnp.int32, full.shape, 1)
-    keep = down // channels == across // fields % GROUP
+    keep = lax.div(down, channels) == group
     full = jnp.where(keep, 0.5 * full, 0.0)
     third = wide // 3
     turned = jnp.concatenate([full[:, 2 * third :], full[:, third : -third], full[:, :third]], axis=1)
@@ -115,15 +115,16 @@
         rows, columns = tap_outs[level].shape
         columns //= level + 1
 
-        def frame_of(axis):
-            place = lax.broadcasted_iota(jnp.int32, (rows, columns), axis) // channels
-            block = place // frames
-            start = jnp.zeros((rows, columns), jnp.int32)
-            for index, slot in enumerate(slots[: (rows, columns)[axis] // channels // frames]):
+        def frame_of(shape, axis, count):
+            place = lax.div(lax.broadcasted_iota(jnp.int32, shape, axis), channels)
+            block = lax.div(place, frames)
+            start = jnp.zeros(shape, jnp.int32)
+            for index, slot in enumerate(slots[: count // channels // frames]):
                 start = jnp.where(block == index, slot * frames, start)
-            return start + place % frames
-
-        gap = frame_of(1) - frame_of(0)
+            return start + lax.rem(place, frames)
+
+        before = spread(frame_of((rows, 128), 0, rows), rows, columns)
+        gap = frame_of((1, columns), 1, columns) - before
         for source in range(level + 1):
             total = jnp.zeros((rows, columns), F32)
             for tap in range(3):
@@ -318,10 +319,16 @@
 
     def store(cells, frame, final):
         done[frame, :, cells] = final
+        if frame == out.shape[0] - 1:
+            index = len(copies)
+            copies.append(
+                pltpu.make_async_copy(
+                    done.at[:, :, cells], out.at[:, far_row, :, cells], sems.at[index]
+                )
+            )
+            copies[index].start()
 
     encode_edge(paired, True, halos, patches, conv, weights, border, out.shape[0], store)
-    copies.append(pltpu.make_async_copy(done, out.at[:, far_row], sems.at[2]))
-    copies[-1].start()
     for copy in copies:
         copy.wait()
 
@@ -439,7 +446,6 @@
 
     if paired:
         near_halos = [near_halo, lax.ppermute(near_halo, "tm", beside)]
-        near_halos[1], own = lax.optimization_barrier((near_halos[1], own))
         blocks = [own, near, beyond]
     else:
         blocks = [own] + [
@@ -461,7 +467,7 @@
         in_specs=[VMEM] * (len(blocks) + 1 + len(weights)),
         out_specs=[VMEM] * 2,
         compiler_params=PARAMS,
-        cost_estimate=cost(0.01),
+        cost_estimate=cost(0.2),
         name="inner",
     )(*blocks, convs[0], *weights)
 
@@ -476,7 +482,7 @@
         out_specs=VMEM,
         scratch_shapes=[pltpu.VMEM((9, total, plane), BF16)],
         compiler_params=PARAMS,
-        cost_estimate=cost(1.0),
+        cost_estimate=cost(1),
         name="near",
     )(*near_halos, patches, convs[2], *weights)
 
@@ -488,7 +494,7 @@
         scratch_shapes=[
             pltpu.VMEM((9, total, plane), BF16),
             pltpu.VMEM((frames, channels, plane), BF16),
-            pltpu.SemaphoreType.DMA((3,)),
+            pltpu.SemaphoreType.DMA((2 + plane // math.gcd(plane, CELLS),)),
         ],
         compiler_params=PARAMS,
         cost_estimate=cost(1.7),

time: 15.8 us -> 15.9 us (level)
  no operation moved by 1% of the time
where the time goes in v8:
time: 15.9 us; the launch traced here: 15.7 us
  starting transfers between devices  8.88 us (56%)
  Pallas kernels  6.59 us (41%)
  waiting for transfers between devices  0.19 us (1%)
    ppermute x1, starting transfers between devices, shards(): far_halo = lax.ppermute(to_far, ('tm', 'space'), far_pairs)  3.54 us
    ppermute x1, starting transfers between devices, shards(): beyond = lax.ppermute(pair, 'tm', across)  2.9 us
    pallas_call x1, Pallas kernels, shards(): pl.pallas_call(functools.partial(far_kernel, paired, len(far_halos)), out...  1.88 us
    pallas_call x1, Pallas kernels, shards(): pl.pallas_call(functools.partial(inner_kernel, paired, len(blocks)), out_...  1.55 us
    ppermute x1, starting transfers between devices, shards(): near_halo = lax.ppermute(to_near, ('tm', 'space'), near_pairs)  1.52 us
    pallas_call x1, Pallas kernels, shards(): pl.pallas_call(functools.partial(near_kernel, paired, len(near_halos)), o...  1.16 us
    pallas_call x1, Pallas kernels, shards(): pl.pallas_call(fetch_kernel, out_shape=[jax.ShapeDtypeStruct(source.shape...  1 us
    pallas_call x1, Pallas kernels, shards(): pl.pallas_call(functools.partial(levels_kernel, slot_of, frames), out_sha...  0.69 us
  transfers between devices with their start and end apart: 6, of which 2 were waited for; matrix products, arithmetic and copies ran while one was open for 0% of the time, Pallas kernels for 30%

profile of v8, /device:TPU:0, one launch (start us, length us, event | category | flops | bytes accessed | tf_op | source)
XLA Modules:
  0.0 15.7 jit_solution(362974808664725603)
XLA Ops:
  0.0 0.5 %collective-permute-start = (bf16[2,4,4,512]{3,2,1,0:T(4,128)(2,1)}, bf16[2,4,4,512]{3,2,1,0:T(4,128)(2,1)S(1)}, u32[]{:S(2)}, u32[]{:S(2)}) collective-permute-start(bf16[2,4,4,512]{3,2,1,0:T(4,128)(2,1)} %refs_0_.1), channel_id=1, source_target_pairs={{0,8},{8,0},{16,24},{24,16},{1,9},{9,1},{17,25},{25,17},{2,10},{10... | collective-permute-start | bytes 98312 | tf_op jit(solution)/shard_map/ppermute | solution.py:385
  0.5 1.0 %fetch.1 = (bf16[2,4,4,512]{3,2,1,0:T(4,128)(2,1)S(1)}, bf16[27,4,32]{2,1,0:T(4,128)(2,1)S(1)}, f32[1,32]{1,0:T(1,128)S(1)}, bf16[3,3,32,32]{3,2,1,0:T(8,128)(2,...) custom-call(bf16[2,4,4,512]{3,2,1,0:T(4,128)(2,1)} %refs_0_.1, ...), custom_call_target="tpu_custom_call" | custom-call | flops 920000000 | bytes 2960000 | tf_op jit(solution)/shard_map/fetch/pallas_call | solution.py:369
  1.5 0.1 collective-permute-done.near.refs_1_
  1.6 2.9 %collective-permute-start.2 = (bf16[2,2,4,4,512]{4,3,2,1,0:T(4,128)(2,1)S(1)}, bf16[2,2,4,4,512]{4,3,2,1,0:T(4,128)(2,1)S(1)}, u32[]{:S(2)}, u32[]{:S(2)}) collective-permute-start(bf16[2,2,4,4,512]{4,3,2,1,0:T(4,128)(2,1)S(1)} %get-tuple-element.41), channel_id=1, source_target_pairs={{0,16},{8,24},{16,0},{24,8},{1,17},{9,25},{17,1},{25,9},{2,18},{10... | collective-permute-start | bytes 196616 | tf_op jit(solution)/shard_map/ppermute | solution.py:403
  4.5 1.5 %collective-permute-start.3 = (bf16[16,512]{1,0:T(8,128)(2,1)S(1)}, bf16[16,512]{1,0:T(8,128)(2,1)S(1)}, u32[]{:S(2)}, u32[]{:S(2)}) collective-permute-start(bf16[16,512]{1,0:T(8,128)(2,1)S(1)} %get-tuple-element.42), channel_id=1, source_target_pairs={{0,1},{1,0},{2,3},{3,2},{4,5},{5,4},{6,7},{7,6},{8,25},{9,24},{10,... | collective-permute-start | bytes 49160 | tf_op jit(solution)/shard_map/ppermute | solution.py:404
  6.0 3.5 %collective-permute-start.1 = (bf16[16,512]{1,0:T(8,128)(2,1)S(1)}, bf16[16,512]{1,0:T(8,128)(2,1)S(1)}, u32[]{:S(2)}, u32[]{:S(2)}) collective-permute-start(bf16[16,512]{1,0:T(8,128)(2,1)S(1)} %get-tuple-element.40), channel_id=1, source_target_pairs={{0,7},{1,2},{2,1},{3,4},{4,3},{5,6},{6,5},{7,0},{8,31},{9,26},{10,... | collective-permute-start | bytes 49160 | tf_op jit(solution)/shard_map/ppermute | solution.py:405
  9.5 0.0 collective-permute-done.3.refs_0_
  9.5 0.2 %collective-permute-start.5 = (bf16[16,512]{1,0:T(8,128)(2,1)S(1)}, bf16[16,512]{1,0:T(8,128)(2,1)S(1)}, u32[]{:S(2)}, u32[]{:S(2)}) collective-permute-start(bf16[16,512]{1,0:T(8,128)(2,1)S(1)} %collective-permute-done.3.refs_0_), channel_id=1, source_target_pairs={{0,8},{8,0},{16,24},{24,16},{1,9},{9,1},{17,25},{25,17},{2,10},{10... | collective-permute-start | bytes 49160 | tf_op jit(solution)/shard_map/ppermute | solution.py:448
  9.7 0.3 %conv.1 = (bf16[128,432]{1,0:T(8,128)(2,1)S(1)}, bf16[128,432]{1,0:T(8,128)(2,1)S(1)}, bf16[128,432]{1,0:T(8,128)(2,1)S(1)}, f32[128,128]{1,0:T(8,128)S(1)}) custom-call(bf16[27,4,32]{2,1,0:T(4,128)(2,1)S(1)} %get-tuple-element.49.conv, f32[1,32]{1,0:T(1,128)S(1)} %get-tuple-element.50.conv_shift), custom_call_target="tpu_custom_call" | custom-call | flops 57500000 | bytes 185000 | tf_op jit(solution)/shard_map/conv/pallas_call | solution.py:414
  10.0 0.7 %levels.1 = (bf16[256,256]{1,0:T(8,128)(2,1)S(1)}, bf16[128,512]{1,0:T(8,128)(2,1)S(1)}, bf16[64,384]{1,0:T(8,128)(2,1)S(1)}, f32[256,128]{1,0:T(8,128)S(1)}, f3...) custom-call(bf16[3,3,32,32]{3,2,1,0:T(8,128)(2,1)S(1)} %get-tuple-element.53., ...), custom_call_target="tpu_custom_call" | custom-call | flops 115000000 | bytes 370000 | tf_op jit(solution)/shard_map/levels/pallas_call | solution.py:436
  10.7 0.0 collective-permute-done.2.refs_2_
  10.7 1.5 %inner.1 = (bf16[4,9,32,512]{3,2,1,0:T(8,128)(2,1)S(1)}, bf16[2,2,32,512]{3,2,1,0:T(8,128)(2,1)S(1)}) custom-call(bf16[2,4,4,512]{3,2,1,0:T(4,128)(2,1)S(1)} %get-tuple-element.39.own.refs_0_, bf16[2,4,4,512]{3,2,1,0:T(4,128)(2,1)S(1)} %collective-permute-done.near.refs_1_, bf16[2,2,4,4,512]{4,3,2,1,0:T(4,128)(2,1)S(1)} %collective-permute-done.2.refs_2_, ...), custom_call_target="tpu_custom_call" | custom-call | flops 230000000 | bytes 740000 | tf_op jit(solution)/shard_map/inner/pallas_call | solution.py:461
  12.3 0.1 collective-permute-done.1.refs_0_
  12.4 0.2 %collective-permute-start.4 = (bf16[16,512]{1,0:T(8,128)(2,1)S(1)}, bf16[16,512]{1,0:T(8,128)(2,1)S(1)}, u32[]{:S(2)}, u32[]{:S(2)}) collective-permute-start(bf16[16,512]{1,0:T(8,128)(2,1)S(1)} %collective-permute-done.1.refs_0_), channel_id=1, source_target_pairs={{0,8},{8,0},{16,24},{24,16},{1,9},{9,1},{17,25},{25,17},{2,10},{10... | collective-permute-start | bytes 49160 | tf_op jit(solution)/shard_map/ppermute | solution.py:476
  12.6 0.0 collective-permute-done.5.refs_1_
  12.7 1.2 %near.1.refs_4_ = bf16[2,32,512]{2,1,0:T(8,128)(2,1)S(1)} custom-call(bf16[16,512]{1,0:T(8,128)(2,1)S(1)} %collective-permute-done.3.refs_0_, bf16[16,512]{1,0:T(8,128)(2,1)S(1)} %collective-permute-done.5.refs_1_, bf16[4,9,32,512]{3,2,1,0:T(8,128)(2,1)S(1)} %get-tuple-element.68.refs_2_, bf16[128,432]{1,0:T(8,128)(2,1)S(1)} %get-tuple-element.71.refs_3_, ...), custom_call_target="tpu_custom_call" | custom-call | flops 1150000000 | bytes 3700000 | tf_op jit(solution)/shard_map/near/pallas_call | solution.py:478
  13.8 0.0 collective-permute-done.4.refs_1_
  13.8 1.9 %far.1 = bf16[2,4,32,512]{3,2,1,0:T(8,128)(2,1)} custom-call(bf16[16,512]{1,0:T(8,128)(2,1)S(1)} %collective-permute-done.1.refs_0_, bf16[16,512]{1,0:T(8,128)(2,1)S(1)} %collective-permute-done.4.refs_1_, bf16[4,9,32,512]{3,2,1,0:T(8,128)(2,1)S(1)} %get-tuple-element.68.refs_2_, bf16[2,2,32,512]{3,2,1,0:T(8,128)(2,1)S(1)} %get-tuple-element.69.refs_3_, ...), custom_call_target="tpu_custom_call" | custom-call | flops 1955000064 | bytes 6290000 | tf_op jit(solution)/shard_map/far/pallas_call | solution.py:489
  (1 shorter events, 0.0 us)
Async XLA Ops:
  0.0 1.5 %collective-permute-start = (bf16[2,4,4,512]{3,2,1,0:T(4,128)(2,1)}, bf16[2,4,4,512]{3,2,1,0:T(4,128)(2,1)S(1)}, u32[]{:S(2)}, u32[]{:S(2)}) collective-permute-start(bf16[2,4,4,512]{3,2,1,0:T(4,128)(2,1)} %refs_0_.1), channel_id=1, source_target_pairs={{0,8},{8,0},{16,24},{24,16},{1,9},{9,1},{17,25},{25,17},{2,10},{10... | collective-permute-start | bytes 98312 | tf_op jit(solution)/shard_map/ppermute | solution.py:385
  1.6 9.2 %collective-permute-start.2 = (bf16[2,2,4,4,512]{4,3,2,1,0:T(4,128)(2,1)S(1)}, bf16[2,2,4,4,512]{4,3,2,1,0:T(4,128)(2,1)S(1)}, u32[]{:S(2)}, u32[]{:S(2)}) collective-permute-start(bf16[2,2,4,4,512]{4,3,2,1,0:T(4,128)(2,1)S(1)} %get-tuple-element.41), channel_id=1, source_target_pairs={{0,16},{8,24},{16,0},{24,8},{1,17},{9,25},{17,1},{25,9},{2,18},{10... | collective-permute-start | bytes 196616 | tf_op jit(solution)/shard_map/ppermute | solution.py:403
  4.5 5.1 %collective-permute-start.3 = (bf16[16,512]{1,0:T(8,128)(2,1)S(1)}, bf16[16,512]{1,0:T(8,128)(2,1)S(1)}, u32[]{:S(2)}, u32[]{:S(2)}) collective-permute-start(bf16[16,512]{1,0:T(8,128)(2,1)S(1)} %get-tuple-element.42), channel_id=1, source_target_pairs={{0,1},{1,0},{2,3},{3,2},{4,5},{5,4},{6,7},{7,6},{8,25},{9,24},{10,... | collective-permute-start | bytes 49160 | tf_op jit(solution)/shard_map/ppermute | solution.py:404
  6.0 6.4 %collective-permute-start.1 = (bf16[16,512]{1,0:T(8,128)(2,1)S(1)}, bf16[16,512]{1,0:T(8,128)(2,1)S(1)}, u32[]{:S(2)}, u32[]{:S(2)}) collective-permute-start(bf16[16,512]{1,0:T(8,128)(2,1)S(1)} %get-tuple-element.40), channel_id=1, source_target_pairs={{0,7},{1,2},{2,1},{3,4},{4,3},{5,6},{6,5},{7,0},{8,31},{9,26},{10,... | collective-permute-start | bytes 49160 | tf_op jit(solution)/shard_map/ppermute | solution.py:405
  9.5 3.1 %collective-permute-start.5 = (bf16[16,512]{1,0:T(8,128)(2,1)S(1)}, bf16[16,512]{1,0:T(8,128)(2,1)S(1)}, u32[]{:S(2)}, u32[]{:S(2)}) collective-permute-start(bf16[16,512]{1,0:T(8,128)(2,1)S(1)} %collective-permute-done.3.refs_0_), channel_id=1, source_target_pairs={{0,8},{8,0},{16,24},{24,16},{1,9},{9,1},{17,25},{25,17},{2,10},{10... | collective-permute-start | bytes 49160 | tf_op jit(solution)/shard_map/ppermute | solution.py:448
  12.4 1.4 %collective-permute-start.4 = (bf16[16,512]{1,0:T(8,128)(2,1)S(1)}, bf16[16,512]{1,0:T(8,128)(2,1)S(1)}, u32[]{:S(2)}, u32[]{:S(2)}) collective-permute-start(bf16[16,512]{1,0:T(8,128)(2,1)S(1)} %collective-permute-done.1.refs_0_), channel_id=1, source_target_pairs={{0,8},{8,0},{16,24},{24,16},{1,9},{9,1},{17,25},{25,17},{2,10},{10... | collective-permute-start | bytes 49160 | tf_op jit(solution)/shard_map/ppermute | solution.py:476

commit v9 on v4

--- a/solution.py
+++ b/solution.py
@@ -82,7 +82,7 @@
         copy.wait()
 
 
-def conv_kernel(paired, conv, conv_shift, *outs):
+def conv_kernel(conv, conv_shift, *outs):
     places, fields, channels = conv.shape
     depth = places * fields
     wide = depth * GROUP
@@ -99,11 +99,9 @@
     full = jnp.where(keep, 0.5 * full, 0.0)
     third = wide // 3
     turned = jnp.concatenate([full[:, 2 * third :], full[:, third : -third], full[:, :third]], axis=1)
-    even = parity(paired) == 0
     outs[0][...] = full.astype(BF16)
-    outs[1][...] = jnp.where(even, full, turned).astype(BF16)
-    outs[2][...] = jnp.where(even, turned, full).astype(BF16)
-    outs[3][...] = lanes(0.5 * column(conv_shift[...], GROUP))
+    outs[1][...] = turned.astype(BF16)
+    outs[2][...] = lanes(0.5 * column(conv_shift[...], GROUP))
 
 
 def levels_kernel(slot_of, frames, taps, tap_shift, mix, mix_shift, *outs):
@@ -167,10 +165,6 @@
             yield pltpu.roll(piece, -delta_y * NZ % plane, 1) if delta_y else piece
 
 
-def parity(paired):
-    return lax.rem(lax.axis_index("space"), 2) if paired else 0
-
-
 def encode(windows, weights, frames, store):
     conv_shift, mix, mix_shift = weights[0], *weights[-2:]
     taps, tap_shifts = weights[1 : 1 + LEVELS], weights[1 + LEVELS : 1 + 2 * LEVELS]
@@ -208,7 +202,6 @@
 
 def pack_kernel(own, near, *outs):
     frames, row_count = near.shape[:2]
-    even = parity(True) == 0
     first = lax.rem(lax.axis_index("tm"), 2) == 0
     rows = []
     for row in (0, row_count - 1):
@@ -223,8 +216,8 @@
         )
     outs[2][0] = own[...]
     outs[2][1] = near[...]
-    outs[0][...] = jnp.where(even, rows[0], rows[1])
-    outs[1][...] = jnp.where(even, rows[1], rows[0])
+    outs[0][...] = rows[1]
+    outs[1][...] = rows[0]
 
 
 def inner_kernel(paired, count, *refs):
@@ -277,11 +270,6 @@
     return jnp.concatenate(parts[0] + parts[1], axis=0)
 
 
-def edge_row(paired, far, row_count):
-    top = (parity(paired) == 0) == far
-    return jnp.where(top, 0, row_count - 1), jnp.where(top, 1, row_count - 2)
-
-
 def outer_kernel(paired, near, far, *refs):
     near, far = near[...], far[...]
     if paired:
@@ -295,7 +283,7 @@
     row_count, _, _, plane = patches.shape
     depth = convs[0].shape[1] // 27
     width = math.gcd(plane, CELLS)
-    rows = [edge_row(paired, far, row_count) for far in (True, False)]
+    rows = [(0, 1), (row_count - 1, row_count - 2)]
     copies = [pltpu.make_async_copy(inner, out.at[:, 1 : row_count - 1], sems.at[0])]
     copies[0].start()
     windows = []
@@ -328,8 +316,8 @@
 
 
 def cost(microseconds):
-    size = int(microseconds * 3.7e6)
-    return pl.CostEstimate(flops=0, bytes_accessed=size, transcendentals=0)
+    size, flops = int(microseconds * 3.7e6), int(microseconds * 1.15e9)
+    return pl.CostEstimate(flops=flops, bytes_accessed=size, transcendentals=0)
 
 
 def ring(count, step):
@@ -387,9 +375,8 @@
         for time in range(times):
             for space in range(spaces):
                 target = (time ^ (time % 2 * 2)) * spaces
-                step = 2 * (space % 2) - 1
-                far_pairs.append((time * spaces + space, target + (space + step) % spaces))
-                near_pairs.append((time * spaces + space, target + space - step))
+                far_pairs.append((time * spaces + space, target + (space + 1) % spaces))
+                near_pairs.append((time * spaces + space, target + (space - 1) % spaces))
         beyond = lax.ppermute(pair, "tm", across)
         near_halo = lax.ppermute(to_near, ("tm", "space"), near_pairs)
         far_halo = lax.ppermute(to_far, ("tm", "space"), far_pairs)
@@ -398,13 +385,13 @@
 
     own, conv, conv_shift, *levels = sources
     *convs, conv_shift = pl.pallas_call(
-        functools.partial(conv_kernel, paired),
-        out_shape=[jax.ShapeDtypeStruct((tall, 27 * GROUP * fields), BF16)] * 3
+        conv_kernel,
+        out_shape=[jax.ShapeDtypeStruct((tall, 27 * GROUP * fields), BF16)] * 2
         + [jax.ShapeDtypeStruct((tall, 128), F32)],
         in_specs=[VMEM] * 2,
-        out_specs=[VMEM] * 4,
+        out_specs=[VMEM] * 3,
         compiler_params=PARAMS,
-        cost_estimate=cost(0.3),
+        cost_estimate=cost(0.01),
         name="conv",
     )(conv, conv_shift)
 
@@ -425,7 +412,7 @@
         in_specs=[VMEM] * 4,
         out_specs=[VMEM] * len(shapes),
         compiler_params=PARAMS,
-        cost_estimate=cost(0.7),
+        cost_estimate=cost(0.02),
         name="levels",
     )(*levels)
     weights = [conv_shift, *weights]
@@ -445,21 +432,8 @@
             lax.ppermute(high, "space", ring(spaces, 1)),
         ]
 
-    patches, inner = pl.pallas_call(
-        functools.partial(inner_kernel, paired, len(blocks)),
-        out_shape=[
-            jax.ShapeDtypeStruct((row_count, 9, total, plane), BF16),
-            jax.ShapeDtypeStruct((frames, row_count - 2, channels, plane), BF16),
-        ],
-        in_specs=[VMEM] * (len(blocks) + 1 + len(weights)),
-        out_specs=[VMEM] * 2,
-        compiler_params=PARAMS,
-        cost_estimate=cost(1.8),
-        name="inner",
-    )(*blocks, convs[0], *weights)
-
     if paired:
-        near_halo, far_halo, inner = lax.optimization_barrier((near_halo, far_halo, inner))
+        far_halo, near_halo, *weights = lax.optimization_barrier((far_halo, near_halo, *weights))
         merged = pl.pallas_call(
             merge_kernel,
             out_shape=jax.ShapeDtypeStruct((total, plane), BF16),
@@ -470,6 +444,19 @@
             name="merge",
         )(near_halo, far_halo)
         halos = [near_halo, far_halo, lax.ppermute(merged, "tm", beside)]
+
+    patches, inner = pl.pallas_call(
+        functools.partial(inner_kernel, paired, len(blocks)),
+        out_shape=[
+            jax.ShapeDtypeStruct((row_count, 9, total, plane), BF16),
+            jax.ShapeDtypeStruct((frames, row_count - 2, channels, plane), BF16),
+        ],
+        in_specs=[VMEM] * (len(blocks) + 1 + len(weights)),
+        out_specs=[VMEM] * 2,
+        compiler_params=PARAMS,
+        cost_estimate=cost(0.5),
+        name="inner",
+    )(*blocks, convs[0], *weights)
 
     return pl.pallas_call(
         functools.partial(outer_kernel, paired),
@@ -484,7 +471,7 @@
         compiler_params=PARAMS,
         cost_estimate=cost(2.5),
         name="outer",
-    )(*halos, patches, inner, *convs[1:], *weights)
+    )(*halos, patches, inner, *convs, *weights)
 
 
 def solution(mesh):

time: 16 us -> 14.9 us (0.931)
  waiting for transfers between devices: 1.63 us -> 0.91 us
  starting transfers between devices: 8.42 us -> 8.08 us
    ppermute x1, starting transfers between devices: 3.54 us -> 1.52 us  [shards(): far_halo = lax.ppermute(to_far, ('tm', 'space'), far_pairs)]
    ppermute x1, starting transfers between devices: 1.52 us -> 3.2 us  [shards(): near_halo = lax.ppermute(to_near, ('tm', 'space'), near_pairs)]
    ppermute x1, waiting for transfers between devices: 1.2 us -> 0.01 us  [shards(): halos = [near_halo, far_halo, lax.ppermute(merged, 'tm', beside)]]
    ppermute x1, waiting for transfers between devices: 0.36 us -> 0.84 us  [shards(): far_halo = lax.ppermute(to_far, ('tm', 'space'), far_pairs)]
  transfers between devices with their start and end apart: 5 -> 5, of which waited for: 3 -> 2; matrix products, arithmetic and copies ran while one was open for 0% -> 0% of each run, Pallas kernels for 22% -> 24%
where the time goes in v9:
time: 14.9 us; the launch traced here: 14.8 us
  starting transfers between devices  8.08 us (54%)
  Pallas kernels  5.72 us (38%)
  waiting for transfers between devices  0.91 us (6%)
    ppermute x1, starting transfers between devices, shards(): near_halo = lax.ppermute(to_near, ('tm', 'space'), near_pairs)  3.2 us
    ppermute x1, starting transfers between devices, shards(): beyond = lax.ppermute(pair, 'tm', across)  2.9 us
    pallas_call x1, Pallas kernels, shards(): pl.pallas_call(functools.partial(outer_kernel, paired), out_shape=jax.Sha...  2.19 us
    pallas_call x1, Pallas kernels, shards(): pl.pallas_call(functools.partial(inner_kernel, paired, len(blocks)), out_...  1.55 us
    ppermute x1, starting transfers between devices, shards(): far_halo = lax.ppermute(to_far, ('tm', 'space'), far_pairs)  1.52 us
    pallas_call x1, Pallas kernels, shards(): pl.pallas_call(fetch_kernel, out_shape=[jax.ShapeDtypeStruct(source.shape...  1 us
    ppermute x1, waiting for transfers between devices, shards(): far_halo = lax.ppermute(to_far, ('tm', 'space'), far_pairs)  0.84 us
    pallas_call x1, Pallas kernels, shards(): pl.pallas_call(functools.partial(levels_kernel, slot_of, frames), out_sha...  0.66 us
  transfers between devices with their start and end apart: 5, of which 2 were waited for; matrix products, arithmetic and copies ran while one was open for 0% of the time, Pallas kernels for 24%

profile of v9, /device:TPU:0, one launch (start us, length us, event | category | flops | bytes accessed | tf_op | source)
XLA Modules:
  0.0 14.8 jit_solution(15528051205913593503)
XLA Ops:
  0.0 0.5 %collective-permute-start = (bf16[2,4,4,512]{3,2,1,0:T(4,128)(2,1)}, bf16[2,4,4,512]{3,2,1,0:T(4,128)(2,1)S(1)}, u32[]{:S(2)}, u32[]{:S(2)}) collective-permute-start(bf16[2,4,4,512]{3,2,1,0:T(4,128)(2,1)} %refs_0_.1), channel_id=1, source_target_pairs={{0,8},{8,0},{16,24},{24,16},{1,9},{9,1},{17,25},{25,17},{2,10},{10... | collective-permute-start | bytes 98312 | tf_op jit(solution)/shard_map/ppermute | solution.py:363
  0.5 1.0 %fetch.1 = (bf16[2,4,4,512]{3,2,1,0:T(4,128)(2,1)S(1)}, bf16[27,4,32]{2,1,0:T(4,128)(2,1)S(1)}, f32[1,32]{1,0:T(1,128)S(1)}, bf16[3,3,32,32]{3,2,1,0:T(8,128)(2,...) custom-call(bf16[2,4,4,512]{3,2,1,0:T(4,128)(2,1)} %refs_0_.1, ...), custom_call_target="tpu_custom_call" | custom-call | flops 920000000 | bytes 2960000 | tf_op jit(solution)/shard_map/fetch/pallas_call | solution.py:347
  1.5 0.1 collective-permute-done.near.refs_1_
  1.6 2.9 %collective-permute-start.4 = (bf16[2,2,4,4,512]{4,3,2,1,0:T(4,128)(2,1)S(1)}, bf16[2,2,4,4,512]{4,3,2,1,0:T(4,128)(2,1)S(1)}, u32[]{:S(2)}, u32[]{:S(2)}) collective-permute-start(bf16[2,2,4,4,512]{4,3,2,1,0:T(4,128)(2,1)S(1)} %get-tuple-element.59), channel_id=1, source_target_pairs={{0,16},{8,24},{16,0},{24,8},{1,17},{9,25},{17,1},{25,9},{2,18},{10... | collective-permute-start | bytes 196616 | tf_op jit(solution)/shard_map/ppermute | solution.py:380
  4.5 1.5 %collective-permute-start.1 = (bf16[16,512]{1,0:T(8,128)(2,1)S(1)}, bf16[16,512]{1,0:T(8,128)(2,1)S(1)}, u32[]{:S(2)}, u32[]{:S(2)}) collective-permute-start(bf16[16,512]{1,0:T(8,128)(2,1)S(1)} %get-tuple-element.40), channel_id=1, source_target_pairs={{0,1},{1,2},{2,3},{3,4},{4,5},{5,6},{6,7},{7,0},{8,25},{9,26},{10,... | collective-permute-start | bytes 49160 | tf_op jit(solution)/shard_map/ppermute | solution.py:382
  6.0 3.2 %collective-permute-start.2 = (bf16[16,512]{1,0:T(8,128)(2,1)S(1)}, bf16[16,512]{1,0:T(8,128)(2,1)S(1)}, u32[]{:S(2)}, u32[]{:S(2)}) collective-permute-start(bf16[16,512]{1,0:T(8,128)(2,1)S(1)} %get-tuple-element.41), channel_id=1, source_target_pairs={{0,7},{1,0},{2,1},{3,2},{4,3},{5,4},{6,5},{7,6},{8,31},{9,24},{10,... | collective-permute-start | bytes 49160 | tf_op jit(solution)/shard_map/ppermute | solution.py:381
  9.2 0.3 %conv.1 = (bf16[128,432]{1,0:T(8,128)(2,1)S(1)}, bf16[128,432]{1,0:T(8,128)(2,1)S(1)}, f32[128,128]{1,0:T(8,128)S(1)}) custom-call(bf16[27,4,32]{2,1,0:T(4,128)(2,1)S(1)} %get-tuple-element.42.conv, f32[1,32]{1,0:T(1,128)S(1)} %get-tuple-element.43.conv_shift), custom_call_target="tpu_custom_call" | custom-call | flops 11500000 | bytes 37000 | tf_op jit(solution)/shard_map/conv/pallas_call | solution.py:387
  9.5 0.7 %levels.1 = (bf16[256,256]{1,0:T(8,128)(2,1)S(1)}, bf16[128,512]{1,0:T(8,128)(2,1)S(1)}, bf16[64,384]{1,0:T(8,128)(2,1)S(1)}, f32[256,128]{1,0:T(8,128)S(1)}, f3...) custom-call(bf16[3,3,32,32]{3,2,1,0:T(8,128)(2,1)S(1)} %get-tuple-element.45., ...), custom_call_target="tpu_custom_call" | custom-call | flops 23000000 | bytes 74000 | tf_op jit(solution)/shard_map/levels/pallas_call | solution.py:409
  10.1 0.8 %collective-permute-done.1.far = bf16[16,512]{1,0:T(8,128)(2,1)S(1)} collective-permute-done((bf16[16,512]{1,0:T(8,128)(2,1)S(1)}, bf16[16,512]{1,0:T(8,128)(2,1)S(1)}, u32[]{:S(2)}, u32[]{:S(2)}) %collective-permute-start.1) | collective-permute-done | bytes 16416 | tf_op jit(solution)/shard_map/ppermute | solution.py:382
  11.0 0.0 collective-permute-done.2.near
  11.0 0.0 collective-permute-start.3
  11.0 0.0 collective-permute-done.4.refs_2_
  11.0 1.5 %inner.1 = (bf16[4,9,32,512]{3,2,1,0:T(8,128)(2,1)S(1)}, bf16[2,2,32,512]{3,2,1,0:T(8,128)(2,1)S(1)}) custom-call(bf16[2,4,4,512]{3,2,1,0:T(4,128)(2,1)S(1)} %get-tuple-element.39.own.refs_0_, bf16[2,4,4,512]{3,2,1,0:T(4,128)(2,1)S(1)} %collective-permute-done.near.refs_1_, bf16[2,2,4,4,512]{4,3,2,1,0:T(4,128)(2,1)S(1)} %collective-permute-done.4.refs_2_, ...), custom_call_target="tpu_custom_call" | custom-call | flops 575000000 | bytes 1850000 | tf_op jit(solution)/shard_map/inner/pallas_call | solution.py:448
  12.5 0.0 collective-permute-done.3.refs_0_
  12.6 2.2 %outer.1 = bf16[2,4,32,512]{3,2,1,0:T(8,128)(2,1)} custom-call(bf16[16,512]{1,0:T(8,128)(2,1)S(1)} %collective-permute-done.2.near, bf16[16,512]{1,0:T(8,128)(2,1)S(1)} %collective-permute-done.1.far, bf16[32,512]{1,0:T(8,128)(2,1)S(1)} %collective-permute-done.3.refs_0_, bf16[4,9,32,512]{3,2,1,0:T(8,128)(2,1)S(1)} %get-tuple-element.70.refs_1_, ...), custom_call_target="tpu_custom_call" | custom-call | flops 2875000064 | bytes 9250000 | tf_op jit(solution)/shard_map/outer/pallas_call | solution.py:461
  (2 shorter events, 0.0 us)
Async XLA Ops:
  0.0 1.5 %collective-permute-start = (bf16[2,4,4,512]{3,2,1,0:T(4,128)(2,1)}, bf16[2,4,4,512]{3,2,1,0:T(4,128)(2,1)S(1)}, u32[]{:S(2)}, u32[]{:S(2)}) collective-permute-start(bf16[2,4,4,512]{3,2,1,0:T(4,128)(2,1)} %refs_0_.1), channel_id=1, source_target_pairs={{0,8},{8,0},{16,24},{24,16},{1,9},{9,1},{17,25},{25,17},{2,10},{10... | collective-permute-start | bytes 98312 | tf_op jit(solution)/shard_map/ppermute | solution.py:363
  1.6 9.4 %collective-permute-start.4 = (bf16[2,2,4,4,512]{4,3,2,1,0:T(4,128)(2,1)S(1)}, bf16[2,2,4,4,512]{4,3,2,1,0:T(4,128)(2,1)S(1)}, u32[]{:S(2)}, u32[]{:S(2)}) collective-permute-start(bf16[2,2,4,4,512]{4,3,2,1,0:T(4,128)(2,1)S(1)} %get-tuple-element.59), channel_id=1, source_target_pairs={{0,16},{8,24},{16,0},{24,8},{1,17},{9,25},{17,1},{25,9},{2,18},{10... | collective-permute-start | bytes 196616 | tf_op jit(solution)/shard_map/ppermute | solution.py:380
  4.5 6.5 %collective-permute-start.1 = (bf16[16,512]{1,0:T(8,128)(2,1)S(1)}, bf16[16,512]{1,0:T(8,128)(2,1)S(1)}, u32[]{:S(2)}, u32[]{:S(2)}) collective-permute-start(bf16[16,512]{1,0:T(8,128)(2,1)S(1)} %get-tuple-element.40), channel_id=1, source_target_pairs={{0,1},{1,2},{2,3},{3,4},{4,5},{5,6},{6,7},{7,0},{8,25},{9,26},{10,... | collective-permute-start | bytes 49160 | tf_op jit(solution)/shard_map/ppermute | solution.py:382
  6.0 5.0 %collective-permute-start.2 = (bf16[16,512]{1,0:T(8,128)(2,1)S(1)}, bf16[16,512]{1,0:T(8,128)(2,1)S(1)}, u32[]{:S(2)}, u32[]{:S(2)}) collective-permute-start(bf16[16,512]{1,0:T(8,128)(2,1)S(1)} %get-tuple-element.41), channel_id=1, source_target_pairs={{0,7},{1,0},{2,1},{3,2},{4,3},{5,4},{6,5},{7,6},{8,31},{9,24},{10,... | collective-permute-start | bytes 49160 | tf_op jit(solution)/shard_map/ppermute | solution.py:381
  11.0 1.6 %collective-permute-start.3 = (bf16[32,512]{1,0:T(8,128)(2,1)S(1)}, bf16[32,512]{1,0:T(8,128)(2,1)S(1)}, u32[]{:S(2)}, u32[]{:S(2)}) collective-permute-start(bf16[32,512]{1,0:T(8,128)(2,1)S(1)} %merge.1), channel_id=1, source_target_pairs={{0,8},{8,0},{16,24},{24,16},{1,9},{9,1},{17,25},{25,17},{2,10},{10... | collective-permute-start | bytes 98312 | tf_op jit(solution)/shard_map/ppermute | solution.py:446

commit v10 on v9

--- a/solution.py
+++ b/solution.py
@@ -384,6 +384,10 @@
         slot_of = lambda index: [(index + offset) % times for offset in offsets]
 
     own, conv, conv_shift, *levels = sources
+    if paired:
+        far_halo, conv, conv_shift, *levels = lax.optimization_barrier(
+            (far_halo, conv, conv_shift, *levels)
+        )
     *convs, conv_shift = pl.pallas_call(
         conv_kernel,
         out_shape=[jax.ShapeDtypeStruct((tall, 27 * GROUP * fields), BF16)] * 2
@@ -391,7 +395,7 @@
         in_specs=[VMEM] * 2,
         out_specs=[VMEM] * 3,
         compiler_params=PARAMS,
-        cost_estimate=cost(0.01),
+        cost_estimate=cost(0.15),
         name="conv",
     )(conv, conv_shift)
 
@@ -412,7 +416,7 @@
         in_specs=[VMEM] * 4,
         out_specs=[VMEM] * len(shapes),
         compiler_params=PARAMS,
-        cost_estimate=cost(0.02),
+        cost_estimate=cost(0.35),
         name="levels",
     )(*levels)
     weights = [conv_shift, *weights]

time: 14.9 us -> 14.6 us (0.980)
  waiting for transfers between devices: 0.91 us -> 0.55 us
    ppermute x1, starting transfers between devices: 2.9 us -> 1.49 us  [shards(): beyond = lax.ppermute(pair, 'tm', across)]
    ppermute x1, starting transfers between devices: 1.52 us -> 2.91 us  [shards(): far_halo = lax.ppermute(to_far, ('tm', 'space'), far_pairs)]
    ppermute x1, waiting for transfers between devices: 0.84 us -> 0.06 us  [shards(): far_halo = lax.ppermute(to_far, ('tm', 'space'), far_pairs)]
    ppermute x1, waiting for transfers between devices: 0.01 us -> 0.42 us  [shards(): near_halo = lax.ppermute(to_near, ('tm', 'space'), near_pairs)]
  transfers between devices with their start and end apart: 5 -> 5, of which waited for: 2 -> 3; matrix products, arithmetic and copies ran while one was open for 0% -> 0% of each run, Pallas kernels for 24% -> 24%
where the time goes in v10:
time: 14.6 us; the launch traced here: 14.5 us
  starting transfers between devices  8.15 us (56%)
  Pallas kernels  5.72 us (39%)
  waiting for transfers between devices  0.55 us (4%)
    ppermute x1, starting transfers between devices, shards(): near_halo = lax.ppermute(to_near, ('tm', 'space'), near_pairs)  3.2 us
    ppermute x1, starting transfers between devices, shards(): far_halo = lax.ppermute(to_far, ('tm', 'space'), far_pairs)  2.91 us
    pallas_call x1, Pallas kernels, shards(): pl.pallas_call(functools.partial(outer_kernel, paired), out_shape=jax.Sha...  2.2 us
    pallas_call x1, Pallas kernels, shards(): pl.pallas_call(functools.partial(inner_kernel, paired, len(blocks)), out_...  1.55 us
    ppermute x1, starting transfers between devices, shards(): beyond = lax.ppermute(pair, 'tm', across)  1.49 us
    pallas_call x1, Pallas kernels, shards(): pl.pallas_call(fetch_kernel, out_shape=[jax.ShapeDtypeStruct(source.shape...  1 us
    pallas_call x1, Pallas kernels, shards(): pl.pallas_call(functools.partial(levels_kernel, slot_of, frames), out_sha...  0.65 us
    ppermute x1, starting transfers between devices, shards(): near = lax.ppermute(snapshots, 'tm', beside)  0.45 us
  transfers between devices with their start and end apart: 5, of which 3 were waited for; matrix products, arithmetic and copies ran while one was open for 0% of the time, Pallas kernels for 24%

profile of v10, /device:TPU:0, one launch (start us, length us, event | category | flops | bytes accessed | tf_op | source)
XLA Modules:
  0.0 14.5 jit_solution(7163444758343820912)
XLA Ops:
  0.0 0.5 %collective-permute-start = (bf16[2,4,4,512]{3,2,1,0:T(4,128)(2,1)}, bf16[2,4,4,512]{3,2,1,0:T(4,128)(2,1)S(1)}, u32[]{:S(2)}, u32[]{:S(2)}) collective-permute-start(bf16[2,4,4,512]{3,2,1,0:T(4,128)(2,1)} %refs_0_.1), channel_id=1, source_target_pairs={{0,8},{8,0},{16,24},{24,16},{1,9},{9,1},{17,25},{25,17},{2,10},{10... | collective-permute-start | bytes 98312 | tf_op jit(solution)/shard_map/ppermute | solution.py:363
  0.5 1.0 %fetch.1 = (bf16[2,4,4,512]{3,2,1,0:T(4,128)(2,1)S(1)}, bf16[27,4,32]{2,1,0:T(4,128)(2,1)S(1)}, f32[1,32]{1,0:T(1,128)S(1)}, bf16[3,3,32,32]{3,2,1,0:T(8,128)(2,...) custom-call(bf16[2,4,4,512]{3,2,1,0:T(4,128)(2,1)} %refs_0_.1, ...), custom_call_target="tpu_custom_call" | custom-call | flops 920000000 | bytes 2960000 | tf_op jit(solution)/shard_map/fetch/pallas_call | solution.py:347
  1.5 0.1 collective-permute-done.near.refs_1_
  1.6 2.9 %collective-permute-start.1 = (bf16[16,512]{1,0:T(8,128)(2,1)S(1)}, bf16[16,512]{1,0:T(8,128)(2,1)S(1)}, u32[]{:S(2)}, u32[]{:S(2)}) collective-permute-start(bf16[16,512]{1,0:T(8,128)(2,1)S(1)} %get-tuple-element.47), channel_id=1, source_target_pairs={{0,1},{1,2},{2,3},{3,4},{4,5},{5,6},{6,7},{7,0},{8,25},{9,26},{10,... | collective-permute-start | bytes 49160 | tf_op jit(solution)/shard_map/ppermute | solution.py:382
  4.5 1.5 %collective-permute-start.4 = (bf16[2,2,4,4,512]{4,3,2,1,0:T(4,128)(2,1)S(1)}, bf16[2,2,4,4,512]{4,3,2,1,0:T(4,128)(2,1)S(1)}, u32[]{:S(2)}, u32[]{:S(2)}) collective-permute-start(bf16[2,2,4,4,512]{4,3,2,1,0:T(4,128)(2,1)S(1)} %get-tuple-element.73), channel_id=1, source_target_pairs={{0,16},{8,24},{16,0},{24,8},{1,17},{9,25},{17,1},{25,9},{2,18},{10... | collective-permute-start | bytes 196616 | tf_op jit(solution)/shard_map/ppermute | solution.py:380
  6.0 3.2 %collective-permute-start.2 = (bf16[16,512]{1,0:T(8,128)(2,1)S(1)}, bf16[16,512]{1,0:T(8,128)(2,1)S(1)}, u32[]{:S(2)}, u32[]{:S(2)}) collective-permute-start(bf16[16,512]{1,0:T(8,128)(2,1)S(1)} %get-tuple-element.55), channel_id=1, source_target_pairs={{0,7},{1,0},{2,1},{3,2},{4,3},{5,4},{6,5},{7,6},{8,31},{9,24},{10,... | collective-permute-start | bytes 49160 | tf_op jit(solution)/shard_map/ppermute | solution.py:381
  9.2 0.1 collective-permute-done.1.far
  9.2 0.7 %levels.1 = (bf16[256,256]{1,0:T(8,128)(2,1)S(1)}, bf16[128,512]{1,0:T(8,128)(2,1)S(1)}, bf16[64,384]{1,0:T(8,128)(2,1)S(1)}, f32[256,128]{1,0:T(8,128)S(1)}, f3...) custom-call(bf16[3,3,32,32]{3,2,1,0:T(8,128)(2,1)S(1)} %get-tuple-element.59., ...), custom_call_target="tpu_custom_call" | custom-call | flops 402500000 | bytes 1295000 | tf_op jit(solution)/shard_map/levels/pallas_call | solution.py:413
  9.9 0.3 %conv.1 = (bf16[128,432]{1,0:T(8,128)(2,1)S(1)}, bf16[128,432]{1,0:T(8,128)(2,1)S(1)}, f32[128,128]{1,0:T(8,128)S(1)}) custom-call(bf16[27,4,32]{2,1,0:T(4,128)(2,1)S(1)} %get-tuple-element.56.conv, f32[1,32]{1,0:T(1,128)S(1)} %get-tuple-element.57.conv_shift), custom_call_target="tpu_custom_call" | custom-call | flops 172500000 | bytes 555000 | tf_op jit(solution)/shard_map/conv/pallas_call | solution.py:391
  10.2 0.4 %collective-permute-done.2.near = bf16[16,512]{1,0:T(8,128)(2,1)S(1)} collective-permute-done((bf16[16,512]{1,0:T(8,128)(2,1)S(1)}, bf16[16,512]{1,0:T(8,128)(2,1)S(1)}, u32[]{:S(2)}, u32[]{:S(2)}) %collective-permute-start.2) | collective-permute-done | bytes 16416 | tf_op jit(solution)/shard_map/ppermute | solution.py:381
  10.6 0.1 collective-permute-start.3
  10.7 0.0 collective-permute-done.4.refs_2_
  10.7 1.5 %inner.1 = (bf16[4,9,32,512]{3,2,1,0:T(8,128)(2,1)S(1)}, bf16[2,2,32,512]{3,2,1,0:T(8,128)(2,1)S(1)}) custom-call(bf16[2,4,4,512]{3,2,1,0:T(4,128)(2,1)S(1)} %get-tuple-element.46.own.refs_0_, bf16[2,4,4,512]{3,2,1,0:T(4,128)(2,1)S(1)} %collective-permute-done.near.refs_1_, bf16[2,2,4,4,512]{4,3,2,1,0:T(4,128)(2,1)S(1)} %collective-permute-done.4.refs_2_, ...), custom_call_target="tpu_custom_call" | custom-call | flops 575000000 | bytes 1850000 | tf_op jit(solution)/shard_map/inner/pallas_call | solution.py:452
  12.3 0.0 collective-permute-done.3.refs_0_
  12.3 2.2 %outer.1 = bf16[2,4,32,512]{3,2,1,0:T(8,128)(2,1)} custom-call(bf16[16,512]{1,0:T(8,128)(2,1)S(1)} %collective-permute-done.2.near, bf16[16,512]{1,0:T(8,128)(2,1)S(1)} %collective-permute-done.1.far, bf16[32,512]{1,0:T(8,128)(2,1)S(1)} %collective-permute-done.3.refs_0_, bf16[4,9,32,512]{3,2,1,0:T(8,128)(2,1)S(1)} %get-tuple-element.84.refs_1_, ...), custom_call_target="tpu_custom_call" | custom-call | flops 2875000064 | bytes 9250000 | tf_op jit(solution)/shard_map/outer/pallas_call | solution.py:465
  (2 shorter events, 0.0 us)
Async XLA Ops:
  0.0 1.5 %collective-permute-start = (bf16[2,4,4,512]{3,2,1,0:T(4,128)(2,1)}, bf16[2,4,4,512]{3,2,1,0:T(4,128)(2,1)S(1)}, u32[]{:S(2)}, u32[]{:S(2)}) collective-permute-start(bf16[2,4,4,512]{3,2,1,0:T(4,128)(2,1)} %refs_0_.1), channel_id=1, source_target_pairs={{0,8},{8,0},{16,24},{24,16},{1,9},{9,1},{17,25},{25,17},{2,10},{10... | collective-permute-start | bytes 98312 | tf_op jit(solution)/shard_map/ppermute | solution.py:363
  1.6 7.7 %collective-permute-start.1 = (bf16[16,512]{1,0:T(8,128)(2,1)S(1)}, bf16[16,512]{1,0:T(8,128)(2,1)S(1)}, u32[]{:S(2)}, u32[]{:S(2)}) collective-permute-start(bf16[16,512]{1,0:T(8,128)(2,1)S(1)} %get-tuple-element.47), channel_id=1, source_target_pairs={{0,1},{1,2},{2,3},{3,4},{4,5},{5,6},{6,7},{7,0},{8,25},{9,26},{10,... | collective-permute-start | bytes 49160 | tf_op jit(solution)/shard_map/ppermute | solution.py:382
  4.5 6.2 %collective-permute-start.4 = (bf16[2,2,4,4,512]{4,3,2,1,0:T(4,128)(2,1)S(1)}, bf16[2,2,4,4,512]{4,3,2,1,0:T(4,128)(2,1)S(1)}, u32[]{:S(2)}, u32[]{:S(2)}) collective-permute-start(bf16[2,2,4,4,512]{4,3,2,1,0:T(4,128)(2,1)S(1)} %get-tuple-element.73), channel_id=1, source_target_pairs={{0,16},{8,24},{16,0},{24,8},{1,17},{9,25},{17,1},{25,9},{2,18},{10... | collective-permute-start | bytes 196616 | tf_op jit(solution)/shard_map/ppermute | solution.py:380
  6.0 4.6 %collective-permute-start.2 = (bf16[16,512]{1,0:T(8,128)(2,1)S(1)}, bf16[16,512]{1,0:T(8,128)(2,1)S(1)}, u32[]{:S(2)}, u32[]{:S(2)}) collective-permute-start(bf16[16,512]{1,0:T(8,128)(2,1)S(1)} %get-tuple-element.55), channel_id=1, source_target_pairs={{0,7},{1,0},{2,1},{3,2},{4,3},{5,4},{6,5},{7,6},{8,31},{9,24},{10,... | collective-permute-start | bytes 49160 | tf_op jit(solution)/shard_map/ppermute | solution.py:381
  10.6 1.7 %collective-permute-start.3 = (bf16[32,512]{1,0:T(8,128)(2,1)S(1)}, bf16[32,512]{1,0:T(8,128)(2,1)S(1)}, u32[]{:S(2)}, u32[]{:S(2)}) collective-permute-start(bf16[32,512]{1,0:T(8,128)(2,1)S(1)} %merge.1), channel_id=1, source_target_pairs={{0,8},{8,0},{16,24},{24,16},{1,9},{9,1},{17,25},{25,17},{2,10},{10... | collective-permute-start | bytes 98312 | tf_op jit(solution)/shard_map/ppermute | solution.py:450

commit v11 on v10

--- a/solution.py
+++ b/solution.py
@@ -220,17 +220,21 @@
     outs[1][...] = rows[0]
 
 
-def inner_kernel(paired, count, *refs):
-    blocks, conv, weights, (patches, out) = refs[:count], refs[count], refs[count + 1 : -2], refs[-2:]
+def patch_kernel(paired, *refs):
+    blocks, patches = refs[:-1], refs[-1]
     if paired:
         own, near, beyond = blocks
         blocks = own, beyond.at[0], near, beyond.at[1]
     frames, row_count = blocks[0].shape[:2]
-    plane = patches.shape[-1]
     for row in range(row_count):
         lines = [block[frame, row] for block in blocks for frame in range(frames)]
         for place, piece in enumerate(shifted(jnp.concatenate(lines, axis=0))):
             patches[row, place] = piece
+
+
+def inner_kernel(patches, conv, *rest):
+    weights, out = rest[:-1], rest[-1]
+    row_count, _, _, plane = patches.shape
     depth = conv.shape[1] // 27
     width = math.gcd(plane, CELLS)
     places = [
@@ -436,8 +440,20 @@
             lax.ppermute(high, "space", ring(spaces, 1)),
         ]
 
-    if paired:
-        far_halo, near_halo, *weights = lax.optimization_barrier((far_halo, near_halo, *weights))
+    patches = pl.pallas_call(
+        functools.partial(patch_kernel, paired),
+        out_shape=jax.ShapeDtypeStruct((row_count, 9, total, plane), BF16),
+        in_specs=[VMEM] * len(blocks),
+        out_specs=VMEM,
+        compiler_params=PARAMS,
+        cost_estimate=cost(0.01),
+        name="patch",
+    )(*blocks)
+
+    if paired:
+        far_halo, near_halo, patches, *weights = lax.optimization_barrier(
+            (far_halo, near_halo, patches, *weights)
+        )
         merged = pl.pallas_call(
             merge_kernel,
             out_shape=jax.ShapeDtypeStruct((total, plane), BF16),
@@ -449,18 +465,15 @@
         )(near_halo, far_halo)
         halos = [near_halo, far_halo, lax.ppermute(merged, "tm", beside)]
 
-    patches, inner = pl.pallas_call(
-        functools.partial(inner_kernel, paired, len(blocks)),
-        out_shape=[
-            jax.ShapeDtypeStruct((row_count, 9, total, plane), BF16),
-            jax.ShapeDtypeStruct((frames, row_count - 2, channels, plane), BF16),
-        ],
-        in_specs=[VMEM] * (len(blocks) + 1 + len(weights)),
-        out_specs=[VMEM] * 2,
+    inner = pl.pallas_call(
+        inner_kernel,
+        out_shape=jax.ShapeDtypeStruct((frames, row_count - 2, channels, plane), BF16),
+        in_specs=[VMEM] * (2 + len(weights)),
+        out_specs=VMEM,
         compiler_params=PARAMS,
         cost_estimate=cost(0.5),
         name="inner",
-    )(*blocks, convs[0], *weights)
+    )(patches, convs[0], *weights)
 
     return pl.pallas_call(
         functools.partial(outer_kernel, paired),

time: 14.6 us -> 15 us (1.027)
  waiting for transfers between devices: 0.55 us -> 0.13 us
  starting transfers between devices: 8.15 us -> 8.56 us
  Pallas kernels: 5.72 us -> 6.11 us
    ppermute x1, waiting for transfers between devices: 0.42 us -> 0.01 us  [shards(): near_halo = lax.ppermute(to_near, ('tm', 'space'), near_pairs)]
    ppermute x1, starting transfers between devices: 0.09 us -> 0.5 us  [shards(): halos = [near_halo, far_halo, lax.ppermute(merged, 'tm', beside)]]
    pallas_call x1 -> x2, Pallas kernels: 1.55 us -> 1.92 us  [the longest x1 1.39 us: shards(): pl.pallas_call(inner_kernel, out_shape=jax.ShapeDtypeStruct((frames, row_...]
  transfers between devices with their start and end apart: 5 -> 5, of which waited for: 3 -> 2; matrix products, arithmetic and copies ran while one was open for 0% -> 0% of each run, Pallas kernels for 24% -> 26%
where the time goes in v11:
time: 15 us; the launch traced here: 14.9 us
  starting transfers between devices  8.56 us (57%)
  Pallas kernels  6.11 us (41%)
    ppermute x1, starting transfers between devices, shards(): near_halo = lax.ppermute(to_near, ('tm', 'space'), near_pairs)  3.2 us
    ppermute x1, starting transfers between devices, shards(): far_halo = lax.ppermute(to_far, ('tm', 'space'), far_pairs)  2.91 us
    pallas_call x1, Pallas kernels, shards(): pl.pallas_call(functools.partial(outer_kernel, paired), out_shape=jax.Sha...  2.22 us
    ppermute x1, starting transfers between devices, shards(): beyond = lax.ppermute(pair, 'tm', across)  1.49 us
    pallas_call x1, Pallas kernels, shards(): pl.pallas_call(inner_kernel, out_shape=jax.ShapeDtypeStruct((frames, row_...  1.39 us
    pallas_call x1, Pallas kernels, shards(): pl.pallas_call(fetch_kernel, out_shape=[jax.ShapeDtypeStruct(source.shape...  1 us
    pallas_call x1, Pallas kernels, shards(): pl.pallas_call(functools.partial(levels_kernel, slot_of, frames), out_sha...  0.65 us
    pallas_call x1, Pallas kernels, shards(): pl.pallas_call(functools.partial(patch_kernel, paired), out_shape=jax.Sha...  0.53 us
  transfers between devices with their start and end apart: 5, of which 2 were waited for; matrix products, arithmetic and copies ran while one was open for 0% of the time, Pallas kernels for 26%

profile of v11, /device:TPU:0, one launch (start us, length us, event | category | flops | bytes accessed | tf_op | source)
XLA Modules:
  0.0 14.9 jit_solution(16262795403938226398)
XLA Ops:
  0.0 0.5 %collective-permute-start = (bf16[2,4,4,512]{3,2,1,0:T(4,128)(2,1)}, bf16[2,4,4,512]{3,2,1,0:T(4,128)(2,1)S(1)}, u32[]{:S(2)}, u32[]{:S(2)}) collective-permute-start(bf16[2,4,4,512]{3,2,1,0:T(4,128)(2,1)} %refs_0_.1), channel_id=1, source_target_pairs={{0,8},{8,0},{16,24},{24,16},{1,9},{9,1},{17,25},{25,17},{2,10},{10... | collective-permute-start | bytes 98312 | tf_op jit(solution)/shard_map/ppermute | solution.py:367
  0.5 1.0 %fetch.1 = (bf16[2,4,4,512]{3,2,1,0:T(4,128)(2,1)S(1)}, bf16[27,4,32]{2,1,0:T(4,128)(2,1)S(1)}, f32[1,32]{1,0:T(1,128)S(1)}, bf16[3,3,32,32]{3,2,1,0:T(8,128)(2,...) custom-call(bf16[2,4,4,512]{3,2,1,0:T(4,128)(2,1)} %refs_0_.1, ...), custom_call_target="tpu_custom_call" | custom-call | flops 920000000 | bytes 2960000 | tf_op jit(solution)/shard_map/fetch/pallas_call | solution.py:351
  1.5 0.1 collective-permute-done.near.refs_1_
  1.6 2.9 %collective-permute-start.1 = (bf16[16,512]{1,0:T(8,128)(2,1)S(1)}, bf16[16,512]{1,0:T(8,128)(2,1)S(1)}, u32[]{:S(2)}, u32[]{:S(2)}) collective-permute-start(bf16[16,512]{1,0:T(8,128)(2,1)S(1)} %get-tuple-element.46), channel_id=1, source_target_pairs={{0,1},{1,2},{2,3},{3,4},{4,5},{5,6},{6,7},{7,0},{8,25},{9,26},{10,... | collective-permute-start | bytes 49160 | tf_op jit(solution)/shard_map/ppermute | solution.py:386
  4.5 1.5 %collective-permute-start.3 = (bf16[2,2,4,4,512]{4,3,2,1,0:T(4,128)(2,1)S(1)}, bf16[2,2,4,4,512]{4,3,2,1,0:T(4,128)(2,1)S(1)}, u32[]{:S(2)}, u32[]{:S(2)}) collective-permute-start(bf16[2,2,4,4,512]{4,3,2,1,0:T(4,128)(2,1)S(1)} %get-tuple-element.55), channel_id=1, source_target_pairs={{0,16},{8,24},{16,0},{24,8},{1,17},{9,25},{17,1},{25,9},{2,18},{10... | collective-permute-start | bytes 196616 | tf_op jit(solution)/shard_map/ppermute | solution.py:384
  6.0 3.2 %collective-permute-start.2 = (bf16[16,512]{1,0:T(8,128)(2,1)S(1)}, bf16[16,512]{1,0:T(8,128)(2,1)S(1)}, u32[]{:S(2)}, u32[]{:S(2)}) collective-permute-start(bf16[16,512]{1,0:T(8,128)(2,1)S(1)} %get-tuple-element.54), channel_id=1, source_target_pairs={{0,7},{1,0},{2,1},{3,2},{4,3},{5,4},{6,5},{7,6},{8,31},{9,24},{10,... | collective-permute-start | bytes 49160 | tf_op jit(solution)/shard_map/ppermute | solution.py:385
  9.2 0.1 collective-permute-done.1.far
  9.2 0.7 %levels.1 = (bf16[256,256]{1,0:T(8,128)(2,1)S(1)}, bf16[128,512]{1,0:T(8,128)(2,1)S(1)}, bf16[64,384]{1,0:T(8,128)(2,1)S(1)}, f32[256,128]{1,0:T(8,128)S(1)}, f3...) custom-call(bf16[3,3,32,32]{3,2,1,0:T(8,128)(2,1)S(1)} %get-tuple-element.59., ...), custom_call_target="tpu_custom_call" | custom-call | flops 402500000 | bytes 1295000 | tf_op jit(solution)/shard_map/levels/pallas_call | solution.py:417
  9.9 0.3 %conv.1 = (bf16[128,432]{1,0:T(8,128)(2,1)S(1)}, bf16[128,432]{1,0:T(8,128)(2,1)S(1)}, f32[128,128]{1,0:T(8,128)S(1)}) custom-call(bf16[27,4,32]{2,1,0:T(4,128)(2,1)S(1)} %get-tuple-element.56.conv, f32[1,32]{1,0:T(1,128)S(1)} %get-tuple-element.57.conv_shift), custom_call_target="tpu_custom_call" | custom-call | flops 172500000 | bytes 555000 | tf_op jit(solution)/shard_map/conv/pallas_call | solution.py:395
  10.2 0.0 collective-permute-done.3.refs_2_
  10.2 0.5 %patch.1.patches.refs_1_ = bf16[4,9,32,512]{3,2,1,0:T(8,128)(2,1)S(1)} custom-call(bf16[2,4,4,512]{3,2,1,0:T(4,128)(2,1)S(1)} %get-tuple-element.45.own.refs_0_, bf16[2,4,4,512]{3,2,1,0:T(4,128)(2,1)S(1)} %collective-permute-done.near.refs_1_, bf16[2,2,4,4,512]{4,3,2,1,0:T(4,128)(2,1)S(1)} %collective-permute-done.3.refs_2_), custom_call_target="tpu_custom_call" | custom-call | flops 11500000 | bytes 37000 | tf_op jit(solution)/shard_map/patch/pallas_call | solution.py:443
  10.7 0.0 collective-permute-done.2.near
  10.8 0.5 %collective-permute-start.4 = (bf16[32,512]{1,0:T(8,128)(2,1)S(1)}, bf16[32,512]{1,0:T(8,128)(2,1)S(1)}, u32[]{:S(2)}, u32[]{:S(2)}) collective-permute-start(bf16[32,512]{1,0:T(8,128)(2,1)S(1)} %merge.1), channel_id=1, source_target_pairs={{0,8},{8,0},{16,24},{24,16},{1,9},{9,1},{17,25},{25,17},{2,10},{10... | collective-permute-start | bytes 98312 | tf_op jit(solution)/shard_map/ppermute | solution.py:466
  11.2 1.4 %inner.1.refs_2_ = bf16[2,2,32,512]{3,2,1,0:T(8,128)(2,1)S(1)} custom-call(bf16[4,9,32,512]{3,2,1,0:T(8,128)(2,1)S(1)} %patch.1.patches.refs_1_, bf16[128,432]{1,0:T(8,128)(2,1)S(1)} %get-tuple-element.74.conv.refs_3_, f32[128,128]{1,0:T(8,128)S(1)} %get-tuple-element.75.rest_0_.refs_5_, bf16[256,256]{1,0:T(8,128)(2,1)S(1)} %get-tuple-element.76.rest_1_.refs_6_, ...), custom_call_target="tpu_custom_call" | custom-call | flops 575000000 | bytes 1850000 | tf_op jit(solution)/shard_map/inner/pallas_call | solution.py:468
  12.6 0.0 collective-permute-done.4.refs_0_
  12.6 2.2 %outer.1 = bf16[2,4,32,512]{3,2,1,0:T(8,128)(2,1)} custom-call(bf16[16,512]{1,0:T(8,128)(2,1)S(1)} %collective-permute-done.2.near, bf16[16,512]{1,0:T(8,128)(2,1)S(1)} %collective-permute-done.1.far, bf16[32,512]{1,0:T(8,128)(2,1)S(1)} %collective-permute-done.4.refs_0_, bf16[4,9,32,512]{3,2,1,0:T(8,128)(2,1)S(1)} %patch.1.patches.refs_1_, ...), custom_call_target="tpu_custom_call" | custom-call | flops 2875000064 | bytes 9250000 | tf_op jit(solution)/shard_map/outer/pallas_call | solution.py:478
  (2 shorter events, 0.0 us)
Async XLA Ops:
  0.0 1.5 %collective-permute-start = (bf16[2,4,4,512]{3,2,1,0:T(4,128)(2,1)}, bf16[2,4,4,512]{3,2,1,0:T(4,128)(2,1)S(1)}, u32[]{:S(2)}, u32[]{:S(2)}) collective-permute-start(bf16[2,4,4,512]{3,2,1,0:T(4,128)(2,1)} %refs_0_.1), channel_id=1, source_target_pairs={{0,8},{8,0},{16,24},{24,16},{1,9},{9,1},{17,25},{25,17},{2,10},{10... | collective-permute-start | bytes 98312 | tf_op jit(solution)/shard_map/ppermute | solution.py:367
  1.6 7.7 %collective-permute-start.1 = (bf16[16,512]{1,0:T(8,128)(2,1)S(1)}, bf16[16,512]{1,0:T(8,128)(2,1)S(1)}, u32[]{:S(2)}, u32[]{:S(2)}) collective-permute-start(bf16[16,512]{1,0:T(8,128)(2,1)S(1)} %get-tuple-element.46), channel_id=1, source_target_pairs={{0,1},{1,2},{2,3},{3,4},{4,5},{5,6},{6,7},{7,0},{8,25},{9,26},{10,... | collective-permute-start | bytes 49160 | tf_op jit(solution)/shard_map/ppermute | solution.py:386
  4.5 5.7 %collective-permute-start.3 = (bf16[2,2,4,4,512]{4,3,2,1,0:T(4,128)(2,1)S(1)}, bf16[2,2,4,4,512]{4,3,2,1,0:T(4,128)(2,1)S(1)}, u32[]{:S(2)}, u32[]{:S(2)}) collective-permute-start(bf16[2,2,4,4,512]{4,3,2,1,0:T(4,128)(2,1)S(1)} %get-tuple-element.55), channel_id=1, source_target_pairs={{0,16},{8,24},{16,0},{24,8},{1,17},{9,25},{17,1},{25,9},{2,18},{10... | collective-permute-start | bytes 196616 | tf_op jit(solution)/shard_map/ppermute | solution.py:384
  6.0 4.8 %collective-permute-start.2 = (bf16[16,512]{1,0:T(8,128)(2,1)S(1)}, bf16[16,512]{1,0:T(8,128)(2,1)S(1)}, u32[]{:S(2)}, u32[]{:S(2)}) collective-permute-start(bf16[16,512]{1,0:T(8,128)(2,1)S(1)} %get-tuple-element.54), channel_id=1, source_target_pairs={{0,7},{1,0},{2,1},{3,2},{4,3},{5,4},{6,5},{7,6},{8,31},{9,24},{10,... | collective-permute-start | bytes 49160 | tf_op jit(solution)/shard_map/ppermute | solution.py:385
  10.8 1.9 %collective-permute-start.4 = (bf16[32,512]{1,0:T(8,128)(2,1)S(1)}, bf16[32,512]{1,0:T(8,128)(2,1)S(1)}, u32[]{:S(2)}, u32[]{:S(2)}) collective-permute-start(bf16[32,512]{1,0:T(8,128)(2,1)S(1)} %merge.1), channel_id=1, source_target_pairs={{0,8},{8,0},{16,24},{24,16},{1,9},{9,1},{17,25},{25,17},{2,10},{10... | collective-permute-start | bytes 98312 | tf_op jit(solution)/shard_map/ppermute | solution.py:466

commit v12 on v11

--- a/solution.py
+++ b/solution.py
@@ -232,6 +232,12 @@
             patches[row, place] = piece
 
 
+def prepare_kernel(paired, count, *refs):
+    blocks, (conv, conv_shift), outs = refs[:count], refs[count : count + 2], refs[count + 2 :]
+    patch_kernel(paired, *blocks, outs[0])
+    conv_kernel(conv, conv_shift, *outs[1:])
+
+
 def inner_kernel(patches, conv, *rest):
     weights, out = rest[:-1], rest[-1]
     row_count, _, _, plane = patches.shape
@@ -392,17 +398,6 @@
         far_halo, conv, conv_shift, *levels = lax.optimization_barrier(
             (far_halo, conv, conv_shift, *levels)
         )
-    *convs, conv_shift = pl.pallas_call(
-        conv_kernel,
-        out_shape=[jax.ShapeDtypeStruct((tall, 27 * GROUP * fields), BF16)] * 2
-        + [jax.ShapeDtypeStruct((tall, 128), F32)],
-        in_specs=[VMEM] * 2,
-        out_specs=[VMEM] * 3,
-        compiler_params=PARAMS,
-        cost_estimate=cost(0.15),
-        name="conv",
-    )(conv, conv_shift)
-
     wide_of = [count * frames * channels for count in counts]
     shapes = []
     for level in range(LEVELS):
@@ -420,10 +415,9 @@
         in_specs=[VMEM] * 4,
         out_specs=[VMEM] * len(shapes),
         compiler_params=PARAMS,
-        cost_estimate=cost(0.35),
+        cost_estimate=cost(0.52),
         name="levels",
     )(*levels)
-    weights = [conv_shift, *weights]
 
     if paired:
         blocks = [own, near, beyond]
@@ -440,15 +434,18 @@
             lax.ppermute(high, "space", ring(spaces, 1)),
         ]
 
-    patches = pl.pallas_call(
-        functools.partial(patch_kernel, paired),
-        out_shape=jax.ShapeDtypeStruct((row_count, 9, total, plane), BF16),
-        in_specs=[VMEM] * len(blocks),
-        out_specs=VMEM,
+    patches, *convs, conv_shift = pl.pallas_call(
+        functools.partial(prepare_kernel, paired, len(blocks)),
+        out_shape=[jax.ShapeDtypeStruct((row_count, 9, total, plane), BF16)]
+        + [jax.ShapeDtypeStruct((tall, 27 * GROUP * fields), BF16)] * 2
+        + [jax.ShapeDtypeStruct((tall, 128), F32)],
+        in_specs=[VMEM] * (len(blocks) + 2),
+        out_specs=[VMEM] * 4,
         compiler_params=PARAMS,
         cost_estimate=cost(0.01),
-        name="patch",
-    )(*blocks)
+        name="prepare",
+    )(*blocks, conv, conv_shift)
+    weights = [conv_shift, *weights]
 
     if paired:
         far_halo, near_halo, patches, *weights = lax.optimization_barrier(

time: 15 us -> 14.9 us (level)
    pallas_call x2 -> x1, Pallas kernels: 0.83 us -> 0.73 us  [shards(): pl.pallas_call(functools.partial(prepare_kernel, paired, len(blocks)), ou...]
where the time goes in v12:
time: 14.9 us; the launch traced here: 14.7 us
  starting transfers between devices  8.56 us (57%)
  Pallas kernels  6.01 us (40%)
    ppermute x1, starting transfers between devices, shards(): near_halo = lax.ppermute(to_near, ('tm', 'space'), near_pairs)  3.2 us
    ppermute x1, starting transfers between devices, shards(): far_halo = lax.ppermute(to_far, ('tm', 'space'), far_pairs)  2.91 us
    pallas_call x1, Pallas kernels, shards(): pl.pallas_call(functools.partial(outer_kernel, paired), out_shape=jax.Sha...  2.22 us
    ppermute x1, starting transfers between devices, shards(): beyond = lax.ppermute(pair, 'tm', across)  1.49 us
    pallas_call x1, Pallas kernels, shards(): pl.pallas_call(inner_kernel, out_shape=jax.ShapeDtypeStruct((frames, row_...  1.38 us
    pallas_call x1, Pallas kernels, shards(): pl.pallas_call(fetch_kernel, out_shape=[jax.ShapeDtypeStruct(source.shape...  1 us
    pallas_call x1, Pallas kernels, shards(): pl.pallas_call(functools.partial(prepare_kernel, paired, len(blocks)), ou...  0.73 us
    pallas_call x1, Pallas kernels, shards(): pl.pallas_call(functools.partial(levels_kernel, slot_of, frames), out_sha...  0.65 us
  transfers between devices with their start and end apart: 5, of which 2 were waited for; matrix products, arithmetic and copies ran while one was open for 0% of the time, Pallas kernels for 26%

profile of v12, /device:TPU:0, one launch (start us, length us, event | category | flops | bytes accessed | tf_op | source)
XLA Modules:
  0.0 14.7 jit_solution(2218233323620172267)
XLA Ops:
  0.0 0.5 %collective-permute-start = (bf16[2,4,4,512]{3,2,1,0:T(4,128)(2,1)}, bf16[2,4,4,512]{3,2,1,0:T(4,128)(2,1)S(1)}, u32[]{:S(2)}, u32[]{:S(2)}) collective-permute-start(bf16[2,4,4,512]{3,2,1,0:T(4,128)(2,1)} %refs_0_.1), channel_id=1, source_target_pairs={{0,8},{8,0},{16,24},{24,16},{1,9},{9,1},{17,25},{25,17},{2,10},{10... | collective-permute-start | bytes 98312 | tf_op jit(solution)/shard_map/ppermute | solution.py:373
  0.5 1.0 %fetch.1 = (bf16[2,4,4,512]{3,2,1,0:T(4,128)(2,1)S(1)}, bf16[27,4,32]{2,1,0:T(4,128)(2,1)S(1)}, f32[1,32]{1,0:T(1,128)S(1)}, bf16[3,3,32,32]{3,2,1,0:T(8,128)(2,...) custom-call(bf16[2,4,4,512]{3,2,1,0:T(4,128)(2,1)} %refs_0_.1, ...), custom_call_target="tpu_custom_call" | custom-call | flops 920000000 | bytes 2960000 | tf_op jit(solution)/shard_map/fetch/pallas_call | solution.py:357
  1.5 0.1 collective-permute-done.near.refs_1_
  1.6 2.9 %collective-permute-start.1 = (bf16[16,512]{1,0:T(8,128)(2,1)S(1)}, bf16[16,512]{1,0:T(8,128)(2,1)S(1)}, u32[]{:S(2)}, u32[]{:S(2)}) collective-permute-start(bf16[16,512]{1,0:T(8,128)(2,1)S(1)} %get-tuple-element.47), channel_id=1, source_target_pairs={{0,1},{1,2},{2,3},{3,4},{4,5},{5,6},{6,7},{7,0},{8,25},{9,26},{10,... | collective-permute-start | bytes 49160 | tf_op jit(solution)/shard_map/ppermute | solution.py:392
  4.5 1.5 %collective-permute-start.3 = (bf16[2,2,4,4,512]{4,3,2,1,0:T(4,128)(2,1)S(1)}, bf16[2,2,4,4,512]{4,3,2,1,0:T(4,128)(2,1)S(1)}, u32[]{:S(2)}, u32[]{:S(2)}) collective-permute-start(bf16[2,2,4,4,512]{4,3,2,1,0:T(4,128)(2,1)S(1)} %get-tuple-element.56), channel_id=1, source_target_pairs={{0,16},{8,24},{16,0},{24,8},{1,17},{9,25},{17,1},{25,9},{2,18},{10... | collective-permute-start | bytes 196616 | tf_op jit(solution)/shard_map/ppermute | solution.py:390
  6.0 3.2 %collective-permute-start.2 = (bf16[16,512]{1,0:T(8,128)(2,1)S(1)}, bf16[16,512]{1,0:T(8,128)(2,1)S(1)}, u32[]{:S(2)}, u32[]{:S(2)}) collective-permute-start(bf16[16,512]{1,0:T(8,128)(2,1)S(1)} %get-tuple-element.55), channel_id=1, source_target_pairs={{0,7},{1,0},{2,1},{3,2},{4,3},{5,4},{6,5},{7,6},{8,31},{9,24},{10,... | collective-permute-start | bytes 49160 | tf_op jit(solution)/shard_map/ppermute | solution.py:391
  9.2 0.1 collective-permute-done.1.far
  9.2 0.7 %levels.1 = (bf16[256,256]{1,0:T(8,128)(2,1)S(1)}, bf16[128,512]{1,0:T(8,128)(2,1)S(1)}, bf16[64,384]{1,0:T(8,128)(2,1)S(1)}, f32[256,128]{1,0:T(8,128)S(1)}, f3...) custom-call(bf16[3,3,32,32]{3,2,1,0:T(8,128)(2,1)S(1)} %get-tuple-element.61., ...), custom_call_target="tpu_custom_call" | custom-call | flops 598000000 | bytes 1924000 | tf_op jit(solution)/shard_map/levels/pallas_call | solution.py:412
  9.9 0.0 collective-permute-done.3.refs_2_
  9.9 0.7 %prepare.1 = (bf16[4,9,32,512]{3,2,1,0:T(8,128)(2,1)S(1)}, bf16[128,432]{1,0:T(8,128)(2,1)S(1)}, bf16[128,432]{1,0:T(8,128)(2,1)S(1)}, f32[128,128]{1,0:T(8,128)S(1)}) custom-call(bf16[2,4,4,512]{3,2,1,0:T(4,128)(2,1)S(1)} %get-tuple-element.46.own.refs_0_, bf16[2,4,4,512]{3,2,1,0:T(4,128)(2,1)S(1)} %collective-permute-done.near.refs_1_, ...), custom_call_target="tpu_custom_call" | custom-call | flops 11500000 | bytes 37000 | tf_op jit(solution)/shard_map/prepare/pallas_call | solution.py:437
  10.6 0.0 collective-permute-done.2.near
  10.6 0.5 %collective-permute-start.4 = (bf16[32,512]{1,0:T(8,128)(2,1)S(1)}, bf16[32,512]{1,0:T(8,128)(2,1)S(1)}, u32[]{:S(2)}, u32[]{:S(2)}) collective-permute-start(bf16[32,512]{1,0:T(8,128)(2,1)S(1)} %merge.1), channel_id=1, source_target_pairs={{0,8},{8,0},{16,24},{24,16},{1,9},{9,1},{17,25},{25,17},{2,10},{10... | collective-permute-start | bytes 98312 | tf_op jit(solution)/shard_map/ppermute | solution.py:463
  11.1 1.4 %inner.1.refs_2_ = bf16[2,2,32,512]{3,2,1,0:T(8,128)(2,1)S(1)} custom-call(bf16[4,9,32,512]{3,2,1,0:T(8,128)(2,1)S(1)} %get-tuple-element.75.patches.refs_1_, bf16[128,432]{1,0:T(8,128)(2,1)S(1)} %get-tuple-element.76.conv.refs_3_, f32[128,128]{1,0:T(8,128)S(1)} %get-tuple-element.77.rest_0_.refs_5_, bf16[256,256]{1,0:T(8,128)(2,1)S(1)} %get-tuple-element.78.rest_1_.refs_6_, ...), custom_call_target="tpu_custom_call" | custom-call | flops 575000000 | bytes 1850000 | tf_op jit(solution)/shard_map/inner/pallas_call | solution.py:465
  12.5 0.0 collective-permute-done.4.refs_0_
  12.5 2.2 %outer.1 = bf16[2,4,32,512]{3,2,1,0:T(8,128)(2,1)} custom-call(bf16[16,512]{1,0:T(8,128)(2,1)S(1)} %collective-permute-done.2.near, bf16[16,512]{1,0:T(8,128)(2,1)S(1)} %collective-permute-done.1.far, bf16[32,512]{1,0:T(8,128)(2,1)S(1)} %collective-permute-done.4.refs_0_, bf16[4,9,32,512]{3,2,1,0:T(8,128)(2,1)S(1)} %get-tuple-element.75.patches.refs_1_, ...), custom_call_target="tpu_custom_call" | custom-call | flops 2875000064 | bytes 9250000 | tf_op jit(solution)/shard_map/outer/pallas_call | solution.py:475
  (2 shorter events, 0.0 us)
Async XLA Ops:
  0.0 1.5 %collective-permute-start = (bf16[2,4,4,512]{3,2,1,0:T(4,128)(2,1)}, bf16[2,4,4,512]{3,2,1,0:T(4,128)(2,1)S(1)}, u32[]{:S(2)}, u32[]{:S(2)}) collective-permute-start(bf16[2,4,4,512]{3,2,1,0:T(4,128)(2,1)} %refs_0_.1), channel_id=1, source_target_pairs={{0,8},{8,0},{16,24},{24,16},{1,9},{9,1},{17,25},{25,17},{2,10},{10... | collective-permute-start | bytes 98312 | tf_op jit(solution)/shard_map/ppermute | solution.py:373
  1.6 7.7 %collective-permute-start.1 = (bf16[16,512]{1,0:T(8,128)(2,1)S(1)}, bf16[16,512]{1,0:T(8,128)(2,1)S(1)}, u32[]{:S(2)}, u32[]{:S(2)}) collective-permute-start(bf16[16,512]{1,0:T(8,128)(2,1)S(1)} %get-tuple-element.47), channel_id=1, source_target_pairs={{0,1},{1,2},{2,3},{3,4},{4,5},{5,6},{6,7},{7,0},{8,25},{9,26},{10,... | collective-permute-start | bytes 49160 | tf_op jit(solution)/shard_map/ppermute | solution.py:392
  4.5 5.4 %collective-permute-start.3 = (bf16[2,2,4,4,512]{4,3,2,1,0:T(4,128)(2,1)S(1)}, bf16[2,2,4,4,512]{4,3,2,1,0:T(4,128)(2,1)S(1)}, u32[]{:S(2)}, u32[]{:S(2)}) collective-permute-start(bf16[2,2,4,4,512]{4,3,2,1,0:T(4,128)(2,1)S(1)} %get-tuple-element.56), channel_id=1, source_target_pairs={{0,16},{8,24},{16,0},{24,8},{1,17},{9,25},{17,1},{25,9},{2,18},{10... | collective-permute-start | bytes 196616 | tf_op jit(solution)/shard_map/ppermute | solution.py:390
  6.0 4.7 %collective-permute-start.2 = (bf16[16,512]{1,0:T(8,128)(2,1)S(1)}, bf16[16,512]{1,0:T(8,128)(2,1)S(1)}, u32[]{:S(2)}, u32[]{:S(2)}) collective-permute-start(bf16[16,512]{1,0:T(8,128)(2,1)S(1)} %get-tuple-element.55), channel_id=1, source_target_pairs={{0,7},{1,0},{2,1},{3,2},{4,3},{5,4},{6,5},{7,6},{8,31},{9,24},{10,... | collective-permute-start | bytes 49160 | tf_op jit(solution)/shard_map/ppermute | solution.py:391
  10.6 1.9 %collective-permute-start.4 = (bf16[32,512]{1,0:T(8,128)(2,1)S(1)}, bf16[32,512]{1,0:T(8,128)(2,1)S(1)}, u32[]{:S(2)}, u32[]{:S(2)}) collective-permute-start(bf16[32,512]{1,0:T(8,128)(2,1)S(1)} %merge.1), channel_id=1, source_target_pairs={{0,8},{8,0},{16,24},{24,16},{1,9},{9,1},{17,25},{25,17},{2,10},{10... | collective-permute-start | bytes 98312 | tf_op jit(solution)/shard_map/ppermute | solution.py:463

commit v13 on v11

--- a/solution.py
+++ b/solution.py
@@ -232,6 +232,11 @@
             patches[row, place] = piece
 
 
+def prepare_kernel(slot_of, frames, conv, conv_shift, *refs):
+    conv_kernel(conv, conv_shift, *refs[4:7])
+    levels_kernel(slot_of, frames, *refs[:4], *refs[7:])
+
+
 def inner_kernel(patches, conv, *rest):
     weights, out = rest[:-1], rest[-1]
     row_count, _, _, plane = patches.shape
@@ -392,17 +397,6 @@
         far_halo, conv, conv_shift, *levels = lax.optimization_barrier(
             (far_halo, conv, conv_shift, *levels)
         )
-    *convs, conv_shift = pl.pallas_call(
-        conv_kernel,
-        out_shape=[jax.ShapeDtypeStruct((tall, 27 * GROUP * fields), BF16)] * 2
-        + [jax.ShapeDtypeStruct((tall, 128), F32)],
-        in_specs=[VMEM] * 2,
-        out_specs=[VMEM] * 3,
-        compiler_params=PARAMS,
-        cost_estimate=cost(0.15),
-        name="conv",
-    )(conv, conv_shift)
-
     wide_of = [count * frames * channels for count in counts]
     shapes = []
     for level in range(LEVELS):
@@ -414,16 +408,18 @@
         jax.ShapeDtypeStruct((wide_of[LEVELS], wide_of[LEVELS] * LEVELS), BF16),
         jax.ShapeDtypeStruct((wide_of[LEVELS], 128), F32),
     ]
-    weights = pl.pallas_call(
-        functools.partial(levels_kernel, slot_of, frames),
-        out_shape=shapes,
-        in_specs=[VMEM] * 4,
-        out_specs=[VMEM] * len(shapes),
+    made = pl.pallas_call(
+        functools.partial(prepare_kernel, slot_of, frames),
+        out_shape=[jax.ShapeDtypeStruct((tall, 27 * GROUP * fields), BF16)] * 2
+        + [jax.ShapeDtypeStruct((tall, 128), F32)]
+        + shapes,
+        in_specs=[VMEM] * 6,
+        out_specs=[VMEM] * (3 + len(shapes)),
         compiler_params=PARAMS,
-        cost_estimate=cost(0.35),
-        name="levels",
-    )(*levels)
-    weights = [conv_shift, *weights]
+        cost_estimate=cost(0.52),
+        name="prepare",
+    )(conv, conv_shift, *levels)
+    convs, weights = made[:2], made[2:]
 
     if paired:
         blocks = [own, near, beyond]

time: 15 us -> 14.8 us (0.987)
  Pallas kernels: 6.11 us -> 5.92 us
    pallas_call x2 -> x1, Pallas kernels: 0.95 us -> 0.76 us  [shards(): pl.pallas_call(functools.partial(prepare_kernel, slot_of, frames), out_sh...]
  transfers between devices with their start and end apart: 5 -> 5, of which waited for: 2 -> 3; matrix products, arithmetic and copies ran while one was open for 0% -> 0% of each run, Pallas kernels for 26% -> 25%
where the time goes in v13:
time: 14.8 us; the launch traced here: 14.7 us
  starting transfers between devices  8.5 us (57%)
  Pallas kernels  5.92 us (40%)
  waiting for transfers between devices  0.2 us (1%)
    ppermute x1, starting transfers between devices, shards(): near_halo = lax.ppermute(to_near, ('tm', 'space'), near_pairs)  3.2 us
    ppermute x1, starting transfers between devices, shards(): far_halo = lax.ppermute(to_far, ('tm', 'space'), far_pairs)  2.91 us
    pallas_call x1, Pallas kernels, shards(): pl.pallas_call(functools.partial(outer_kernel, paired), out_shape=jax.Sha...  2.22 us
    ppermute x1, starting transfers between devices, shards(): beyond = lax.ppermute(pair, 'tm', across)  1.49 us
    pallas_call x1, Pallas kernels, shards(): pl.pallas_call(inner_kernel, out_shape=jax.ShapeDtypeStruct((frames, row_...  1.38 us
    pallas_call x1, Pallas kernels, shards(): pl.pallas_call(fetch_kernel, out_shape=[jax.ShapeDtypeStruct(source.shape...  1 us
    pallas_call x1, Pallas kernels, shards(): pl.pallas_call(functools.partial(prepare_kernel, slot_of, frames), out_sh...  0.76 us
    pallas_call x1, Pallas kernels, shards(): pl.pallas_call(functools.partial(patch_kernel, paired), out_shape=jax.Sha...  0.53 us
  transfers between devices with their start and end apart: 5, of which 3 were waited for; matrix products, arithmetic and copies ran while one was open for 0% of the time, Pallas kernels for 25%

profile of v13, /device:TPU:0, one launch (start us, length us, event | category | flops | bytes accessed | tf_op | source)
XLA Modules:
  0.0 14.7 jit_solution(17984506751783541326)
XLA Ops:
  0.0 0.5 %collective-permute-start = (bf16[2,4,4,512]{3,2,1,0:T(4,128)(2,1)}, bf16[2,4,4,512]{3,2,1,0:T(4,128)(2,1)S(1)}, u32[]{:S(2)}, u32[]{:S(2)}) collective-permute-start(bf16[2,4,4,512]{3,2,1,0:T(4,128)(2,1)} %refs_0_.1), channel_id=1, source_target_pairs={{0,8},{8,0},{16,24},{24,16},{1,9},{9,1},{17,25},{25,17},{2,10},{10... | collective-permute-start | bytes 98312 | tf_op jit(solution)/shard_map/ppermute | solution.py:372
  0.5 1.0 %fetch.1 = (bf16[2,4,4,512]{3,2,1,0:T(4,128)(2,1)S(1)}, bf16[27,4,32]{2,1,0:T(4,128)(2,1)S(1)}, f32[1,32]{1,0:T(1,128)S(1)}, bf16[3,3,32,32]{3,2,1,0:T(8,128)(2,...) custom-call(bf16[2,4,4,512]{3,2,1,0:T(4,128)(2,1)} %refs_0_.1, ...), custom_call_target="tpu_custom_call" | custom-call | flops 920000000 | bytes 2960000 | tf_op jit(solution)/shard_map/fetch/pallas_call | solution.py:356
  1.5 0.1 collective-permute-done.near.refs_1_
  1.6 2.9 %collective-permute-start.1 = (bf16[16,512]{1,0:T(8,128)(2,1)S(1)}, bf16[16,512]{1,0:T(8,128)(2,1)S(1)}, u32[]{:S(2)}, u32[]{:S(2)}) collective-permute-start(bf16[16,512]{1,0:T(8,128)(2,1)S(1)} %get-tuple-element.46), channel_id=1, source_target_pairs={{0,1},{1,2},{2,3},{3,4},{4,5},{5,6},{6,7},{7,0},{8,25},{9,26},{10,... | collective-permute-start | bytes 49160 | tf_op jit(solution)/shard_map/ppermute | solution.py:391
  4.5 1.5 %collective-permute-start.3 = (bf16[2,2,4,4,512]{4,3,2,1,0:T(4,128)(2,1)S(1)}, bf16[2,2,4,4,512]{4,3,2,1,0:T(4,128)(2,1)S(1)}, u32[]{:S(2)}, u32[]{:S(2)}) collective-permute-start(bf16[2,2,4,4,512]{4,3,2,1,0:T(4,128)(2,1)S(1)} %get-tuple-element.55), channel_id=1, source_target_pairs={{0,16},{8,24},{16,0},{24,8},{1,17},{9,25},{17,1},{25,9},{2,18},{10... | collective-permute-start | bytes 196616 | tf_op jit(solution)/shard_map/ppermute | solution.py:389
  6.0 3.2 %collective-permute-start.2 = (bf16[16,512]{1,0:T(8,128)(2,1)S(1)}, bf16[16,512]{1,0:T(8,128)(2,1)S(1)}, u32[]{:S(2)}, u32[]{:S(2)}) collective-permute-start(bf16[16,512]{1,0:T(8,128)(2,1)S(1)} %get-tuple-element.54), channel_id=1, source_target_pairs={{0,7},{1,0},{2,1},{3,2},{4,3},{5,4},{6,5},{7,6},{8,31},{9,24},{10,... | collective-permute-start | bytes 49160 | tf_op jit(solution)/shard_map/ppermute | solution.py:390
  9.2 0.1 collective-permute-done.1.far
  9.2 0.8 %prepare.1 = (bf16[128,432]{1,0:T(8,128)(2,1)S(1)}, bf16[128,432]{1,0:T(8,128)(2,1)S(1)}, f32[128,128]{1,0:T(8,128)S(1)}, bf16[256,256]{1,0:T(8,128)(2,1)S(1)}, ...) custom-call(bf16[27,4,32]{2,1,0:T(4,128)(2,1)S(1)} %get-tuple-elemen, ...), custom_call_target="tpu_custom_call" | custom-call | flops 598000000 | bytes 1924000 | tf_op jit(solution)/shard_map/prepare/pallas_call | solution.py:411
  10.0 0.0 collective-permute-done.3.refs_2_
  10.0 0.5 %patch.1.patches.refs_1_ = bf16[4,9,32,512]{3,2,1,0:T(8,128)(2,1)S(1)} custom-call(bf16[2,4,4,512]{3,2,1,0:T(4,128)(2,1)S(1)} %get-tuple-element.45.own.refs_0_, bf16[2,4,4,512]{3,2,1,0:T(4,128)(2,1)S(1)} %collective-permute-done.near.refs_1_, bf16[2,2,4,4,512]{4,3,2,1,0:T(4,128)(2,1)S(1)} %collective-permute-done.3.refs_2_), custom_call_target="tpu_custom_call" | custom-call | flops 11500000 | bytes 37000 | tf_op jit(solution)/shard_map/patch/pallas_call | solution.py:439
  10.5 0.1 collective-permute-done.2.near
  10.6 0.4 %collective-permute-start.4 = (bf16[32,512]{1,0:T(8,128)(2,1)S(1)}, bf16[32,512]{1,0:T(8,128)(2,1)S(1)}, u32[]{:S(2)}, u32[]{:S(2)}) collective-permute-start(bf16[32,512]{1,0:T(8,128)(2,1)S(1)} %merge.1), channel_id=1, source_target_pairs={{0,8},{8,0},{16,24},{24,16},{1,9},{9,1},{17,25},{25,17},{2,10},{10... | collective-permute-start | bytes 98312 | tf_op jit(solution)/shard_map/ppermute | solution.py:462
  11.0 1.4 %inner.1.refs_2_ = bf16[2,2,32,512]{3,2,1,0:T(8,128)(2,1)S(1)} custom-call(bf16[4,9,32,512]{3,2,1,0:T(8,128)(2,1)S(1)} %patch.1.patches.refs_1_, bf16[128,432]{1,0:T(8,128)(2,1)S(1)} %get-tuple-element.74.conv.refs_3_, f32[128,128]{1,0:T(8,128)S(1)} %get-tuple-element.75.rest_0_.refs_5_, bf16[256,256]{1,0:T(8,128)(2,1)S(1)} %get-tuple-element.76.rest_1_.refs_6_, ...), custom_call_target="tpu_custom_call" | custom-call | flops 575000000 | bytes 1850000 | tf_op jit(solution)/shard_map/inner/pallas_call | solution.py:464
  12.4 0.0 collective-permute-done.4.refs_0_
  12.4 2.2 %outer.1 = bf16[2,4,32,512]{3,2,1,0:T(8,128)(2,1)} custom-call(bf16[16,512]{1,0:T(8,128)(2,1)S(1)} %collective-permute-done.2.near, bf16[16,512]{1,0:T(8,128)(2,1)S(1)} %collective-permute-done.1.far, bf16[32,512]{1,0:T(8,128)(2,1)S(1)} %collective-permute-done.4.refs_0_, bf16[4,9,32,512]{3,2,1,0:T(8,128)(2,1)S(1)} %patch.1.patches.refs_1_, ...), custom_call_target="tpu_custom_call" | custom-call | flops 2875000064 | bytes 9250000 | tf_op jit(solution)/shard_map/outer/pallas_call | solution.py:474
  (2 shorter events, 0.0 us)
Async XLA Ops:
  0.0 1.5 %collective-permute-start = (bf16[2,4,4,512]{3,2,1,0:T(4,128)(2,1)}, bf16[2,4,4,512]{3,2,1,0:T(4,128)(2,1)S(1)}, u32[]{:S(2)}, u32[]{:S(2)}) collective-permute-start(bf16[2,4,4,512]{3,2,1,0:T(4,128)(2,1)} %refs_0_.1), channel_id=1, source_target_pairs={{0,8},{8,0},{16,24},{24,16},{1,9},{9,1},{17,25},{25,17},{2,10},{10... | collective-permute-start | bytes 98312 | tf_op jit(solution)/shard_map/ppermute | solution.py:372
  1.6 7.7 %collective-permute-start.1 = (bf16[16,512]{1,0:T(8,128)(2,1)S(1)}, bf16[16,512]{1,0:T(8,128)(2,1)S(1)}, u32[]{:S(2)}, u32[]{:S(2)}) collective-permute-start(bf16[16,512]{1,0:T(8,128)(2,1)S(1)} %get-tuple-element.46), channel_id=1, source_target_pairs={{0,1},{1,2},{2,3},{3,4},{4,5},{5,6},{6,7},{7,0},{8,25},{9,26},{10,... | collective-permute-start | bytes 49160 | tf_op jit(solution)/shard_map/ppermute | solution.py:391
  4.5 5.5 %collective-permute-start.3 = (bf16[2,2,4,4,512]{4,3,2,1,0:T(4,128)(2,1)S(1)}, bf16[2,2,4,4,512]{4,3,2,1,0:T(4,128)(2,1)S(1)}, u32[]{:S(2)}, u32[]{:S(2)}) collective-permute-start(bf16[2,2,4,4,512]{4,3,2,1,0:T(4,128)(2,1)S(1)} %get-tuple-element.55), channel_id=1, source_target_pairs={{0,16},{8,24},{16,0},{24,8},{1,17},{9,25},{17,1},{25,9},{2,18},{10... | collective-permute-start | bytes 196616 | tf_op jit(solution)/shard_map/ppermute | solution.py:389
  6.0 4.6 %collective-permute-start.2 = (bf16[16,512]{1,0:T(8,128)(2,1)S(1)}, bf16[16,512]{1,0:T(8,128)(2,1)S(1)}, u32[]{:S(2)}, u32[]{:S(2)}) collective-permute-start(bf16[16,512]{1,0:T(8,128)(2,1)S(1)} %get-tuple-element.54), channel_id=1, source_target_pairs={{0,7},{1,0},{2,1},{3,2},{4,3},{5,4},{6,5},{7,6},{8,31},{9,24},{10,... | collective-permute-start | bytes 49160 | tf_op jit(solution)/shard_map/ppermute | solution.py:390
  10.6 1.8 %collective-permute-start.4 = (bf16[32,512]{1,0:T(8,128)(2,1)S(1)}, bf16[32,512]{1,0:T(8,128)(2,1)S(1)}, u32[]{:S(2)}, u32[]{:S(2)}) collective-permute-start(bf16[32,512]{1,0:T(8,128)(2,1)S(1)} %merge.1), channel_id=1, source_target_pairs={{0,8},{8,0},{16,24},{24,16},{1,9},{9,1},{17,25},{25,17},{2,10},{10... | collective-permute-start | bytes 98312 | tf_op jit(solution)/shard_map/ppermute | solution.py:462
